TPU v7x, 256 devices: a whole 4x4x8 slice. The times are simulated.
256 devices in a mesh: slab: 32 (over x, z), col: 4 (over y), pb: 2 (over core).
Axes of the slice: x: 4, y: 4, z: 8, core: 2. Of those that a mesh axis runs over, the one named last changes fastest.
Arguments:
- queries_raw: float32 [1024, 768], P(('slab', 'col', 'pb')), may hold values from -1.5 to 1.5
- projection: float32 [768, 768], replicated, may hold values from -0.21875 to 0.21875
- passages: bfloat16 [524288, 768], P(('slab', 'col')), may hold values from -17 to 17
- positives: int32 [1024, 4], P(('slab', 'col', 'pb')), may hold values from 0 to 524287
Outputs:
- loss: float32 [1024], P(('slab', 'col', 'pb'))
- grad_raw: float32 [1024, 768], P(('slab', 'col', 'pb'))
- grad_projection: float32 [768, 768], replicated
All inputs are finite; a program needn't handle non-finite values.
Results may differ from a plain program's by a relative error of at most 0.0053.
Values may be sent and summed in bfloat16 or wider, within the bound.
No kernel may reach another device: no remote copies, remote signals or barrier semaphores. Data moves between devices by JAX's collectives and lax.ppermute only.
A program may use at most 128 MiB of HBM per device.

v0:
```python
import jax
import jax.numpy as jnp
from jax import lax
from jax.sharding import PartitionSpec as P

POS = 4


def shards(queries_raw, projection, passages, positives):
    hp = lax.Precision.HIGHEST
    local_rows = passages.shape[0]
    own_queries = queries_raw.shape[0]
    group = lax.axis_size(("slab", "col"))
    scale = 1.0 / (4.0 * local_rows * group)
    projected = jnp.dot(queries_raw, projection, precision=hp, preferred_element_type=jnp.float32)
    query_emb = projected.astype(jnp.bfloat16)
    all_emb, all_pos = (
        lax.all_gather(query_emb, ("slab", "col"), axis=0, tiled=True),
        lax.all_gather(positives, ("slab", "col"), axis=0, tiled=True),
    )
    offset = lax.axis_index(("slab", "col")) * local_rows
    scores = lax.dot_general(
        all_emb, passages, (((1,), (1,)), ((), ())), preferred_element_type=jnp.float32
    )
    columns = jnp.arange(local_rows, dtype=jnp.int32)[None, :]
    local_pos = all_pos - offset
    owned = [local_pos[:, slot : slot + 1] == columns for slot in range(POS)]
    partial_pos = jnp.stack(
        [jnp.sum(jnp.where(owned[slot], scores, 0.0), axis=1) for slot in range(POS)], axis=1
    )
    pos_scores = lax.psum(partial_pos, ("slab", "col"))
    loss_part = jnp.zeros((scores.shape[0],), jnp.float32)
    slope_sum = jnp.zeros_like(scores)
    pos_list = []
    for slot in range(POS):
        sig = jax.nn.sigmoid(scores - pos_scores[:, slot : slot + 1])
        loss_part = loss_part + jnp.sum(sig, axis=1)
        slope = sig * (1.0 - sig)
        slope_sum = slope_sum + slope
        pos_list.append(-jnp.sum(slope, axis=1))
    pos_part = jnp.stack(pos_list, axis=1) * scale
    pos_grad, loss_total = lax.psum((pos_part, loss_part * scale), ("slab", "col"))
    grad = slope_sum * scale
    for slot in range(POS):
        grad = grad + jnp.where(owned[slot], pos_grad[:, slot : slot + 1], 0.0)
    grad_b = grad.astype(jnp.bfloat16)
    home = lax.axis_index(("slab", "col")) * own_queries
    summed = lax.psum(
        jnp.dot(grad_b, passages, preferred_element_type=jnp.float32), ("slab", "col")
    )
    query_grad = lax.dynamic_slice_in_dim(summed, home, own_queries, 0)
    loss = lax.dynamic_slice_in_dim(loss_total, home, own_queries, 0)
    grad_raw = jnp.dot(query_grad, projection.T, precision=hp, preferred_element_type=jnp.float32)
    term = jnp.dot(queries_raw.T, query_grad, precision=hp, preferred_element_type=jnp.float32)
    grad_projection = lax.psum(term, ("slab", "col", "pb"))
    return (loss, grad_raw, grad_projection)


def solution(mesh):
    in_specs = (
        P(("slab", "col", "pb"), None),
        P(),
        P(("slab", "col"), None),
        P(("slab", "col", "pb"), None),
    )
    out_specs = (P(("slab", "col", "pb")), P(("slab", "col", "pb"), None), P())
    return jax.shard_map(shards, mesh=mesh, in_specs=in_specs, out_specs=out_specs, check_vma=False)
```

profile of v0, /device:TPU:1, one launch (start us, length us, event | category | flops | bytes accessed | tf_op | source)
XLA Modules:
  0.0 2271.9 jit_solution(6751082720767750001)
XLA Ops:
  7.2 0.0 copy-start
  7.2 0.0 all-reduce.4.cloned.1.call-start
  7.2 295.5 %all-gather.1 = s32[128,4,4]{2,1,0:T(4,128)S(1)} all-gather(s32[1,4,4]{2,1,0:T(4,128)} %bitcast.45), channel_id=1, replica_groups=mesh['slab'=32,'col'=4,'pb'=2] {'slab','col'}, dimensions={0}, use_global_device_ids=true | all-gather | bytes 8256 | tf_op jit(solution)/shard_map/all_gather | solution.py:19
  302.8 0.0 copy-done
  302.8 1.9 fusion.5
  304.7 286.7 %all-gather = bf16[128,4,768]{2,1,0:T(4,128)(2,1)S(1)} all-gather(bf16[1,4,768]{2,1,0:T(4,128)(2,1)S(1)} %fusion.5), channel_id=1, replica_groups=mesh['slab'=32,'col'=4,'pb'=2] {'slab','col'}, dimensions={0}, use_global_device_ids=true | all-gather | bytes 792576 | tf_op jit(solution)/shard_map/all_gather | solution.py:18
  591.4 1.1 reshape.39
  592.5 0.3 fusion.14
  592.8 0.1 copy.19
  592.9 0.1 copy.20
  593.0 0.1 copy.18
  593.1 0.1 copy.21
  593.2 11.6 select_reduce_fusion.3
  604.9 293.2 %psum.35 = f32[512,4]{0,1:T(4,128)S(1)} all-reduce(f32[512,4]{0,1:T(4,128)S(1)} %pad_maximum_fusion), channel_id=1, replica_groups=mesh['slab'=32,'col'=4,'pb'=2] {'slab','col'}, use_global_device_ids=true, to_apply=%region_4.5 | all-reduce | flops 2048 | bytes 16384 | tf_op jit(solution)/shard_map/psum | solution.py:31
  898.1 17.1 fusion.1
  915.3 572.0 %all-reduce = (f32[512]{0:T(512)S(1)}, f32[512,4]{0,1:T(4,128)S(1)}) all-reduce(f32[512]{0:T(512)S(1)} %add_multiply_fusion, f32[512,4]{0,1:T(4,128)S(1)} %maximum_multiply_fusion), channel_id=1, replica_groups=mesh['slab'=32,'col'=4,'pb'=2] {'slab','col'}, use_global_device_ids=true, to_apply=%region_9.10 | all-reduce | flops 2560 | bytes 20480 | tf_op jit(solution)/shard_map/psum | solution.py:42
  1487.3 0.0 copy-start.1
  1487.3 21.1 fusion.4
  1508.4 0.0 all-reduce.4.cloned.1.call-update
  1508.4 0.0 all-reduce.6.cloned.1.call-start
  1508.5 485.4 %all-reduce.4.cloned.1.call-done = f32[512,768]{1,0:T(8,128)} async-done(((f32[512,768]{1,0:T(8,128)}), f32[512,768]{1,0:T(8,128)}) %all-reduce.4.cloned.1.call-update) | async-done | bytes 1572880 | tf_op jit(solution)/shard_map/psum | solution.py:48
  1993.9 0.0 copy-done.1
  1993.9 4.2 convolution_bitcast_fusion
  1998.1 0.0 all-reduce.6.cloned.1.call-update
  1998.2 0.6 dynamic_slice.6
  1998.7 3.4 fusion.7
  2002.1 260.0 %all-reduce.6.cloned.1.call-done = f32[768,768]{0,1:T(8,128)} async-done(((f32[768,768]{0,1:T(8,128)}), f32[768,768]{0,1:T(8,128)}) %all-reduce.6.cloned.1.call-update) | async-done | bytes 2359312 | tf_op jit(solution)/shard_map/psum | solution.py:55
  2262.1 3.0 copy.17
  (10 shorter events, 0.1 us)
Async XLA Ops:
  7.2 295.6 %copy-start = (f32[768,768]{1,0:T(8,128)S(1)}, f32[768,768]{1,0:T(8,128)}, u32[]{:S(2)}) copy-start(f32[768,768]{1,0:T(8,128)} %param.5) | copy-start | bytes 7077892
  7.2 1986.7 %all-reduce.4.cloned.1.call-start = ((), (), s32[]{:S(2)}) async-start(), calls=%async_computation | async-start | bytes 3145728 | tf_op jit(solution)/shard_map/psum | solution.py:48
  1487.3 506.6 %copy-start.1 = (f32[4,768]{1,0:T(4,128)S(1)}, f32[4,768]{1,0:T(4,128)}, u32[]{:S(2)}) copy-start(f32[4,768]{1,0:T(4,128)} %param.4) | copy-start | bytes 36868
  1508.4 753.6 %all-reduce.6.cloned.1.call-start = ((), (), s32[]{:S(2)}) async-start(), calls=%async_computation.1 | async-start | bytes 4718592 | tf_op jit(solution)/shard_map/psum | solution.py:55
Sparse Core Ops, SparseCore 0:
  1508.5 485.3 all-reduce.3
  2000.8 261.2 all-reduce.5
where the time goes:
time: 2270 us
  blocking collectives  1450 us (64%)
  waiting for transfers between devices  745 us (33%)
  matrix products  42.2 us (2%)
    psum x1, blocking collectives, shards(): lax.psum((pos_part, loss_part * scale), ('slab', 'col'))  572 us
    psum x1, waiting for transfers between devices, shards(): lax.psum(jnp.dot(grad_b, passages, preferred_element_type=jnp.float32), (...  485 us
    all_gather x1, blocking collectives, shards(): lax.all_gather(positives, ('slab', 'col'), axis=0, tiled=True)  296 us
    psum x1, blocking collectives, shards(): pos_scores = lax.psum(partial_pos, ('slab', 'col'))  293 us
    all_gather x1, blocking collectives, shards(): lax.all_gather(query_emb, ('slab', 'col'), axis=0, tiled=True)  287 us
    psum x1, waiting for transfers between devices, shards(): grad_projection = lax.psum(term, ('slab', 'col', 'pb'))  260 us
  transfers between devices with their start and end apart: 2, of which 2 were waited for; matrix products, arithmetic and copies ran while one was open for 0% of the time, Pallas kernels for 0%

commit v1 on v0

v1 whole, which is shorter than its diff:
```python
import jax
import jax.numpy as jnp
from jax import lax
from jax.sharding import Mesh, PartitionSpec as P

POS = 4
ALL = ("x", "z", "y", "c")
XY = ("x", "y")


def exchange(v, axes):
    return lax.all_to_all(v, axes, 0, 0, tiled=False)


def spread(v, axes):
    n = lax.axis_size(axes)
    return exchange(jnp.broadcast_to(v[None], (n,) + v.shape), axes)


def total(v):
    v = jnp.sum(spread(v, XY), axis=0)
    return jnp.sum(spread(v, "z"), axis=0)


def shards(queries_raw, projection, passages, positives):
    hp = lax.Precision.HIGHEST
    rows, dim = passages.shape
    own = queries_raw.shape[0]
    nz, nxy = lax.axis_size("z"), lax.axis_size(XY)
    plane = nz * own
    queries = nxy * plane
    scale = 1.0 / (4.0 * rows * nz * nxy)
    bf16 = jnp.bfloat16

    raw_all = lax.all_gather(queries_raw.astype(bf16), ALL, axis=0, tiled=True)

    projected = jnp.dot(queries_raw, projection, precision=hp, preferred_element_type=jnp.float32)
    ids = jnp.concatenate([positives >> 14, (positives >> 7) & 127, positives & 127], axis=1)
    ids = jnp.pad(ids, ((0, 0), (0, 128 - 3 * POS)))
    packet = jnp.concatenate([projected.astype(bf16), ids.astype(bf16)], axis=1)
    packet = spread(packet, "z").reshape(plane, dim + 128)
    packet = spread(packet, XY).reshape(queries, dim + 128)
    all_emb = packet[:, :dim]
    ids = packet[:, dim : dim + 3 * POS].astype(jnp.float32).astype(jnp.int32)
    all_pos = (ids[:, :POS] << 14) + (ids[:, POS : 2 * POS] << 7) + ids[:, 2 * POS :]

    shard = (lax.axis_index("x") * nz + lax.axis_index("z")) * lax.axis_size("y") + lax.axis_index("y")
    local_pos = all_pos - shard * rows
    scores = lax.dot_general(
        all_emb, passages, (((1,), (1,)), ((), ())), preferred_element_type=jnp.float32
    )
    columns = jnp.arange(rows, dtype=jnp.int32)[None, :]
    owned = [local_pos[:, slot : slot + 1] == columns for slot in range(POS)]
    partial_pos = jnp.stack(
        [jnp.sum(jnp.where(owned[slot], scores, 0.0), axis=1) for slot in range(POS)], axis=0
    )
    pos_scores = total(partial_pos).T
    loss_part = jnp.zeros((queries,), jnp.float32)
    slope_sum = jnp.zeros_like(scores)
    parts = []
    for slot in range(POS):
        sig = jax.nn.sigmoid(scores - pos_scores[:, slot : slot + 1])
        loss_part = loss_part + jnp.sum(sig, axis=1)
        slope = sig * (1.0 - sig)
        slope_sum = slope_sum + slope
        parts.append(-jnp.sum(slope, axis=1))
    sums = total(jnp.stack(parts + [loss_part], axis=0) * scale)
    pos_grad = sums[:POS].T
    grad = slope_sum * scale
    for slot in range(POS):
        grad = grad + jnp.where(owned[slot], pos_grad[:, slot : slot + 1], 0.0)
    part = jnp.dot(grad.astype(bf16), passages, preferred_element_type=jnp.float32)

    part = exchange(part.astype(bf16).reshape(nxy, plane, dim), XY)
    part = jnp.sum(part.astype(jnp.float32), axis=0).astype(bf16)
    summed = jnp.sum(spread(part, "z").astype(jnp.float32), axis=0)

    home = lax.axis_index("z") * own
    query_grad = lax.dynamic_slice_in_dim(summed, home, own, 0)
    grad_raw = jnp.dot(query_grad, projection.T, precision=hp, preferred_element_type=jnp.float32)
    first = lax.axis_index(XY) * plane + home
    loss = lax.dynamic_slice_in_dim(sums[POS], first, own, 0)

    mine = spread(summed.astype(bf16), XY).reshape(queries, dim)
    other = lax.ppermute(mine, "c", [(0, 1), (1, 0)])
    even = lax.axis_index("c") == 0
    grads = jnp.concatenate([jnp.where(even, mine, other), jnp.where(even, other, mine)], axis=0)
    sizes = [lax.axis_size(a) for a in ALL]
    raw = raw_all.reshape(*sizes, own, dim).transpose(3, 0, 2, 1, 4, 5).reshape(2 * queries, dim)
    grad_projection = lax.dot_general(
        raw, grads, (((0,), (0,)), ((), ())), preferred_element_type=jnp.float32
    )
    return (loss, grad_raw, grad_projection)


def solution(mesh):
    axes = Mesh(mesh.devices.reshape(4, 8, 4, 2), ALL)
    in_specs = (P(ALL, None), P(), P(("x", "z", "y"), None), P(ALL, None))
    out_specs = (P(ALL), P(ALL, None), P())
    return jax.shard_map(shards, mesh=axes, in_specs=in_specs, out_specs=out_specs, check_vma=False)
```

time: 2270 us -> 248 us (0.11)
  blocking collectives: 1450 us -> 87.4 us
  waiting for transfers between devices: 745 us -> 49.3 us
    psum x2 -> x0, blocking collectives: 865 us -> none  [the longest x1 572 us: shards(): lax.psum((pos_part, loss_part * scale), ('slab', 'col'))]
    psum x2 -> x0, waiting for transfers between devices: 745 us -> none  [the longest x1 485 us: shards(): lax.psum(jnp.dot(grad_b, passages, preferred_element_type=jnp.float32), (...]
    all_gather x2 -> x0, blocking collectives: 582 us -> none  [the longest x1 296 us: shards(): lax.all_gather(positives, ('slab', 'col'), axis=0, tiled=True)]
    all_to_all x0 -> x7, blocking collectives: none -> 87.4 us  [exchange(): return lax.all_to_all(v, axes, 0, 0, tiled=False)]
    all_gather x0 -> x1, waiting for transfers between devices: none -> 28.9 us  [shards(): raw_all = lax.all_gather(queries_raw.astype(bf16), ALL, axis=0, tiled=True)]
  transfers between devices with their start and end apart: 2 -> 4, of which waited for: 2 -> 3; matrix products, arithmetic and copies ran while one was open for 0% -> 13% of each run, Pallas kernels for 0% -> 0%
where the time goes in v1:
time: 248 us; the launch traced here: 247 us
  blocking collectives  87.4 us (35%)
  waiting for transfers between devices  49.3 us (20%)
  matrix products  40.5 us (16%)
  starting transfers between devices  21.2 us (9%)
  other arithmetic  20.4 us (8%)
  between operations  14.2 us (6%)
  local copies, waits for them, and re-layouts  14.1 us (6%)
    all_to_all x7, blocking collectives, exchange(): return lax.all_to_all(v, axes, 0, 0, tiled=False)  87.4 us
    all_gather x1, waiting for transfers between devices, shards(): raw_all = lax.all_gather(queries_raw.astype(bf16), ALL, axis=0, tiled=True)  28.9 us
    all_to_all x2, waiting for transfers between devices, exchange(): return lax.all_to_all(v, axes, 0, 0, tiled=False)  20.3 us
    dot_general x1, matrix products, shards(): jnp.dot(grad.astype(bf16), passages, preferred_element_type=jnp.float32)  20.3 us
    reduce_sum x1, other arithmetic, shards(): loss_part = loss_part + jnp.sum(sig, axis=1)  17 us
    dot_general x1, matrix products, shards(): lax.dot_general(all_emb, passages, (((1,), (1,)), ((), ())), preferred_el...  11.5 us
    ppermute x1, starting transfers between devices, shards(): other = lax.ppermute(mine, 'c', [(0, 1), (1, 0)])  10.9 us
    all_to_all x2, starting transfers between devices, exchange(): return lax.all_to_all(v, axes, 0, 0, tiled=False)  10.1 us
  transfers between devices with their start and end apart: 4, of which 3 were waited for; matrix products, arithmetic and copies ran while one was open for 13% of the time, Pallas kernels for 0%

profile of v1, /device:TPU:1, one launch (start us, length us, event | category | flops | bytes accessed | tf_op | source)
XLA Modules:
  0.0 247.1 jit_solution(9730011516197225526)
XLA Ops:
  7.2 0.0 copy-start
  7.2 0.8 shift-right-arithmetic_convert_fusion
  8.0 0.8 copy-done
  8.9 1.9 convolution_convert_fusion
  10.8 0.1 fusion.19
  10.9 16.1 %all_to_all.45 = bf16[8,4,896]{2,1,0:T(4,128)(2,1)S(1)} all-to-all(bf16[8,4,896]{2,1,0:T(4,128)(2,1)S(1)} %broadcast_in_dim.93), channel_id=1, replica_groups=mesh['x'=4,'z'=8,'y'=4,'c'=2] {'z'}, dimensions={0} | all-to-all | bytes 114688 | tf_op jit(solution)/shard_map/all_to_all | solution.py:12
  27.0 1.0 broadcast_in_dim.95
  28.0 6.8 %all-to-all-start.1 = ((bf16[16,32,896]{2,1,0:T(8,128)(2,1)}), bf16[16,32,896]{2,1,0:T(8,128)(2,1)S(1)}, u32[]{:S(2)}, u32[]{:S(2)}) async-start(bf16[16,32,896]{2,1,0:T(8,128)(2,1)} %broadcast_in_dim.95), calls=%async_computation.1 | async-start | bytes 1835008 | tf_op jit(solution)/shard_map/all_to_all | solution.py:12
  34.7 13.4 %all-to-all-done.1 = bf16[16,32,896]{2,1,0:T(8,128)(2,1)S(1)} async-done(((bf16[16,32,896]{2,1,0:T(8,128)(2,1)}), bf16[16,32,896]{2,1,0:T(8,128)(2,1)S(1)}, u32[]{:S(2)}, u32[]{:S(2)}) %all-to-all-start.1) | async-done | bytes 917536 | tf_op jit(solution)/shard_map/all_to_all | solution.py:12
  48.1 0.2 fusion.11
  48.3 0.6 slice_reduce_fusion.3
  48.9 11.5 %select_reduce_fusion.3 = (f32[512]{0:T(512)S(1)}, f32[512]{0:T(512)S(1)}, f32[512]{0:T(512)S(1)}, f32[512]{0:T(512)S(1)}, f32[512,4096]{1,0:T(8,128)}) fusion(s32[512]{0:T(512)S(1)} %get-tuple-element.33, s32[512]{0:T(512)S(1)} %get-tuple-element.34, s32[512]{0:T(512)S(1)} %get-tuple-element.35, s32[512]{0:T(512)S(1)} %get-tuple-element.36, ...), kind=kOutput, calls=%fused_computation.15 | convolution fusion | flops 3246389248 | bytes 15482880 | tf_op jit(solution)/shard_map/dot_general | solution.py:49
  60.4 11.2 %all_to_all.46 = f32[16,4,512]{2,1,0:T(4,128)S(1)} all-to-all(f32[16,4,512]{2,1,0:T(4,128)S(1)} %broadcast_in_dim.97), channel_id=1, replica_groups=mesh['x'=4,'z'=8,'y'=4,'c'=2] {'x','y'}, dimensions={0} | all-to-all | bytes 262144 | tf_op jit(solution)/shard_map/all_to_all | solution.py:12
  71.6 9.6 %all_to_all.47 = f32[8,4,512]{2,1,0:T(4,128)S(1)} all-to-all(f32[8,4,512]{2,1,0:T(4,128)S(1)} %broadcast_in_dim.98), channel_id=1, replica_groups=mesh['x'=4,'z'=8,'y'=4,'c'=2] {'z'}, dimensions={0} | all-to-all | bytes 131072 | tf_op jit(solution)/shard_map/all_to_all | solution.py:12
  81.3 0.0 copy-start.1
  81.3 17.0 %fusion.28 = (f32[512]{0:T(512)S(1)}, f32[512]{0:T(512)S(1)}, f32[512,4096]{1,0:T(8,128)}, f32[512]{0:T(512)S(1)}, f32[512]{0:T(512)S(1)}, /*index=5*/f32[512,40...) fusion(f32[512,4096]{1,0:T(8,128)} %get-tuple-element.63, ...), kind=kLoop, calls=%fused_computation.70 | loop fusion | flops 67104768 | bytes 41967616 | tf_op jit(solution)/shard_map/reduce_sum | solution.py:63
  98.5 10.7 %all_to_all.48 = f32[16,5,512]{2,1,0:T(8,128)S(1)} all-to-all(f32[16,5,512]{2,1,0:T(8,128)S(1)} %broadcast_in_dim.99), channel_id=1, replica_groups=mesh['x'=4,'z'=8,'y'=4,'c'=2] {'x','y'}, dimensions={0} | all-to-all | bytes 327680 | tf_op jit(solution)/shard_map/all_to_all | solution.py:12
  109.2 0.7 broadcast_in_dim.100
  109.9 3.4 %all-to-all-start.5 = ((f32[8,5,512]{2,1,0:T(8,128)}), f32[8,5,512]{2,1,0:T(8,128)S(1)}, u32[]{:S(2)}, u32[]{:S(2)}) async-start(f32[8,5,512]{2,1,0:T(8,128)} %broadcast_in_dim.100), calls=%async_computation.5 | async-start | bytes 262144 | tf_op jit(solution)/shard_map/all_to_all | solution.py:12
  113.2 0.2 all-gather.3.cloned.1.call-start
  113.5 0.0 copy-done.1
  113.5 0.6 convert_bitcast_fusion
  114.1 0.0 all-gather.3.cloned.1.call-update
  114.1 7.0 %all-to-all-done.5 = f32[8,5,512]{2,1,0:T(8,128)S(1)} async-done(((f32[8,5,512]{2,1,0:T(8,128)}), f32[8,5,512]{2,1,0:T(8,128)S(1)}, u32[]{:S(2)}, u32[]{:S(2)}) %all-to-all-start.5) | async-done | bytes 81952 | tf_op jit(solution)/shard_map/all_to_all | solution.py:12
  121.1 20.3 %fusion.8 = bf16[512,768]{1,0:T(8,128)(2,1)S(1)} fusion(bf16[4096,768]{1,0:T(8,128)(2,1)} %param.6, f32[512,4096]{1,0:T(8,128)} %get-tuple-element.43, f32[512,4096]{1,0:T(8,128)} %get-tuple-element.49, f32[512,4096]{1,0:T(8,128)} %get-tuple-element.46, f32[512,4096]{1,0:T(8,128)} %get-tuple-element.37, f32[512]{0:T(512)S(1)} %bitcast.58, ...), kind=kOutput, calls=%fused_computation.27 | convolution fusion | flops 3274047488 | bytes 40648704 | tf_op jit(solution)/shard_map/dot_general | solution.py:72
  141.4 13.4 %all_to_all.49 = bf16[16,32,768]{2,1,0:T(8,128)(2,1)S(1)} all-to-all(bf16[16,32,768]{2,1,0:T(8,128)(2,1)S(1)} %bitcast.46), channel_id=1, replica_groups=mesh['x'=4,'z'=8,'y'=4,'c'=2] {'x','y'}, dimensions={0} | all-to-all | bytes 1572864 | tf_op jit(solution)/shard_map/all_to_all | solution.py:12
  154.8 0.1 reduce_sum.181
  154.9 13.1 %all_to_all.50 = bf16[8,32,768]{2,1,0:T(8,128)(2,1)S(1)} all-to-all(bf16[8,32,768]{2,1,0:T(8,128)(2,1)S(1)} %broadcast_in_dim.109), channel_id=1, replica_groups=mesh['x'=4,'z'=8,'y'=4,'c'=2] {'z'}, dimensions={0} | all-to-all | bytes 786432 | tf_op jit(solution)/shard_map/all_to_all | solution.py:12
  168.0 0.1 convert_reduce_fusion
  168.1 0.1 broadcast_in_dim.110
  168.2 13.4 %all_to_all.51 = bf16[16,32,768]{2,1,0:T(8,128)(2,1)S(1)} all-to-all(bf16[16,32,768]{2,1,0:T(8,128)(2,1)S(1)} %broadcast_in_dim.110), channel_id=1, replica_groups=mesh['x'=4,'z'=8,'y'=4,'c'=2] {'x','y'}, dimensions={0} | all-to-all | bytes 1572864 | tf_op jit(solution)/shard_map/all_to_all | solution.py:12
  181.6 10.9 %collective-permute-start = (bf16[512,768]{1,0:T(8,128)(2,1)S(1)}, bf16[512,768]{1,0:T(8,128)(2,1)}, u32[]{:S(2)}, u32[]{:S(2)}) collective-permute-start(bf16[512,768]{1,0:T(8,128)(2,1)S(1)} %bitcast.42), channel_id=1, source_target_pairs={{0,1},{1,0},{2,3},{3,2},{4,5},{5,4},{6,7},{7,6},{8,9},{9,8},{10,11... | collective-permute-start | bytes 2359304 | tf_op jit(solution)/shard_map/ppermute | solution.py:85
  192.5 0.6 dynamic-slice_bitcast_fusion
  193.0 2.6 %fusion.13 = f32[4,768]{1,0:T(4,128)} fusion(f32[768,768]{1,0:T(8,128)S(1)} %copy-done, f32[32,768]{1,0:T(8,128)S(1)} %convert_reduce_fusion, s32[]{:T(128)S(6)} %select_n.53), kind=kOutput, calls=%fused_computation.44 | convolution fusion | flops 28311552 | bytes 2383876 | tf_op jit(solution)/shard_map/dot_general | solution.py:80
  195.7 28.9 %all-gather.3.cloned.1.call-done = bf16[256,4,768]{2,1,0:T(4,128)(2,1)} async-done(((bf16[1,4,768]{2,1,0:T(4,128)(2,1)}), bf16[256,4,768]{2,1,0:T(4,128)(2,1)}) %all-gather.3.cloned.1.call-update) | async-done | bytes 1572880 | tf_op jit(solution)/shard_map/all_gather | solution.py:35
  224.6 3.4 %copy.31 = bf16[4,8,4,2,4,768]{5,4,1,2,0,3:T(4,128)(2,1)} copy(bf16[4,8,4,2,4,768]{5,4,3,2,1,0:T(4,128)(2,1)} %bitcast.43) | data formatting | bytes 3145728 | tf_op jit(solution)/shard_map/reshape | solution.py:89
  228.0 3.7 %reshape.137 = bf16[1024,768]{1,0:T(8,128)(2,1)} reshape(bf16[2,4,4,8,4,768]{5,4,3,2,1,0:T(4,128)(2,1)} %bitcast.41) | data formatting | bytes 3145728 | tf_op jit(solution)/shard_map/reshape | solution.py:89
  231.7 0.0 collective-permute-done
  231.7 1.2 broadcast_select_fusion.1
  232.9 4.3 %convolution_bitcast_fusion = f32[768,768]{0,1:T(8,128)} fusion(bf16[1024,768]{1,0:T(8,128)(2,1)} %reshape.137, bf16[512,768]{1,0:T(8,128)(2,1)S(1)} %get-tuple-element.51, bf16[512,768]{1,0:T(8,128)(2,1)S(1)} %get-tuple-element.50), kind=kOutput, calls=%fused_computation.22 | convolution fusion | flops 1211105280 | bytes 5505024 | tf_op jit(solution)/shard_map/dot_general | solution.py:90
  237.2 3.0 %copy.22 = f32[768,768]{1,0:T(8,128)} copy(f32[768,768]{0,1:T(8,128)} %convolution_bitcast_fusion) | data formatting | bytes 4718592
  (25 shorter events, 0.4 us)
Async XLA Ops:
  7.2 1.7 copy-start
  28.0 20.1 %all-to-all-start.1 = ((bf16[16,32,896]{2,1,0:T(8,128)(2,1)}), bf16[16,32,896]{2,1,0:T(8,128)(2,1)S(1)}, u32[]{:S(2)}, u32[]{:S(2)}) async-start(bf16[16,32,896]{2,1,0:T(8,128)(2,1)} %broadcast_in_dim.95), calls=%async_computation.1 | async-start | bytes 1835008 | tf_op jit(solution)/shard_map/all_to_all | solution.py:12
  81.3 32.2 %copy-start.1 = (f32[4,768]{1,0:T(4,128)S(1)}, f32[4,768]{1,0:T(4,128)}, u32[]{:S(2)}) copy-start(f32[4,768]{1,0:T(4,128)} %param.4) | copy-start | bytes 36868
  109.9 11.2 %all-to-all-start.5 = ((f32[8,5,512]{2,1,0:T(8,128)}), f32[8,5,512]{2,1,0:T(8,128)S(1)}, u32[]{:S(2)}, u32[]{:S(2)}) async-start(f32[8,5,512]{2,1,0:T(8,128)} %broadcast_in_dim.100), calls=%async_computation.5 | async-start | bytes 262144 | tf_op jit(solution)/shard_map/all_to_all | solution.py:12
  113.2 111.3 %all-gather.3.cloned.1.call-start = ((), (), s32[]{:S(2)}) async-start(), calls=%async_computation.9 | async-start | bytes 1579008 | tf_op jit(solution)/shard_map/all_gather | solution.py:35
  181.6 50.1 %collective-permute-start = (bf16[512,768]{1,0:T(8,128)(2,1)S(1)}, bf16[512,768]{1,0:T(8,128)(2,1)}, u32[]{:S(2)}, u32[]{:S(2)}) collective-permute-start(bf16[512,768]{1,0:T(8,128)(2,1)S(1)} %bitcast.42), channel_id=1, source_target_pairs={{0,1},{1,0},{2,3},{3,2},{4,5},{5,4},{6,7},{7,6},{8,9},{9,8},{10,11... | collective-permute-start | bytes 2359304 | tf_op jit(solution)/shard_map/ppermute | solution.py:85
Sparse Core Ops, SparseCore 0:
  117.8 106.7 all-gather.2

commit v2 on v1

v2 whole, which is shorter than its diff:
```python
import functools

import jax
import jax.numpy as jnp
from jax import lax
from jax.experimental import pallas as pl
from jax.experimental.pallas import tpu as pltpu
from jax.sharding import Mesh, PartitionSpec as P

POS = 4
ALL = ("x", "z", "y", "c")
XY = ("x", "y")
LANES = 128
CLAMP = 80.0
BF16 = jnp.bfloat16
F32 = jnp.float32


def params(*semantics):
    return pltpu.CompilerParams(dimension_semantics=semantics or None, vmem_limit_bytes=50 * 1024 * 1024)


def columns_to_rows(columns):
    rows = columns[0].shape[0]
    lane = lax.broadcasted_iota(jnp.int32, (rows, LANES), 1)
    table = jnp.zeros((rows, LANES), F32)
    for k, column in enumerate(columns):
        table = jnp.where(lane == k, column, table)
    return table.T[:8]


def rows_to_columns(rows):
    wide = jnp.concatenate([rows, jnp.zeros((LANES - 8, rows.shape[1]), F32)], axis=0)
    return wide.T


def score_kernel(packet_ref, passages_ref, ids_ref, scores_ref, pos_ref, chunk, found):
    step = pl.program_id(0)
    groups, _, dim = packet_ref.shape
    queries, width = scores_ref.shape

    @pl.when(step == 0)
    def _():
        for k in range(POS):
            ids = ids_ref[:, k : k + 1]
            chunk[k] = jnp.broadcast_to(ids >> 7, (queries, LANES))
        found[...] = jnp.zeros_like(found)

    emb = packet_ref[:, : queries // groups, :].reshape(queries, dim)
    scores = lax.dot_general(
        emb, passages_ref[...], (((1,), (1,)), ((), ())), preferred_element_type=F32
    )
    scores_ref[...] = scores
    first = step * (width // LANES)
    for tile in range(queries // 8):
        rows = slice(tile * 8, tile * 8 + 8)
        for k in range(POS):
            want = chunk[k, rows, :] - first
            best = found[k, rows, :]
            for c in range(width // LANES):
                best = jnp.where(want == c, scores[rows, c * LANES : (c + 1) * LANES], best)
            found[k, rows, :] = best

    @pl.when(step == pl.num_programs(0) - 1)
    def _():
        lane = lax.broadcasted_iota(jnp.int32, (queries, LANES), 1)
        columns = []
        for k in range(POS):
            hit = lane == (ids_ref[:, k : k + 1] & (LANES - 1))
            columns.append(jnp.sum(jnp.where(hit, found[k], 0.0), axis=1, keepdims=True))
        rows = columns_to_rows(columns)
        for g in range(pos_ref.shape[0]):
            pos_ref[g] = rows


def score_call(packet, passages, ids, queries, block=512):
    rows, dim = passages.shape
    groups = packet.shape[0]
    return pl.pallas_call(
        score_kernel,
        grid=(rows // block,),
        in_specs=[
            pl.BlockSpec(packet.shape, lambda j: (0, 0, 0)),
            pl.BlockSpec((block, dim), lambda j: (j, 0)),
            pl.BlockSpec(ids.shape, lambda j: (0, 0)),
        ],
        out_specs=[
            pl.BlockSpec((queries, block), lambda j: (0, j)),
            pl.BlockSpec((groups, 8, queries), lambda j: (0, 0, 0)),
        ],
        out_shape=[
            jax.ShapeDtypeStruct((queries, rows), F32),
            jax.ShapeDtypeStruct((groups, 8, queries), F32),
        ],
        scratch_shapes=[
            pltpu.VMEM((POS, queries, LANES), jnp.int32),
            pltpu.VMEM((POS, queries, LANES), F32),
        ],
        compiler_params=params("arbitrary"),
        cost_estimate=pl.CostEstimate(
            flops=2 * queries * rows * dim, bytes_accessed=rows * dim * 2 + queries * rows * 4, transcendentals=0
        ),
        name="score",
    )(packet, passages, ids)


def sigmoid_kernel(scale, pos_ref, scores_ref, slopes_ref, sums_ref, pos, sums):
    step = pl.program_id(0)
    block, width = scores_ref.shape

    @pl.when(step == 0)
    def _():
        rows = pos_ref[0]
        for g in range(1, pos_ref.shape[0]):
            rows = rows + pos_ref[g]
        pos[...] = rows_to_columns(rows)

    def tile(t, carry):
        at = pl.multiple_of(t * 8, 8)
        own = pl.ds(pl.multiple_of(step * block + t * 8, 8), 8)
        columns = pos[own, :]
        p = [jnp.broadcast_to(columns[:, k : k + 1], (8, LANES)) for k in range(POS)]
        slope_acc = [jnp.zeros((8, LANES), F32) for _ in range(POS)]
        loss_acc = jnp.zeros((8, LANES), F32)
        for c in range(width // LANES):
            s = scores_ref[pl.ds(at, 8), c * LANES : (c + 1) * LANES]
            both = None
            for k in range(POS):
                e = jnp.exp(jnp.minimum(p[k] - s, CLAMP))
                sig = 1.0 / (1.0 + e)
                slope = e * (sig * sig)
                loss_acc = loss_acc + sig
                slope_acc[k] = slope_acc[k] + slope
                both = slope if both is None else both + slope
            slopes_ref[pl.ds(at, 8), c * LANES : (c + 1) * LANES] = both * scale
        for k in range(POS):
            sums[k, own, :] = slope_acc[k]
        sums[POS, own, :] = loss_acc
        return carry

    lax.fori_loop(0, block // 8, tile, 0)

    @pl.when(step == pl.num_programs(0) - 1)
    def _():
        columns = [jnp.sum(sums[k], axis=1, keepdims=True) * (scale if k == POS else -scale) for k in range(POS + 1)]
        rows = columns_to_rows(columns)
        for g in range(sums_ref.shape[0]):
            sums_ref[g] = rows


def sigmoid_call(pos, scores, scale, groups, block=64):
    queries, width = scores.shape
    return pl.pallas_call(
        functools.partial(sigmoid_kernel, scale),
        grid=(queries // block,),
        in_specs=[
            pl.BlockSpec(pos.shape, lambda j: (0, 0, 0)),
            pl.BlockSpec((block, width), lambda j: (j, 0)),
        ],
        out_specs=[
            pl.BlockSpec((block, width), lambda j: (j, 0)),
            pl.BlockSpec((groups, 8, queries), lambda j: (0, 0, 0)),
        ],
        out_shape=[
            jax.ShapeDtypeStruct((queries, width), F32),
            jax.ShapeDtypeStruct((groups, 8, queries), F32),
        ],
        scratch_shapes=[
            pltpu.VMEM((queries, LANES), F32),
            pltpu.VMEM((POS + 1, queries, LANES), F32),
        ],
        compiler_params=params("arbitrary"),
        cost_estimate=pl.CostEstimate(
            flops=40 * queries * width, bytes_accessed=queries * width * 8, transcendentals=8 * queries * width
        ),
        name="sigmoid",
    )(pos, scores)


def grad_kernel(sums_ref, slopes_ref, passages_ref, ids_ref, part_ref, total_ref, ids, grads, left, acc):
    step = pl.program_id(0)
    queries, width = slopes_ref.shape

    @pl.when(step == 0)
    def _():
        rows = sums_ref[0]
        for g in range(1, sums_ref.shape[0]):
            rows = rows + sums_ref[g]
        total_ref[...] = rows
        columns = rows_to_columns(rows)
        for k in range(POS):
            ids[k] = jnp.broadcast_to(ids_ref[:, k : k + 1], (queries, LANES))
            grads[k] = jnp.broadcast_to(columns[:, k : k + 1], (queries, LANES))

    lane = lax.broadcasted_iota(jnp.int32, (16, LANES), 1)
    for tile in range(queries // 16):
        rows = slice(tile * 16, tile * 16 + 16)
        want = [ids[k, rows, :] - step * width - lane for k in range(POS)]
        give = [grads[k, rows, :] for k in range(POS)]
        for c in range(width // LANES):
            g = slopes_ref[rows, c * LANES : (c + 1) * LANES]
            for k in range(POS):
                g = g + jnp.where(want[k] == c * LANES, give[k], 0.0)
            left[rows, c * LANES : (c + 1) * LANES] = g.astype(BF16)
    product = jnp.dot(left[...], passages_ref[...], preferred_element_type=F32)

    @pl.when(step == 0)
    def _():
        acc[...] = product

    @pl.when(step > 0)
    def _():
        acc[...] += product

    @pl.when(step == pl.num_programs(0) - 1)
    def _():
        part_ref[...] = acc[...].astype(BF16).reshape(part_ref.shape)


def grad_call(sums, slopes, passages, ids, groups, block=1024):
    rows, dim = passages.shape
    queries = slopes.shape[0]
    return pl.pallas_call(
        grad_kernel,
        grid=(rows // block,),
        in_specs=[
            pl.BlockSpec(sums.shape, lambda j: (0, 0, 0)),
            pl.BlockSpec((queries, block), lambda j: (0, j)),
            pl.BlockSpec((block, dim), lambda j: (j, 0)),
            pl.BlockSpec(ids.shape, lambda j: (0, 0)),
        ],
        out_specs=[
            pl.BlockSpec((groups, queries // groups, dim), lambda j: (0, 0, 0)),
            pl.BlockSpec((8, queries), lambda j: (0, 0)),
        ],
        out_shape=[
            jax.ShapeDtypeStruct((groups, queries // groups, dim), BF16),
            jax.ShapeDtypeStruct((8, queries), F32),
        ],
        scratch_shapes=[
            pltpu.VMEM((POS, queries, LANES), jnp.int32),
            pltpu.VMEM((POS, queries, LANES), F32),
            pltpu.VMEM((queries, block), BF16),
            pltpu.VMEM((queries, dim), F32),
        ],
        compiler_params=params("arbitrary"),
        cost_estimate=pl.CostEstimate(
            flops=2 * queries * rows * dim, bytes_accessed=rows * dim * 2 + queries * rows * 4, transcendentals=0
        ),
        name="grad",
    )(sums, slopes, passages, ids)


def fold_kernel(parts_ref, out_ref):
    acc = parts_ref[0].astype(F32)
    for g in range(1, parts_ref.shape[0]):
        acc = acc + parts_ref[g].astype(F32)
    for g in range(out_ref.shape[0]):
        out_ref[g] = acc.astype(out_ref.dtype)


def fold_call(parts, n):
    return pl.pallas_call(
        fold_kernel,
        out_shape=jax.ShapeDtypeStruct((n,) + parts.shape[1:], parts.dtype),
        compiler_params=params(),
        name="fold",
    )(parts)


def fold_both_kernel(parts_ref, out_ref, sum_ref):
    acc = parts_ref[0].astype(F32)
    for g in range(1, parts_ref.shape[0]):
        acc = acc + parts_ref[g].astype(F32)
    sum_ref[...] = acc
    for g in range(out_ref.shape[0]):
        out_ref[g] = acc.astype(out_ref.dtype)


def fold_both_call(parts, n):
    return pl.pallas_call(
        fold_both_kernel,
        out_shape=[
            jax.ShapeDtypeStruct((n,) + parts.shape[1:], parts.dtype),
            jax.ShapeDtypeStruct(parts.shape[1:], F32),
        ],
        compiler_params=params(),
        name="fold_both",
    )(parts)


def final_kernel(core_ref, packet_ref, raw_ref, mine_ref, other_ref, out_ref):
    groups, plane, dim = mine_ref.shape
    queries = groups * plane

    def term(raw, grads):
        return lax.dot_general(raw, grads, (((0,), (0,)), ((), ())), preferred_element_type=F32)

    def both(first, second):
        out_ref[...] = term(*first)
        out_ref[...] += term(*second)

    own = (packet_ref[:, plane : 2 * plane, :].reshape(queries, dim), mine_ref[...].reshape(queries, dim))
    peer = (raw_ref[...].reshape(queries, dim), other_ref[...].reshape(queries, dim))

    @pl.when(core_ref[0] == 0)
    def _():
        both(own, peer)

    @pl.when(core_ref[0] != 0)
    def _():
        both(peer, own)


def final_call(core, packet, raw, mine, other):
    dim = mine.shape[-1]
    return pl.pallas_call(
        final_kernel,
        in_specs=[pl.BlockSpec(memory_space=pltpu.SMEM)] + [pl.BlockSpec(memory_space=pltpu.VMEM)] * 4,
        out_shape=jax.ShapeDtypeStruct((dim, dim), F32),
        compiler_params=params(),
        name="final",
    )(core, packet, raw, mine, other)


def exchange(v, axes):
    return lax.all_to_all(v, axes, 0, 0, tiled=False)


def spread(v, axes):
    return exchange(jnp.broadcast_to(v[None], (lax.axis_size(axes),) + v.shape), axes)


def shards(queries_raw, projection, passages, positives):
    hp = lax.Precision.HIGHEST
    rows, dim = passages.shape
    own = queries_raw.shape[0]
    nz, nxy = lax.axis_size("z"), lax.axis_size(XY)
    plane = nz * own
    queries = nxy * plane
    scale = 1.0 / (4.0 * rows * nz * nxy)
    core = lax.axis_index("c")
    swap = [(0, 1), (1, 0)]

    projected = jnp.dot(queries_raw, projection, precision=hp, preferred_element_type=F32)
    ids = jnp.concatenate([positives >> 14, (positives >> 7) & 127, positives & 127], axis=1)
    ids = jnp.pad(ids, ((0, 0), (0, LANES - 3 * POS)))
    packet = jnp.concatenate([projected.astype(BF16), queries_raw.astype(BF16), ids.astype(BF16)], axis=1)
    packet = spread(packet, "z").reshape(plane, 2 * dim + LANES)
    ids = packet[:, 2 * dim : 2 * dim + 3 * POS].reshape(1, 3 * POS * plane)
    ids = jnp.pad(ids, ((0, 7), (0, dim - 3 * POS * plane)))
    packet = jnp.concatenate([packet[:, :dim], packet[:, dim : 2 * dim], ids], axis=0)
    packet = spread(packet, XY)

    raw_other = lax.ppermute(packet[:, plane : 2 * plane, :], "c", swap)
    ids = packet[:, 2 * plane, : 3 * POS * plane].reshape(queries, 3 * POS).astype(F32).astype(jnp.int32)
    all_pos = (ids[:, :POS] << 14) + (ids[:, POS : 2 * POS] << 7) + ids[:, 2 * POS :]
    shard = (lax.axis_index("x") * nz + lax.axis_index("z")) * lax.axis_size("y") + lax.axis_index("y")
    local_pos = all_pos - shard * rows

    scores, pos = score_call(packet, passages, local_pos, queries)
    pos = exchange(fold_call(exchange(pos, XY), nz), "z")
    slopes, sums = sigmoid_call(pos, scores, scale, nxy)
    sums = exchange(fold_call(exchange(sums, XY), nz), "z")
    part, sums = grad_call(sums, slopes, passages, local_pos, nxy)

    part = exchange(fold_call(exchange(part, XY), nz), "z")
    part, summed = fold_both_call(part, nxy)
    mine = exchange(part, XY)
    other = lax.ppermute(mine, "c", swap)

    home = lax.axis_index("z") * own
    query_grad = lax.dynamic_slice_in_dim(summed, home, own, 0)
    grad_raw = jnp.dot(query_grad, projection.T, precision=hp, preferred_element_type=F32)
    first = lax.axis_index(XY) * plane + home
    loss = lax.dynamic_slice_in_dim(sums[POS], first, own, 0)
    grad_projection = final_call(core.reshape(1), packet, raw_other, mine, other)
    return (loss, grad_raw, grad_projection)


def solution(mesh):
    axes = Mesh(mesh.devices.reshape(4, 8, 4, 2), ALL)
    in_specs = (P(ALL, None), P(), P(("x", "z", "y"), None), P(ALL, None))
    out_specs = (P(ALL), P(ALL, None), P())
    return jax.shard_map(shards, mesh=axes, in_specs=in_specs, out_specs=out_specs, check_vma=False)
```

time: 248 us -> 202 us (0.81)
  Pallas kernels: 0 us -> 49 us
  matrix products: 40.5 us -> 4.53 us
  waiting for transfers between devices: 49.3 us -> 22.2 us
  other arithmetic: 20.4 us -> 2.83 us
  between operations: 14.2 us -> 0.77 us
  local copies, waits for them, and re-layouts: 14.1 us -> 5.46 us
  starting transfers between devices: 21.2 us -> 29.8 us
    pallas_call x0 -> x8, Pallas kernels: none -> 49 us  [the longest x1 20.2 us: sigmoid_call(): pl.pallas_call(functools.partial(sigmoid_kernel, scale), grid=(queries //...]
    dot_general x5 -> x2, matrix products: 40.5 us -> 4.53 us  [the longest x1 2.62 us: shards(): jnp.dot(query_grad, projection.T, precision=hp, preferred_element_type=F32)]
    all_gather x1 -> x0, waiting for transfers between devices: 28.9 us -> none  [shards(): raw_all = lax.all_gather(queries_raw.astype(bf16), ALL, axis=0, tiled=True)]
    reduce_sum x7 -> x0, other arithmetic: 17.3 us -> none  [the longest x1 17 us: shards(): loss_part = loss_part + jnp.sum(sig, axis=1)]
    ppermute x1 -> x2, starting transfers between devices: 10.9 us -> 19.4 us  [the longest x1 10 us: shards(): raw_other = lax.ppermute(packet[:, plane:2 * plane, :], 'c', swap)]
    reshape x2, local copies, waits for them, and re-layouts: 7.1 us -> 0.14 us  [the longest x1 0.11 us: shards(): ids = packet[:, 2 * dim:2 * dim + 3 * POS].reshape(1, 3 * POS * plane)]
    unnamed x5 -> x4, local copies, waits for them, and re-layouts: 3.89 us -> 1.04 us
  transfers between devices with their start and end apart: 4 -> 4, of which waited for: 3 -> 1; matrix products, arithmetic and copies ran while one was open for 13% -> 3% of each run, Pallas kernels for 0% -> 0%
where the time goes in v2:
time: 202 us; the launch traced here: 201 us
  blocking collectives  86.8 us (43%)
  Pallas kernels  49 us (24%)
  starting transfers between devices  29.8 us (15%)
  waiting for transfers between devices  22.2 us (11%)
  local copies, waits for them, and re-layouts  5.46 us (3%)
  matrix products  4.53 us (2%)
  other arithmetic  2.83 us (1%)
    all_to_all x7, blocking collectives, exchange(): return lax.all_to_all(v, axes, 0, 0, tiled=False)  86.8 us
    all_to_all x2, waiting for transfers between devices, exchange(): return lax.all_to_all(v, axes, 0, 0, tiled=False)  22.2 us
    pallas_call x1, Pallas kernels, sigmoid_call(): pl.pallas_call(functools.partial(sigmoid_kernel, scale), grid=(queries //...  20.2 us
    pallas_call x1, Pallas kernels, score_call(): pl.pallas_call(score_kernel, grid=(rows // block,), in_specs=[pl.BlockSpe...  12.4 us
    pallas_call x1, Pallas kernels, grad_call(): pl.pallas_call(grad_kernel, grid=(rows // block,), in_specs=[pl.BlockSpec...  11.2 us
    all_to_all x2, starting transfers between devices, exchange(): return lax.all_to_all(v, axes, 0, 0, tiled=False)  10.4 us
    ppermute x1, starting transfers between devices, shards(): raw_other = lax.ppermute(packet[:, plane:2 * plane, :], 'c', swap)  10 us
    ppermute x1, starting transfers between devices, shards(): other = lax.ppermute(mine, 'c', swap)  9.42 us
  transfers between devices with their start and end apart: 4, of which 1 were waited for; matrix products, arithmetic and copies ran while one was open for 3% of the time, Pallas kernels for 0%

profile of v2, /device:TPU:1, one launch (start us, length us, event | category | flops | bytes accessed | tf_op | source)
XLA Modules:
  0.0 201.4 jit_solution(9607714282654172021)
XLA Ops:
  0.6 0.0 copy-start
  0.6 0.8 shift-right-arithmetic_convert_fusion
  1.5 0.7 convert_element_type.20
  2.2 0.1 copy-done
  2.3 1.9 convolution_convert_fusion
  4.2 0.1 fusion.12
  4.4 16.4 %all_to_all.45 = bf16[8,4,1664]{2,1,0:T(4,128)(2,1)S(1)} all-to-all(bf16[8,4,1664]{2,1,0:T(4,128)(2,1)S(1)} %broadcast_in_dim.4), channel_id=1, replica_groups=mesh['x'=4,'z'=8,'y'=4,'c'=2] {'z'}, dimensions={0} | all-to-all | bytes 212992 | tf_op jit(solution)/shard_map/all_to_all | solution.py:327
  20.8 0.1 reshape.21
  20.9 1.3 broadcast_in_dim.5
  22.2 6.8 %all-to-all-start.1 = ((bf16[16,72,768]{2,1,0:T(8,128)(2,1)}), bf16[16,72,768]{2,1,0:T(8,128)(2,1)}, u32[]{:S(2)}, u32[]{:S(2)}) async-start(bf16[16,72,768]{2,1,0:T(8,128)(2,1)} %broadcast_in_dim.5), calls=%async_computation.1 | async-start | bytes 3538944 | tf_op jit(solution)/shard_map/all_to_all | solution.py:327
  29.1 22.2 %all-to-all-done.1.packet_ref = bf16[16,72,768]{2,1,0:T(8,128)(2,1)} async-done(((bf16[16,72,768]{2,1,0:T(8,128)(2,1)}), bf16[16,72,768]{2,1,0:T(8,128)(2,1)}, u32[]{:S(2)}, u32[]{:S(2)}) %all-to-all-start.1) | async-done | bytes 1769504 | tf_op jit(solution)/shard_map/all_to_all | solution.py:327
  51.2 1.0 fusion.5
  52.2 0.3 convert_element_type.23
  52.5 0.2 fusion.ids_ref
  52.7 12.4 %score.1 = (f32[512,4096]{1,0:T(8,128)}, f32[16,8,512]{2,1,0:T(8,128)S(1)}) custom-call(bf16[16,72,768]{2,1,0:T(8,128)(2,1)} %all-to-all-done.1.packet_ref, bf16[4096,768]{1,0:T(8,128)(2,1)} %passages_ref.3, s32[512,4]{1,0:T(8,128)S(1)} %fusion.ids_ref), custom_call_target="tpu_custom_call" | custom-call | flops 3221225472 | bytes 14680064 | tf_op jit(solution)/shard_map/score/pallas_call | solution.py:79
  65.1 12.6 %all_to_all.46.parts_ref = f32[16,8,512]{2,1,0:T(8,128)S(1)} all-to-all(f32[16,8,512]{2,1,0:T(8,128)S(1)} %get-tuple-element.11), channel_id=1, replica_groups=mesh['x'=4,'z'=8,'y'=4,'c'=2] {'x','y'}, dimensions={0} | all-to-all | bytes 524288 | tf_op jit(solution)/shard_map/all_to_all | solution.py:327
  77.7 10.3 %all_to_all.47.pos_ref = f32[8,8,512]{2,1,0:T(8,128)S(1)} all-to-all(f32[8,8,512]{2,1,0:T(8,128)S(1)} %fold.3), channel_id=1, replica_groups=mesh['x'=4,'z'=8,'y'=4,'c'=2] {'z'}, dimensions={0} | all-to-all | bytes 262144 | tf_op jit(solution)/shard_map/all_to_all | solution.py:327
  88.0 20.2 %sigmoid.1 = (f32[512,4096]{1,0:T(8,128)}, f32[16,8,512]{2,1,0:T(8,128)S(1)}) custom-call(f32[8,8,512]{2,1,0:T(8,128)S(1)} %all_to_all.47.pos_ref, f32[512,4096]{1,0:T(8,128)} %get-tuple-element.12.scores_ref), custom_call_target="tpu_custom_call" | custom-call | flops 83886080 | bytes 16777216 | tf_op jit(solution)/shard_map/sigmoid/pallas_call | solution.py:153
  108.3 10.7 %all_to_all.48.parts_ref = f32[16,8,512]{2,1,0:T(8,128)S(1)} all-to-all(f32[16,8,512]{2,1,0:T(8,128)S(1)} %get-tuple-element.13), channel_id=1, replica_groups=mesh['x'=4,'z'=8,'y'=4,'c'=2] {'x','y'}, dimensions={0} | all-to-all | bytes 524288 | tf_op jit(solution)/shard_map/all_to_all | solution.py:327
  119.0 10.3 %all_to_all.49.sums_ref = f32[8,8,512]{2,1,0:T(8,128)S(1)} all-to-all(f32[8,8,512]{2,1,0:T(8,128)S(1)} %fold.4), channel_id=1, replica_groups=mesh['x'=4,'z'=8,'y'=4,'c'=2] {'z'}, dimensions={0} | all-to-all | bytes 262144 | tf_op jit(solution)/shard_map/all_to_all | solution.py:327
  129.3 11.2 %grad.1 = (bf16[16,32,768]{2,1,0:T(8,128)(2,1)S(1)}, f32[8,512]{1,0:T(8,128)S(1)}) custom-call(f32[8,8,512]{2,1,0:T(8,128)S(1)} %all_to_all.49.sums_ref, f32[512,4096]{1,0:T(8,128)} %get-tuple-element.14.slopes_ref, bf16[4096,768]{1,0:T(8,128)(2,1)} %passages_ref.3, s32[512,4]{1,0:T(8,128)S(1)} %fusion.ids_ref), custom_call_target="tpu_custom_call" | custom-call | flops 3221225472 | bytes 14680064 | tf_op jit(solution)/shard_map/grad/pallas_call | solution.py:223
  140.5 13.4 %all_to_all.50.parts_ref = bf16[16,32,768]{2,1,0:T(8,128)(2,1)S(1)} all-to-all(bf16[16,32,768]{2,1,0:T(8,128)(2,1)S(1)} %get-tuple-element.16), channel_id=1, replica_groups=mesh['x'=4,'z'=8,'y'=4,'c'=2] {'x','y'}, dimensions={0} | all-to-all | bytes 1572864 | tf_op jit(solution)/shard_map/all_to_all | solution.py:327
  153.9 0.1 fold.5
  154.0 13.1 %all_to_all.51.parts_ref = bf16[8,32,768]{2,1,0:T(8,128)(2,1)S(1)} all-to-all(bf16[8,32,768]{2,1,0:T(8,128)(2,1)S(1)} %fold.5), channel_id=1, replica_groups=mesh['x'=4,'z'=8,'y'=4,'c'=2] {'z'}, dimensions={0} | all-to-all | bytes 786432 | tf_op jit(solution)/shard_map/all_to_all | solution.py:327
  167.1 0.1 fold_both.1
  167.2 0.0 copy-start.1
  167.2 0.9 copy-done.1
  168.1 3.6 %all-to-all-start.8 = ((bf16[16,32,768]{2,1,0:T(8,128)(2,1)}), bf16[16,32,768]{2,1,0:T(8,128)(2,1)S(1)}, u32[]{:S(2)}, u32[]{:S(2)}) async-start(bf16[16,32,768]{2,1,0:T(8,128)(2,1)} %copy-done.1), calls=%async_computation.8 | async-start | bytes 1572864 | tf_op jit(solution)/shard_map/all_to_all | solution.py:327
  171.8 2.1 %slice.43 = bf16[16,32,768]{2,1,0:T(8,128)(2,1)} slice(bf16[16,72,768]{2,1,0:T(8,128)(2,1)} %all-to-all-done.1.packet_ref), slice={[0:16], [32:64], [0:768]} | slice | bytes 1572864 | tf_op jit(solution)/shard_map/slice | solution.py:355
  173.8 10.0 %collective-permute-start = (bf16[16,32,768]{2,1,0:T(8,128)(2,1)}, bf16[16,32,768]{2,1,0:T(8,128)(2,1)}, u32[]{:S(2)}, u32[]{:S(2)}) collective-permute-start(bf16[16,32,768]{2,1,0:T(8,128)(2,1)} %slice.43), channel_id=1, source_target_pairs={{0,1},{1,0},{2,3},{3,2},{4,5},{5,4},{6,7},{7,6},{8,9},{9,8},{10,11... | collective-permute-start | bytes 2359304 | tf_op jit(solution)/shard_map/ppermute | solution.py:355
  183.8 0.0 all-to-all-done.8.mine_ref
  183.8 9.4 %collective-permute-start.1 = (bf16[16,32,768]{2,1,0:T(8,128)(2,1)S(1)}, bf16[16,32,768]{2,1,0:T(8,128)(2,1)}, u32[]{:S(2)}, u32[]{:S(2)}) collective-permute-start(bf16[16,32,768]{2,1,0:T(8,128)(2,1)S(1)} %all-to-all-done.8.mine_ref), channel_id=1, source_target_pairs={{0,1},{1,0},{2,3},{3,2},{4,5},{5,4},{6,7},{7,6},{8,9},{9,8},{10,11... | collective-permute-start | bytes 2359304 | tf_op jit(solution)/shard_map/ppermute | solution.py:370
  193.3 0.6 dynamic-slice_bitcast_fusion
  193.8 2.6 %fusion.6 = f32[4,768]{1,0:T(4,128)} fusion(f32[768,768]{1,0:T(8,128)S(1)} %copy-done, f32[32,768]{1,0:T(8,128)S(1)} %get-tuple-element.17, s32[]{:T(128)S(6)} %select_n.7), kind=kOutput, calls=%fused_computation.13 | convolution fusion | flops 28311552 | bytes 2383876 | tf_op jit(solution)/shard_map/dot_general | solution.py:374
  196.5 0.0 collective-permute-done.raw_ref
  196.5 0.0 collective-permute-done.1.other_ref
  196.5 4.9 %final.1 = f32[768,768]{1,0:T(8,128)} custom-call(s32[1]{0:T(128)} %bitcast.1.core_ref, bf16[16,72,768]{2,1,0:T(8,128)(2,1)} %all-to-all-done.1.packet_ref, bf16[16,32,768]{2,1,0:T(8,128)(2,1)} %collective-permute-done.raw_ref, bf16[16,32,768]{2,1,0:T(8,128)(2,1)S(1)} %all-to-all-done.8.mine_ref, bf16[16,32,768]{2,1,0:T(8,128)(2,1)} %collective-permute-done.1.other_ref), custom_call_target="tpu_custom_call" | custom-call | tf_op jit(solution)/shard_map/final/pallas_call | solution.py:317
  (9 shorter events, 0.2 us)
Async XLA Ops:
  0.6 1.7 copy-start
  22.2 29.0 %all-to-all-start.1 = ((bf16[16,72,768]{2,1,0:T(8,128)(2,1)}), bf16[16,72,768]{2,1,0:T(8,128)(2,1)}, u32[]{:S(2)}, u32[]{:S(2)}) async-start(bf16[16,72,768]{2,1,0:T(8,128)(2,1)} %broadcast_in_dim.5), calls=%async_computation.1 | async-start | bytes 3538944 | tf_op jit(solution)/shard_map/all_to_all | solution.py:327
  167.2 0.9 copy-start.1
  168.1 15.7 %all-to-all-start.8 = ((bf16[16,32,768]{2,1,0:T(8,128)(2,1)}), bf16[16,32,768]{2,1,0:T(8,128)(2,1)S(1)}, u32[]{:S(2)}, u32[]{:S(2)}) async-start(bf16[16,32,768]{2,1,0:T(8,128)(2,1)} %copy-done.1), calls=%async_computation.8 | async-start | bytes 1572864 | tf_op jit(solution)/shard_map/all_to_all | solution.py:327
  173.8 22.6 %collective-permute-start = (bf16[16,32,768]{2,1,0:T(8,128)(2,1)}, bf16[16,32,768]{2,1,0:T(8,128)(2,1)}, u32[]{:S(2)}, u32[]{:S(2)}) collective-permute-start(bf16[16,32,768]{2,1,0:T(8,128)(2,1)} %slice.43), channel_id=1, source_target_pairs={{0,1},{1,0},{2,3},{3,2},{4,5},{5,4},{6,7},{7,6},{8,9},{9,8},{10,11... | collective-permute-start | bytes 2359304 | tf_op jit(solution)/shard_map/ppermute | solution.py:355
  183.8 12.6 %collective-permute-start.1 = (bf16[16,32,768]{2,1,0:T(8,128)(2,1)S(1)}, bf16[16,32,768]{2,1,0:T(8,128)(2,1)}, u32[]{:S(2)}, u32[]{:S(2)}) collective-permute-start(bf16[16,32,768]{2,1,0:T(8,128)(2,1)S(1)} %all-to-all-done.8.mine_ref), channel_id=1, source_target_pairs={{0,1},{1,0},{2,3},{3,2},{4,5},{5,4},{6,7},{7,6},{8,9},{9,8},{10,11... | collective-permute-start | bytes 2359304 | tf_op jit(solution)/shard_map/ppermute | solution.py:370

commit v3 on v2

v3 whole, which is shorter than its diff:
```python
import functools

import jax
import jax.numpy as jnp
from jax import lax
from jax.experimental import pallas as pl
from jax.experimental.pallas import tpu as pltpu
from jax.sharding import Mesh, PartitionSpec as P

POS = 4
ALL = ("x", "z", "y", "c")
XY = ("x", "y")
LANES = 128
BF16 = jnp.bfloat16
F32 = jnp.float32


def params():
    return pltpu.CompilerParams(vmem_limit_bytes=26 * 1024 * 1024)


def columns_to_rows(columns):
    rows = columns[0].shape[0]
    lane = lax.broadcasted_iota(jnp.int32, (rows, LANES), 1)
    table = jnp.zeros((rows, LANES), F32)
    for k, column in enumerate(columns):
        table = jnp.where(lane == k, column, table)
    return table.T[:8]


def rows_to_columns(rows):
    wide = jnp.concatenate([rows, jnp.zeros((LANES - 8, rows.shape[1]), F32)], axis=0)
    return wide.T


def score_kernel(shard_ref, packet_ref, passages_ref, scores_ref, pos_ref, ids_ref, chunk, found):
    groups, plane, _ = packet_ref.shape
    rows, dim = passages_ref.shape
    queries = groups * plane
    width = 512

    codes = packet_ref[:, :, 2 * dim :].reshape(queries, LANES).astype(F32).astype(jnp.int32)
    for k in range(POS):
        high, mid, low = (codes[:, k + POS * part : k + POS * part + 1] for part in range(3))
        ids = (high << 14) + (mid << 7) + low - shard_ref[0] * rows
        ids = jnp.broadcast_to(ids, (queries, LANES))
        ids_ref[k] = ids
        chunk[k] = ids >> 7
    found[...] = jnp.zeros_like(found)

    def product(j):
        at = pl.multiple_of(j * width, width)
        emb = packet_ref[:, :, :dim].reshape(queries, dim)
        scores_ref[:, pl.ds(at, width)] = lax.dot_general(
            emb, passages_ref[pl.ds(at, width), :], (((1,), (1,)), ((), ())), preferred_element_type=F32
        )

    def extract(j):
        first = j * (width // LANES)
        for tile in range(queries // 8):
            here = slice(tile * 8, tile * 8 + 8)
            scores = [
                scores_ref[here, pl.ds(pl.multiple_of(j * width + c * LANES, LANES), LANES)]
                for c in range(width // LANES)
            ]
            for k in range(POS):
                want = chunk[k, here, :] - first
                best = found[k, here, :]
                for c, s in enumerate(scores):
                    best = jnp.where(want == c, s, best)
                found[k, here, :] = best

    def step(j, carry):
        extract(j - 1)
        product(j)
        return carry

    steps = rows // width
    product(0)
    lax.fori_loop(1, steps, step, 0)
    extract(steps - 1)

    lane = lax.broadcasted_iota(jnp.int32, (queries, LANES), 1)
    columns = []
    for k in range(POS):
        hit = lane == (ids_ref[k] & (LANES - 1))
        columns.append(jnp.sum(jnp.where(hit, found[k], 0.0), axis=1, keepdims=True))
    table = columns_to_rows(columns)
    for g in range(groups):
        pos_ref[g] = table


def score_call(shard, packet, passages):
    rows, dim = passages.shape
    groups, plane, _ = packet.shape
    queries = groups * plane
    return pl.pallas_call(
        score_kernel,
        in_specs=[pl.BlockSpec(memory_space=pltpu.SMEM)] + [pl.BlockSpec(memory_space=pltpu.VMEM)] * 2,
        out_shape=[
            jax.ShapeDtypeStruct((queries, rows), F32),
            jax.ShapeDtypeStruct((groups, 8, queries), F32),
            jax.ShapeDtypeStruct((POS, queries, LANES), jnp.int32),
        ],
        scratch_shapes=[
            pltpu.VMEM((POS, queries, LANES), jnp.int32),
            pltpu.VMEM((POS, queries, LANES), F32),
        ],
        compiler_params=params(),
        cost_estimate=pl.CostEstimate(
            flops=4 * queries * rows * dim, bytes_accessed=rows * dim * 2 + queries * rows * 4, transcendentals=0
        ),
        name="score",
    )(shard, packet, passages)


def sigmoid_kernel(scale, pos_ref, scores_ref, slopes_ref, sums_ref, pos, sums):
    queries, width = scores_ref.shape
    size = 16
    rows = pos_ref[0]
    for g in range(1, pos_ref.shape[0]):
        rows = rows + pos_ref[g]
    pos[...] = rows_to_columns(rows)

    def tile(t, carry):
        at = pl.ds(pl.multiple_of(t * size, size), size)
        columns = pos[at, :]
        p = [jnp.broadcast_to(columns[:, k : k + 1], (size, LANES)) for k in range(POS)]
        slope_acc = [jnp.zeros((size, LANES), F32) for _ in range(POS)]
        loss_acc = jnp.zeros((size, LANES), F32)
        for c in range(width // LANES):
            s = scores_ref[at, c * LANES : (c + 1) * LANES]
            sigs = [jax.nn.sigmoid(s - p[k]) for k in range(POS)]
            slopes = [sig * (1.0 - sig) for sig in sigs]
            loss_acc = loss_acc + ((sigs[0] + sigs[1]) + (sigs[2] + sigs[3]))
            slope_acc = [slope_acc[k] + slopes[k] for k in range(POS)]
            both = (slopes[0] + slopes[1]) + (slopes[2] + slopes[3])
            slopes_ref[at, c * LANES : (c + 1) * LANES] = both * scale
        for k in range(POS):
            sums[k, at, :] = slope_acc[k]
        sums[POS, at, :] = loss_acc
        return carry

    lax.fori_loop(0, queries // size, tile, 0)
    columns = [jnp.sum(sums[k], axis=1, keepdims=True) * (scale if k == POS else -scale) for k in range(POS + 1)]
    rows = columns_to_rows(columns)
    for g in range(sums_ref.shape[0]):
        sums_ref[g] = rows


def sigmoid_call(pos, scores, scale, groups):
    queries, width = scores.shape
    return pl.pallas_call(
        functools.partial(sigmoid_kernel, scale),
        in_specs=[pl.BlockSpec(memory_space=pltpu.VMEM)] * 2,
        out_shape=[
            jax.ShapeDtypeStruct((queries, width), F32),
            jax.ShapeDtypeStruct((groups, 8, queries), F32),
        ],
        scratch_shapes=[
            pltpu.VMEM((queries, LANES), F32),
            pltpu.VMEM((POS + 1, queries, LANES), F32),
        ],
        compiler_params=params(),
        cost_estimate=pl.CostEstimate(
            flops=40 * queries * width, bytes_accessed=queries * width * 8, transcendentals=8 * queries * width
        ),
        name="sigmoid",
    )(pos, scores)


def grad_kernel(sums_ref, slopes_ref, passages_ref, ids_ref, part_ref, total_ref, grads, left_a, left_b, acc):
    queries, rows = slopes_ref.shape
    width = left_a.shape[1]
    table = sums_ref[0]
    for g in range(1, sums_ref.shape[0]):
        table = table + sums_ref[g]
    total_ref[...] = table
    columns = rows_to_columns(table)
    for k in range(POS):
        give = columns[:, k : k + 1]
        for other in range(POS):
            if other != k:
                same = ids_ref[k] == ids_ref[other]
                give = give + jnp.where(same, columns[:, other : other + 1], 0.0)
        grads[k] = jnp.broadcast_to(give, (queries, LANES))

    def build(left, j):
        lane = lax.broadcasted_iota(jnp.int32, (16, LANES), 1) + j * width
        for tile in range(queries // 16):
            here = slice(tile * 16, tile * 16 + 16)
            want = [ids_ref[k, here, :] - lane for k in range(POS)]
            give = [grads[k, here, :] for k in range(POS)]
            for c in range(width // LANES):
                extra = jnp.zeros((16, LANES), F32)
                for k in range(POS):
                    extra = jnp.where(want[k] == c * LANES, give[k], extra)
                at = pl.ds(pl.multiple_of(j * width + c * LANES, LANES), LANES)
                left[here, c * LANES : (c + 1) * LANES] = (slopes_ref[here, at] + extra).astype(BF16)

    def product(left, j):
        block = passages_ref[pl.ds(pl.multiple_of(j * width, width), width), :]
        return jnp.dot(left[...], block, preferred_element_type=F32)

    steps = rows // width
    build(left_a, 0)
    for j in range(steps):
        now, later = (left_a, left_b) if j % 2 == 0 else (left_b, left_a)
        if j + 1 < steps:
            build(later, j + 1)
        term = product(now, j)
        if j == 0:
            acc[...] = term
        elif j + 1 < steps:
            acc[...] += term
        else:
            part_ref[...] = (acc[...] + term).astype(BF16).reshape(part_ref.shape)


def grad_call(sums, slopes, passages, ids, groups, block=1024):
    rows, dim = passages.shape
    queries = slopes.shape[0]
    return pl.pallas_call(
        grad_kernel,
        in_specs=[pl.BlockSpec(memory_space=pltpu.VMEM)] * 4,
        out_shape=[
            jax.ShapeDtypeStruct((groups, queries // groups, dim), BF16),
            jax.ShapeDtypeStruct((8, queries), F32),
        ],
        scratch_shapes=[
            pltpu.VMEM((POS, queries, LANES), F32),
            pltpu.VMEM((queries, block), BF16),
            pltpu.VMEM((queries, block), BF16),
            pltpu.VMEM((queries, dim), F32),
        ],
        compiler_params=params(),
        cost_estimate=pl.CostEstimate(
            flops=4 * queries * rows * dim, bytes_accessed=rows * dim * 2 + queries * rows * 4, transcendentals=0
        ),
        name="grad",
    )(sums, slopes, passages, ids)


def fold_kernel(parts_ref, out_ref):
    acc = parts_ref[0].astype(F32)
    for g in range(1, parts_ref.shape[0]):
        acc = acc + parts_ref[g].astype(F32)
    for g in range(out_ref.shape[0]):
        out_ref[g] = acc.astype(out_ref.dtype)


def fold_call(parts, n):
    return pl.pallas_call(
        fold_kernel,
        out_shape=jax.ShapeDtypeStruct((n,) + parts.shape[1:], parts.dtype),
        compiler_params=params(),
        name="fold",
    )(parts)


def fold_both_kernel(parts_ref, out_ref, sum_ref):
    acc = parts_ref[0].astype(F32)
    for g in range(1, parts_ref.shape[0]):
        acc = acc + parts_ref[g].astype(F32)
    sum_ref[...] = acc
    for g in range(out_ref.shape[0]):
        out_ref[g] = acc.astype(out_ref.dtype)


def fold_both_call(parts, n):
    return pl.pallas_call(
        fold_both_kernel,
        out_shape=[
            jax.ShapeDtypeStruct((n,) + parts.shape[1:], parts.dtype),
            jax.ShapeDtypeStruct(parts.shape[1:], F32),
        ],
        compiler_params=params(),
        name="fold_both",
    )(parts)


def final_kernel(core_ref, packet_ref, peer_ref, mine_ref, other_ref, out_ref):
    groups, plane, dim = mine_ref.shape
    queries = groups * plane

    def term(raw, grads):
        return lax.dot_general(raw, grads, (((0,), (0,)), ((), ())), preferred_element_type=F32)

    def both(first, second):
        out_ref[...] = term(*first)
        out_ref[...] += term(*second)

    own = (packet_ref[:, :, dim : 2 * dim].reshape(queries, dim), mine_ref[...].reshape(queries, dim))
    peer = (peer_ref[:, :, dim : 2 * dim].reshape(queries, dim), other_ref[...].reshape(queries, dim))

    @pl.when(core_ref[0] == 0)
    def _():
        both(own, peer)

    @pl.when(core_ref[0] != 0)
    def _():
        both(peer, own)


def final_call(core, packet, peer, mine, other):
    dim = mine.shape[-1]
    return pl.pallas_call(
        final_kernel,
        in_specs=[pl.BlockSpec(memory_space=pltpu.SMEM)] + [pl.BlockSpec(memory_space=pltpu.VMEM)] * 4,
        out_shape=jax.ShapeDtypeStruct((dim, dim), F32),
        compiler_params=params(),
        name="final",
    )(core, packet, peer, mine, other)


def exchange(v, axes):
    return lax.all_to_all(v, axes, 0, 0, tiled=False)


def spread(v, axes):
    return exchange(jnp.broadcast_to(v[None], (lax.axis_size(axes),) + v.shape), axes)


def shards(queries_raw, projection, passages, positives):
    hp = lax.Precision.HIGHEST
    rows, dim = passages.shape
    own = queries_raw.shape[0]
    nz, nxy = lax.axis_size("z"), lax.axis_size(XY)
    plane = nz * own
    scale = 1.0 / (4.0 * rows * nz * nxy)
    core = lax.axis_index("c")
    swap = [(0, 1), (1, 0)]

    projected = jnp.dot(queries_raw, projection, precision=hp, preferred_element_type=F32)
    ids = jnp.concatenate([positives >> 14, (positives >> 7) & 127, positives & 127], axis=1)
    ids = jnp.pad(ids, ((0, 0), (0, LANES - 3 * POS)))
    packet = jnp.concatenate([projected.astype(BF16), queries_raw.astype(BF16), ids.astype(BF16)], axis=1)
    shard = (lax.axis_index("x") * nz + lax.axis_index("z")) * lax.axis_size("y") + lax.axis_index("y")
    packet, shard = lax.optimization_barrier((packet, shard))
    packet = spread(packet, "z").reshape(plane, 2 * dim + LANES)
    packet = spread(packet, XY)
    peer = lax.ppermute(packet, "c", swap)

    scores, pos, local_pos = score_call(shard.reshape(1), packet, passages)
    pos = exchange(fold_call(exchange(pos, XY), nz), "z")
    pos, peer = lax.optimization_barrier((pos, peer))
    slopes, sums = sigmoid_call(pos, scores, scale, nxy)
    sums = exchange(fold_call(exchange(sums, XY), nz), "z")
    part, sums = grad_call(sums, slopes, passages, local_pos, nxy)

    part = exchange(fold_call(exchange(part, XY), nz), "z")
    part, summed = fold_both_call(part, nxy)
    mine = exchange(part, XY)
    other = lax.ppermute(mine, "c", swap)

    home = lax.axis_index("z") * own
    query_grad = lax.dynamic_slice_in_dim(summed, home, own, 0)
    grad_raw = jnp.dot(query_grad, projection.T, precision=hp, preferred_element_type=F32)
    first = lax.axis_index(XY) * plane + home
    loss = lax.dynamic_slice_in_dim(sums[POS], first, own, 0)
    grad_projection = final_call(core.reshape(1), packet, peer, mine, other)
    return (loss, grad_raw, grad_projection)


def solution(mesh):
    axes = Mesh(mesh.devices.reshape(4, 8, 4, 2), ALL)
    in_specs = (P(ALL, None), P(), P(("x", "z", "y"), None), P(ALL, None))
    out_specs = (P(ALL), P(ALL, None), P())
    return jax.shard_map(shards, mesh=axes, in_specs=in_specs, out_specs=out_specs, check_vma=False)
```

time: 202 us -> 190 us (0.941)
  blocking collectives: 86.8 us -> 126 us
  waiting for transfers between devices: 22.2 us -> 0.01 us
  Pallas kernels: 49 us -> 30.1 us
  starting transfers between devices: 29.8 us -> 13.3 us
  local copies, waits for them, and re-layouts: 5.46 us -> 12.4 us
    all_to_all x7 -> x9, blocking collectives: 86.8 us -> 126 us  [exchange(): return lax.all_to_all(v, axes, 0, 0, tiled=False)]
    all_to_all x2 -> x0, waiting for transfers between devices: 22.2 us -> none  [exchange(): return lax.all_to_all(v, axes, 0, 0, tiled=False)]
    pallas_call x3, Pallas kernels: 43.8 us -> 25.7 us  [the longest x1 12.1 us: sigmoid_call(): pl.pallas_call(functools.partial(sigmoid_kernel, scale), in_specs=[pl.Blo...]
    unnamed x4 -> x24, local copies, waits for them, and re-layouts: 1.04 us -> 11.6 us
    all_to_all x2 -> x0, starting transfers between devices: 10.4 us -> none  [exchange(): return lax.all_to_all(v, axes, 0, 0, tiled=False)]
    ppermute x1, starting transfers between devices: 10 us -> 3.72 us  [shards(): peer = lax.ppermute(packet, 'c', swap)]
    slice x3 -> x0, local copies, waits for them, and re-layouts: 2.08 us -> none  [the longest x1 2.07 us: shards(): raw_other = lax.ppermute(packet[:, plane:2 * plane, :], 'c', swap)]
  transfers between devices with their start and end apart: 4 -> 2, of which waited for: 1 -> 0; matrix products, arithmetic and copies ran while one was open for 3% -> 2% of each run, Pallas kernels for 0% -> 3%
where the time goes in v3:
time: 190 us; the launch traced here: 189 us
  blocking collectives  126 us (66%)
  Pallas kernels  30.1 us (16%)
  starting transfers between devices  13.3 us (7%)
  local copies, waits for them, and re-layouts  12.4 us (7%)
  matrix products  4.53 us (2%)
    all_to_all x9, blocking collectives, exchange(): return lax.all_to_all(v, axes, 0, 0, tiled=False)  126 us
    pallas_call x1, Pallas kernels, sigmoid_call(): pl.pallas_call(functools.partial(sigmoid_kernel, scale), in_specs=[pl.Blo...  12.1 us
    unnamed x24, local copies, waits for them, and re-layouts  11.6 us
    ppermute x1, starting transfers between devices, shards(): other = lax.ppermute(mine, 'c', swap)  9.54 us
    pallas_call x1, Pallas kernels, grad_call(): pl.pallas_call(grad_kernel, in_specs=[pl.BlockSpec(memory_space=pltpu.VME...  7.08 us
    pallas_call x1, Pallas kernels, score_call(): pl.pallas_call(score_kernel, in_specs=[pl.BlockSpec(memory_space=pltpu.SM...  6.5 us
    pallas_call x1, Pallas kernels, final_call(): pl.pallas_call(final_kernel, in_specs=[pl.BlockSpec(memory_space=pltpu.SM...  4.15 us
  transfers between devices with their start and end apart: 2, of which 0 were waited for; matrix products, arithmetic and copies ran while one was open for 2% of the time, Pallas kernels for 3%

profile of v3, /device:TPU:1, one launch (start us, length us, event | category | flops | bytes accessed | tf_op | source)
XLA Modules:
  0.0 189.0 jit_solution(16630748250451865145)
XLA Ops:
  0.6 0.0 copy-start
  0.7 0.8 shift-right-arithmetic_convert_fusion
  1.5 0.7 convert_element_type.8
  2.2 0.1 copy-done
  2.3 1.9 %convolution_convert_fusion = bf16[4,768]{1,0:T(4,128)(2,1)S(1)} fusion(f32[4,768]{1,0:T(4,128)} %param.4, f32[768,768]{1,0:T(8,128)S(1)} %copy-done), kind=kOutput, calls=%fused_computation | convolution fusion | flops 28314624 | bytes 2377728 | tf_op jit(solution)/shard_map/dot_general | solution.py:334
  4.2 0.1 fusion.6
  4.4 16.4 %all_to_all.45 = bf16[8,4,1664]{2,1,0:T(4,128)(2,1)S(1)} all-to-all(bf16[8,4,1664]{2,1,0:T(4,128)(2,1)S(1)} %broadcast_in_dim.6), channel_id=1, replica_groups=mesh['x'=4,'z'=8,'y'=4,'c'=2] {'z'}, dimensions={0} | all-to-all | bytes 212992 | tf_op jit(solution)/shard_map/all_to_all | solution.py:317
  20.8 0.1 broadcast_in_dim.15
  20.9 27.8 %all_to_all.46.packet_ref = bf16[16,32,1664]{2,1,0:T(8,128)(2,1)S(1)} all-to-all(bf16[16,32,1664]{2,1,0:T(8,128)(2,1)S(1)} %broadcast_in_dim.15), channel_id=1, replica_groups=mesh['x'=4,'z'=8,'y'=4,'c'=2] {'x','y'}, dimensions={0} | all-to-all | bytes 3407872 | tf_op jit(solution)/shard_map/all_to_all | solution.py:317
  48.6 0.0 copy-start.1
  48.7 3.7 %collective-permute-start = (bf16[16,32,1664]{2,1,0:T(8,128)(2,1)S(1)}, bf16[16,32,1664]{2,1,0:T(8,128)(2,1)S(1)}, u32[]{:S(2)}, u32[]{:S(2)}) collective-permute-start(bf16[16,32,1664]{2,1,0:T(8,128)(2,1)S(1)} %all_to_all.46.packet_ref), channel_id=1, source_target_pairs={{0,1},{1,0},{2,3},{3,2},{4,5},{5,4},{6,7},{7,6},{8,9},{9,8},{10,11... | collective-permute-start | bytes 5111816 | tf_op jit(solution)/shard_map/ppermute | solution.py:342
  52.4 0.0 copy-start.5
  52.4 2.8 %copy-done.5 = bf16[4096,768]{1,0:T(8,128)(2,1)S(1)} copy-done((bf16[4096,768]{1,0:T(8,128)(2,1)S(1)}, bf16[4096,768]{1,0:T(8,128)(2,1)}, u32[]{:S(2)}) %copy-start.5) | copy-done | bytes 6291480
  55.2 6.5 %score.1 = (f32[512,4096]{1,0:T(8,128)S(1)}, f32[16,8,512]{2,1,0:T(8,128)S(1)}, s32[4,512,128]{2,1,0:T(8,128)S(1)}) custom-call(s32[1]{0:T(128)} %bitcast.shard_ref, bf16[16,32,1664]{2,1,0:T(8,128)(2,1)S(1)} %all_to_all.46.packet_ref, bf16[4096,768]{1,0:T(8,128)(2,1)S(1)} %copy-done.5), custom_call_target="tpu_custom_call" | custom-call | flops 6442450944 | bytes 14680064 | tf_op jit(solution)/shard_map/score/pallas_call | solution.py:97
  61.7 0.0 copy-done.1
  61.7 0.0 copy-start.6
  61.7 3.2 %copy-done.6 = f32[512,4096]{1,0:T(8,128)} copy-done((f32[512,4096]{1,0:T(8,128)}, f32[512,4096]{1,0:T(8,128)S(1)}, u32[]{:S(2)}) %copy-start.6) | copy-done | bytes 8388632
  64.9 0.0 copy-start.8
  64.9 0.0 slice-start
  64.9 10.9 %all_to_all.47.parts_ref = f32[16,8,512]{2,1,0:T(8,128)S(1)} all-to-all(f32[16,8,512]{2,1,0:T(8,128)S(1)} %get-tuple-element.18), channel_id=1, replica_groups=mesh['x'=4,'z'=8,'y'=4,'c'=2] {'x','y'}, dimensions={0} | all-to-all | bytes 524288 | tf_op jit(solution)/shard_map/all_to_all | solution.py:317
  75.9 10.4 %all_to_all.48.pos_ref = f32[8,8,512]{2,1,0:T(8,128)S(1)} all-to-all(f32[8,8,512]{2,1,0:T(8,128)S(1)} %fold.3), channel_id=1, replica_groups=mesh['x'=4,'z'=8,'y'=4,'c'=2] {'z'}, dimensions={0} | all-to-all | bytes 262144 | tf_op jit(solution)/shard_map/all_to_all | solution.py:317
  86.3 0.0 collective-permute-done.peer_ref
  86.3 0.0 copy-done.8
  86.3 0.0 copy-start.7
  86.3 4.0 %copy-done.7 = f32[512,4096]{1,0:T(8,128)S(1)} copy-done((f32[512,4096]{1,0:T(8,128)S(1)}, f32[512,4096]{1,0:T(8,128)}, u32[]{:S(2)}) %copy-start.7) | copy-done | bytes 8388632
  90.3 0.0 slice-start.1
  90.3 0.0 copy-start.9
  90.3 12.1 %sigmoid.1 = (f32[512,4096]{1,0:T(8,128)S(1)}, f32[16,8,512]{2,1,0:T(8,128)S(1)}) custom-call(f32[8,8,512]{2,1,0:T(8,128)S(1)} %all_to_all.48.pos_ref, f32[512,4096]{1,0:T(8,128)S(1)} %copy-done.7), custom_call_target="tpu_custom_call" | custom-call | flops 83886080 | bytes 16777216 | tf_op jit(solution)/shard_map/sigmoid/pallas_call | solution.py:153
  102.4 0.0 copy-done.3
  102.5 10.6 %all_to_all.49.parts_ref = f32[16,8,512]{2,1,0:T(8,128)S(1)} all-to-all(f32[16,8,512]{2,1,0:T(8,128)S(1)} %get-tuple-element.21), channel_id=1, replica_groups=mesh['x'=4,'z'=8,'y'=4,'c'=2] {'x','y'}, dimensions={0} | all-to-all | bytes 524288 | tf_op jit(solution)/shard_map/all_to_all | solution.py:317
  113.0 10.3 %all_to_all.50.sums_ref = f32[8,8,512]{2,1,0:T(8,128)S(1)} all-to-all(f32[8,8,512]{2,1,0:T(8,128)S(1)} %fold.4), channel_id=1, replica_groups=mesh['x'=4,'z'=8,'y'=4,'c'=2] {'z'}, dimensions={0} | all-to-all | bytes 262144 | tf_op jit(solution)/shard_map/all_to_all | solution.py:317
  123.4 0.0 slice-done
  123.4 0.0 slice-done.1
  123.4 0.0 copy-done.9
  123.4 7.1 %grad.1 = (bf16[16,32,768]{2,1,0:T(8,128)(2,1)S(1)}, f32[8,512]{1,0:T(8,128)S(1)}) custom-call(f32[8,8,512]{2,1,0:T(8,128)S(1)} %all_to_all.50.sums_ref, f32[512,4096]{1,0:T(8,128)S(1)} %get-tuple-element.22.slopes_ref, bf16[4096,768]{1,0:T(8,128)(2,1)S(1)} %bitcast.8, s32[4,512,128]{2,1,0:T(8,128)S(1)} %copy-done.9), custom_call_target="tpu_custom_call" | custom-call | flops 6442450944 | bytes 14680064 | tf_op jit(solution)/shard_map/grad/pallas_call | solution.py:223
  130.5 13.4 %all_to_all.51.parts_ref = bf16[16,32,768]{2,1,0:T(8,128)(2,1)S(1)} all-to-all(bf16[16,32,768]{2,1,0:T(8,128)(2,1)S(1)} %get-tuple-element.25), channel_id=1, replica_groups=mesh['x'=4,'z'=8,'y'=4,'c'=2] {'x','y'}, dimensions={0} | all-to-all | bytes 1572864 | tf_op jit(solution)/shard_map/all_to_all | solution.py:317
  143.8 0.1 fold.5
  143.9 13.3 %all_to_all.52.parts_ref = bf16[8,32,768]{2,1,0:T(8,128)(2,1)S(1)} all-to-all(bf16[8,32,768]{2,1,0:T(8,128)(2,1)S(1)} %fold.5), channel_id=1, replica_groups=mesh['x'=4,'z'=8,'y'=4,'c'=2] {'z'}, dimensions={0} | all-to-all | bytes 786432 | tf_op jit(solution)/shard_map/all_to_all | solution.py:317
  157.2 0.1 fold_both.1
  157.3 13.3 %all_to_all.53.mine_ref = bf16[16,32,768]{2,1,0:T(8,128)(2,1)S(1)} all-to-all(bf16[16,32,768]{2,1,0:T(8,128)(2,1)S(1)} %get-tuple-element.28), channel_id=1, replica_groups=mesh['x'=4,'z'=8,'y'=4,'c'=2] {'x','y'}, dimensions={0} | all-to-all | bytes 1572864 | tf_op jit(solution)/shard_map/all_to_all | solution.py:317
  170.7 9.5 %collective-permute-start.1 = (bf16[16,32,768]{2,1,0:T(8,128)(2,1)S(1)}, bf16[16,32,768]{2,1,0:T(8,128)(2,1)}, u32[]{:S(2)}, u32[]{:S(2)}) collective-permute-start(bf16[16,32,768]{2,1,0:T(8,128)(2,1)S(1)} %all_to_all.53.mine_ref), channel_id=1, source_target_pairs={{0,1},{1,0},{2,3},{3,2},{4,5},{5,4},{6,7},{7,6},{8,9},{9,8},{10,11... | collective-permute-start | bytes 2359304 | tf_op jit(solution)/shard_map/ppermute | solution.py:354
  180.2 0.0 copy-start.2
  180.2 0.6 dynamic-slice_bitcast_fusion
  180.8 2.6 %fusion = f32[4,768]{1,0:T(4,128)} fusion(f32[768,768]{1,0:T(8,128)S(1)} %copy-done, f32[32,768]{1,0:T(8,128)S(1)} %get-tuple-element.26, s32[]{:T(128)S(6)} %select_n.7), kind=kOutput, calls=%fused_computation.2 | convolution fusion | flops 28311552 | bytes 2383876 | tf_op jit(solution)/shard_map/dot_general | solution.py:358
  183.4 0.0 collective-permute-done.1.other_ref
  183.4 0.0 copy-done.2
  183.4 1.5 copy-done.4
  184.9 4.2 %final.1 = f32[768,768]{1,0:T(8,128)} custom-call(s32[1]{0:T(128)} %bitcast.2.core_ref, bf16[16,32,1664]{2,1,0:T(8,128)(2,1)S(1)} %copy-done.2, bf16[16,32,1664]{2,1,0:T(8,128)(2,1)S(1)} %copy-done.4, bf16[16,32,768]{2,1,0:T(8,128)(2,1)S(1)} %all_to_all.53.mine_ref, bf16[16,32,768]{2,1,0:T(8,128)(2,1)} %collective-permute-done.1.other_ref), custom_call_target="tpu_custom_call" | custom-call | tf_op jit(solution)/shard_map/final/pallas_call | solution.py:307
  (9 shorter events, 0.1 us)
Async XLA Ops:
  0.6 1.7 copy-start
  48.6 13.0 %copy-start.1 = (bf16[16,32,1664]{2,1,0:T(8,128)(2,1)}, bf16[16,32,1664]{2,1,0:T(8,128)(2,1)S(1)}, u32[]{:S(2)}) copy-start(bf16[16,32,1664]{2,1,0:T(8,128)(2,1)S(1)} %all_to_all.46.packet_ref) | copy-start | bytes 5111812
  48.7 37.7 %collective-permute-start = (bf16[16,32,1664]{2,1,0:T(8,128)(2,1)S(1)}, bf16[16,32,1664]{2,1,0:T(8,128)(2,1)S(1)}, u32[]{:S(2)}, u32[]{:S(2)}) collective-permute-start(bf16[16,32,1664]{2,1,0:T(8,128)(2,1)S(1)} %all_to_all.46.packet_ref), channel_id=1, source_target_pairs={{0,1},{1,0},{2,3},{3,2},{4,5},{5,4},{6,7},{7,6},{8,9},{9,8},{10,11... | collective-permute-start | bytes 5111816 | tf_op jit(solution)/shard_map/ppermute | solution.py:342
  52.4 2.8 %copy-start.5 = (bf16[4096,768]{1,0:T(8,128)(2,1)S(1)}, bf16[4096,768]{1,0:T(8,128)(2,1)}, u32[]{:S(2)}) copy-start(bf16[4096,768]{1,0:T(8,128)(2,1)} %passages_ref.3) | copy-start | bytes 18874372
  61.7 3.2 %copy-start.6 = (f32[512,4096]{1,0:T(8,128)}, f32[512,4096]{1,0:T(8,128)S(1)}, u32[]{:S(2)}) copy-start(f32[512,4096]{1,0:T(8,128)S(1)} %get-tuple-element.20.scores_ref) | copy-start | bytes 25165828
  64.9 21.4 %copy-start.8 = (s32[4,512,128]{2,1,0:T(8,128)}, s32[4,512,128]{2,1,0:T(8,128)S(1)}, u32[]{:S(2)}) copy-start(s32[4,512,128]{2,1,0:T(8,128)S(1)} %get-tuple-element.23.ids_ref) | copy-start | bytes 3145732
  64.9 58.4 %slice-start = ((s8[6291456]{0:T(1024)(128)(4,1)}), s8[2097152]{0:T(1024)(128)(4,1)S(1)}, s32[]{:S(2)}) async-start(s8[6291456]{0:T(1024)(128)(4,1)} %bitcast.7), calls=%async_computation.9 | async-start | bytes 4194304
  86.3 16.1 %copy-start.3 = (bf16[16,32,1664]{2,1,0:T(8,128)(2,1)}, bf16[16,32,1664]{2,1,0:T(8,128)(2,1)S(1)}, u32[]{:S(2)}) copy-start(bf16[16,32,1664]{2,1,0:T(8,128)(2,1)S(1)} %collective-permute-done.peer_ref) | copy-start | bytes 5111812
  86.3 4.0 %copy-start.7 = (f32[512,4096]{1,0:T(8,128)S(1)}, f32[512,4096]{1,0:T(8,128)}, u32[]{:S(2)}) copy-start(f32[512,4096]{1,0:T(8,128)} %copy-done.6) | copy-start | bytes 25165828
  90.3 33.1 %slice-start.1 = ((s8[6291456]{0:T(1024)(128)(4,1)}), s8[4194304]{0:T(1024)(128)(4,1)S(1)}, s32[]{:S(2)}) async-start(s8[6291456]{0:T(1024)(128)(4,1)} %bitcast.7), calls=%async_computation.10 | async-start | bytes 8388608
  90.3 33.1 %copy-start.9 = (s32[4,512,128]{2,1,0:T(8,128)S(1)}, s32[4,512,128]{2,1,0:T(8,128)}, u32[]{:S(2)}) copy-start(s32[4,512,128]{2,1,0:T(8,128)} %copy-done.8) | copy-start | bytes 3145732
  170.7 12.8 %collective-permute-start.1 = (bf16[16,32,768]{2,1,0:T(8,128)(2,1)S(1)}, bf16[16,32,768]{2,1,0:T(8,128)(2,1)}, u32[]{:S(2)}, u32[]{:S(2)}) collective-permute-start(bf16[16,32,768]{2,1,0:T(8,128)(2,1)S(1)} %all_to_all.53.mine_ref), channel_id=1, source_target_pairs={{0,1},{1,0},{2,3},{3,2},{4,5},{5,4},{6,7},{7,6},{8,9},{9,8},{10,11... | collective-permute-start | bytes 2359304 | tf_op jit(solution)/shard_map/ppermute | solution.py:354
  180.2 3.2 %copy-start.2 = (bf16[16,32,1664]{2,1,0:T(8,128)(2,1)S(1)}, bf16[16,32,1664]{2,1,0:T(8,128)(2,1)}, u32[]{:S(2)}) copy-start(bf16[16,32,1664]{2,1,0:T(8,128)(2,1)} %copy-done.1) | copy-start | bytes 5111812
  183.4 1.5 copy-start.4

commit v4 on v3

--- a/solution.py
+++ b/solution.py
@@ -15,8 +15,25 @@
 F32 = jnp.float32
 
 
-def params():
-    return pltpu.CompilerParams(vmem_limit_bytes=26 * 1024 * 1024)
+def params(mib):
+    return pltpu.CompilerParams(vmem_limit_bytes=mib * 1024 * 1024)
+
+
+def passage_copies(far, near, sems):
+    width = near.shape[0] // sems.shape[0]
+
+    def copy(j):
+        at = pl.ds(pl.multiple_of(j * width, width), width)
+        return pltpu.make_async_copy(far.at[at, :], near.at[at, :], sems.at[j])
+
+    return copy
+
+
+def in_three(x):
+    high = x.astype(BF16).astype(F32)
+    rest = x - high
+    mid = rest.astype(BF16).astype(F32)
+    return high, mid, rest - mid
 
 
 def columns_to_rows(columns):
@@ -33,13 +50,17 @@
     return wide.T
 
 
-def score_kernel(shard_ref, packet_ref, passages_ref, scores_ref, pos_ref, ids_ref, chunk, found):
+def score_kernel(shard_ref, packet_ref, raw_ref, passages_hbm, scores_ref, note_ref, ids_ref, chunk, found, passages, sems):
     groups, plane, _ = packet_ref.shape
-    rows, dim = passages_ref.shape
+    rows, dim = passages.shape
     queries = groups * plane
-    width = 512
-
-    codes = packet_ref[:, :, 2 * dim :].reshape(queries, LANES).astype(F32).astype(jnp.int32)
+    steps = sems.shape[0]
+    width = rows // steps
+    copy = passage_copies(passages_hbm, passages, sems)
+    for j in range(steps):
+        copy(j).start()
+
+    codes = packet_ref[:, :, dim:].reshape(queries, LANES).astype(F32).astype(jnp.int32)
     for k in range(POS):
         high, mid, low = (codes[:, k + POS * part : k + POS * part + 1] for part in range(3))
         ids = (high << 14) + (mid << 7) + low - shard_ref[0] * rows
@@ -49,10 +70,11 @@
     found[...] = jnp.zeros_like(found)
 
     def product(j):
+        copy(j).wait()
         at = pl.multiple_of(j * width, width)
         emb = packet_ref[:, :, :dim].reshape(queries, dim)
         scores_ref[:, pl.ds(at, width)] = lax.dot_general(
-            emb, passages_ref[pl.ds(at, width), :], (((1,), (1,)), ((), ())), preferred_element_type=F32
+            emb, passages[pl.ds(at, width), :], (((1,), (1,)), ((), ())), preferred_element_type=F32
         )
 
     def extract(j):
@@ -75,7 +97,6 @@
         product(j)
         return carry
 
-    steps = rows // width
     product(0)
     lax.fori_loop(1, steps, step, 0)
     extract(steps - 1)
@@ -85,33 +106,67 @@
     for k in range(POS):
         hit = lane == (ids_ref[k] & (LANES - 1))
         columns.append(jnp.sum(jnp.where(hit, found[k], 0.0), axis=1, keepdims=True))
-    table = columns_to_rows(columns)
+    high, mid, low = (part[:POS] for part in in_three(columns_to_rows(columns)))
+    split = dim - queries
+    low = jnp.concatenate([low[:, :split], low[:, split:]], axis=0)
+    rest = jnp.concatenate([jnp.concatenate([high, mid], axis=0), low], axis=1).astype(BF16)
     for g in range(groups):
-        pos_ref[g] = table
-
-
-def score_call(shard, packet, passages):
+        note_ref[g, :plane, :] = raw_ref[...]
+        note_ref[g, plane:, :] = rest
+
+
+def score_call(shard, packet, raw, passages):
     rows, dim = passages.shape
     groups, plane, _ = packet.shape
     queries = groups * plane
     return pl.pallas_call(
         score_kernel,
-        in_specs=[pl.BlockSpec(memory_space=pltpu.SMEM)] + [pl.BlockSpec(memory_space=pltpu.VMEM)] * 2,
+        in_specs=[
+            pl.BlockSpec(memory_space=pltpu.SMEM),
+            pl.BlockSpec(memory_space=pltpu.VMEM),
+            pl.BlockSpec(memory_space=pltpu.VMEM),
+            pl.BlockSpec(memory_space=pltpu.HBM),
+        ],
         out_shape=[
             jax.ShapeDtypeStruct((queries, rows), F32),
-            jax.ShapeDtypeStruct((groups, 8, queries), F32),
+            jax.ShapeDtypeStruct((groups, plane + 8, dim), BF16),
             jax.ShapeDtypeStruct((POS, queries, LANES), jnp.int32),
         ],
         scratch_shapes=[
             pltpu.VMEM((POS, queries, LANES), jnp.int32),
             pltpu.VMEM((POS, queries, LANES), F32),
-        ],
-        compiler_params=params(),
+            pltpu.VMEM((rows, dim), BF16),
+            pltpu.SemaphoreType.DMA((8,)),
+        ],
+        compiler_params=params(24),
         cost_estimate=pl.CostEstimate(
             flops=4 * queries * rows * dim, bytes_accessed=rows * dim * 2 + queries * rows * 4, transcendentals=0
         ),
         name="score",
-    )(shard, packet, passages)
+    )(shard, packet, raw, passages)
+
+
+def read_kernel(notes_ref, out_ref):
+    n, queries = out_ref.shape[0], out_ref.shape[2]
+    first = notes_ref.shape[1] - 8
+    split = notes_ref.shape[2] - queries
+    table = jnp.zeros((POS, queries), F32)
+    for g in range(notes_ref.shape[0]):
+        rest = notes_ref[g, first:, :].astype(F32)
+        low = jnp.concatenate([rest[:POS, queries:], rest[POS:, queries:]], axis=1)
+        table = table + ((rest[:POS, :queries] + rest[POS:, :queries]) + low)
+    table = jnp.concatenate([table, jnp.zeros((8 - POS, queries), F32)], axis=0)
+    for g in range(n):
+        out_ref[g] = table
+
+
+def read_call(notes, n, queries):
+    return pl.pallas_call(
+        read_kernel,
+        out_shape=jax.ShapeDtypeStruct((n, 8, queries), F32),
+        compiler_params=params(6),
+        name="read",
+    )(notes)
 
 
 def sigmoid_kernel(scale, pos_ref, scores_ref, slopes_ref, sums_ref, pos, sums):
@@ -161,17 +216,24 @@
             pltpu.VMEM((queries, LANES), F32),
             pltpu.VMEM((POS + 1, queries, LANES), F32),
         ],
-        compiler_params=params(),
+        compiler_params=params(24),
         cost_estimate=pl.CostEstimate(
             flops=40 * queries * width, bytes_accessed=queries * width * 8, transcendentals=8 * queries * width
         ),
+        input_output_aliases={1: 0},
         name="sigmoid",
     )(pos, scores)
 
 
-def grad_kernel(sums_ref, slopes_ref, passages_ref, ids_ref, part_ref, total_ref, grads, left_a, left_b, acc):
+def grad_kernel(
+    sums_ref, slopes_ref, passages_hbm, ids_ref, part_ref, total_ref, grads, left_a, left_b, acc, passages, sems
+):
     queries, rows = slopes_ref.shape
     width = left_a.shape[1]
+    steps = sems.shape[0]
+    copy = passage_copies(passages_hbm, passages, sems)
+    for j in range(steps):
+        copy(j).start()
     table = sums_ref[0]
     for g in range(1, sums_ref.shape[0]):
         table = table + sums_ref[g]
@@ -199,10 +261,10 @@
                 left[here, c * LANES : (c + 1) * LANES] = (slopes_ref[here, at] + extra).astype(BF16)
 
     def product(left, j):
-        block = passages_ref[pl.ds(pl.multiple_of(j * width, width), width), :]
+        copy(j).wait()
+        block = passages[pl.ds(pl.multiple_of(j * width, width), width), :]
         return jnp.dot(left[...], block, preferred_element_type=F32)
 
-    steps = rows // width
     build(left_a, 0)
     for j in range(steps):
         now, later = (left_a, left_b) if j % 2 == 0 else (left_b, left_a)
@@ -222,7 +284,12 @@
     queries = slopes.shape[0]
     return pl.pallas_call(
         grad_kernel,
-        in_specs=[pl.BlockSpec(memory_space=pltpu.VMEM)] * 4,
+        in_specs=[
+            pl.BlockSpec(memory_space=pltpu.VMEM),
+            pl.BlockSpec(memory_space=pltpu.VMEM),
+            pl.BlockSpec(memory_space=pltpu.HBM),
+            pl.BlockSpec(memory_space=pltpu.VMEM),
+        ],
         out_shape=[
             jax.ShapeDtypeStruct((groups, queries // groups, dim), BF16),
             jax.ShapeDtypeStruct((8, queries), F32),
@@ -232,8 +299,10 @@
             pltpu.VMEM((queries, block), BF16),
             pltpu.VMEM((queries, block), BF16),
             pltpu.VMEM((queries, dim), F32),
-        ],
-        compiler_params=params(),
+            pltpu.VMEM((rows, dim), BF16),
+            pltpu.SemaphoreType.DMA((rows // block,)),
+        ],
+        compiler_params=params(30),
         cost_estimate=pl.CostEstimate(
             flops=4 * queries * rows * dim, bytes_accessed=rows * dim * 2 + queries * rows * 4, transcendentals=0
         ),
@@ -253,7 +322,7 @@
     return pl.pallas_call(
         fold_kernel,
         out_shape=jax.ShapeDtypeStruct((n,) + parts.shape[1:], parts.dtype),
-        compiler_params=params(),
+        compiler_params=params(6),
         name="fold",
     )(parts)
 
@@ -274,12 +343,12 @@
             jax.ShapeDtypeStruct((n,) + parts.shape[1:], parts.dtype),
             jax.ShapeDtypeStruct(parts.shape[1:], F32),
         ],
-        compiler_params=params(),
+        compiler_params=params(6),
         name="fold_both",
     )(parts)
 
 
-def final_kernel(core_ref, packet_ref, peer_ref, mine_ref, other_ref, out_ref):
+def final_kernel(core_ref, notes_ref, peer_ref, mine_ref, other_ref, out_ref):
     groups, plane, dim = mine_ref.shape
     queries = groups * plane
 
@@ -290,8 +359,8 @@
         out_ref[...] = term(*first)
         out_ref[...] += term(*second)
 
-    own = (packet_ref[:, :, dim : 2 * dim].reshape(queries, dim), mine_ref[...].reshape(queries, dim))
-    peer = (peer_ref[:, :, dim : 2 * dim].reshape(queries, dim), other_ref[...].reshape(queries, dim))
+    own = (notes_ref[:, :plane, :].reshape(queries, dim), mine_ref[...].reshape(queries, dim))
+    peer = (peer_ref[:, :plane, :].reshape(queries, dim), other_ref[...].reshape(queries, dim))
 
     @pl.when(core_ref[0] == 0)
     def _():
@@ -302,15 +371,15 @@
         both(peer, own)
 
 
-def final_call(core, packet, peer, mine, other):
+def final_call(core, notes, peer, mine, other):
     dim = mine.shape[-1]
     return pl.pallas_call(
         final_kernel,
         in_specs=[pl.BlockSpec(memory_space=pltpu.SMEM)] + [pl.BlockSpec(memory_space=pltpu.VMEM)] * 4,
         out_shape=jax.ShapeDtypeStruct((dim, dim), F32),
-        compiler_params=params(),
+        compiler_params=params(20),
         name="final",
-    )(core, packet, peer, mine, other)
+    )(core, notes, peer, mine, other)
 
 
 def exchange(v, axes):
@@ -334,15 +403,18 @@
     projected = jnp.dot(queries_raw, projection, precision=hp, preferred_element_type=F32)
     ids = jnp.concatenate([positives >> 14, (positives >> 7) & 127, positives & 127], axis=1)
     ids = jnp.pad(ids, ((0, 0), (0, LANES - 3 * POS)))
-    packet = jnp.concatenate([projected.astype(BF16), queries_raw.astype(BF16), ids.astype(BF16)], axis=1)
+    packet = jnp.concatenate([projected.astype(BF16), ids.astype(BF16), queries_raw.astype(BF16)], axis=1)
     shard = (lax.axis_index("x") * nz + lax.axis_index("z")) * lax.axis_size("y") + lax.axis_index("y")
     packet, shard = lax.optimization_barrier((packet, shard))
     packet = spread(packet, "z").reshape(plane, 2 * dim + LANES)
+    packet, raw = lax.optimization_barrier((packet[:, : dim + LANES], packet[:, dim + LANES :]))
     packet = spread(packet, XY)
-    peer = lax.ppermute(packet, "c", swap)
-
-    scores, pos, local_pos = score_call(shard.reshape(1), packet, passages)
-    pos = exchange(fold_call(exchange(pos, XY), nz), "z")
+
+    passages = pltpu.with_memory_space_constraint(passages, pltpu.HBM)
+    scores, notes, local_pos = score_call(shard.reshape(1), packet, raw, passages)
+    notes = exchange(notes, XY)
+    peer = lax.ppermute(notes, "c", swap)
+    pos = exchange(read_call(notes, nz, nxy * plane), "z")
     pos, peer = lax.optimization_barrier((pos, peer))
     slopes, sums = sigmoid_call(pos, scores, scale, nxy)
     sums = exchange(fold_call(exchange(sums, XY), nz), "z")
@@ -358,7 +430,7 @@
     grad_raw = jnp.dot(query_grad, projection.T, precision=hp, preferred_element_type=F32)
     first = lax.axis_index(XY) * plane + home
     loss = lax.dynamic_slice_in_dim(sums[POS], first, own, 0)
-    grad_projection = final_call(core.reshape(1), packet, peer, mine, other)
+    grad_projection = final_call(core.reshape(1), notes, peer, mine, other)
     return (loss, grad_raw, grad_projection)
 
 

time: 190 us -> 189 us (level)
  Pallas kernels: 30.1 us -> 42.9 us
  local copies, waits for them, and re-layouts: 12.4 us -> 1.8 us
  starting transfers between devices: 13.3 us -> 11.4 us
    unnamed x24 -> x6, local copies, waits for them, and re-layouts: 11.6 us -> 1.07 us
    pallas_call x1, Pallas kernels: 12.1 us -> 21.3 us  [sigmoid_call(): pl.pallas_call(functools.partial(sigmoid_kernel, scale), in_specs=[pl.Blo...]
    ppermute x1, starting transfers between devices: 9.54 us -> 6.6 us  [shards(): other = lax.ppermute(mine, 'c', swap)]
    pallas_call x1, Pallas kernels: 6.5 us -> 8.95 us  [score_call(): pl.pallas_call(score_kernel, in_specs=[pl.BlockSpec(memory_space=pltpu.SM...]
  transfers between devices with their start and end apart: 2 -> 2, of which waited for: 0 -> 0; matrix products, arithmetic and copies ran while one was open for 2% -> 2% of each run, Pallas kernels for 3% -> 0%
where the time goes in v4:
time: 189 us; the launch traced here: 188 us
  blocking collectives  125 us (66%)
  Pallas kernels  42.9 us (23%)
  starting transfers between devices  11.4 us (6%)
  matrix products  4.53 us (2%)
    all_to_all x9, blocking collectives, exchange(): return lax.all_to_all(v, axes, 0, 0, tiled=False)  125 us
    pallas_call x1, Pallas kernels, sigmoid_call(): pl.pallas_call(functools.partial(sigmoid_kernel, scale), in_specs=[pl.Blo...  21.3 us
    pallas_call x1, Pallas kernels, score_call(): pl.pallas_call(score_kernel, in_specs=[pl.BlockSpec(memory_space=pltpu.SM...  8.95 us
    pallas_call x1, Pallas kernels, grad_call(): pl.pallas_call(grad_kernel, in_specs=[pl.BlockSpec(memory_space=pltpu.VME...  7.96 us
    ppermute x1, starting transfers between devices, shards(): other = lax.ppermute(mine, 'c', swap)  6.6 us
    ppermute x1, starting transfers between devices, shards(): peer = lax.ppermute(notes, 'c', swap)  4.81 us
    pallas_call x1, Pallas kernels, final_call(): pl.pallas_call(final_kernel, in_specs=[pl.BlockSpec(memory_space=pltpu.SM...  4.39 us
  transfers between devices with their start and end apart: 2, of which 0 were waited for; matrix products, arithmetic and copies ran while one was open for 2% of the time, Pallas kernels for 0%

profile of v4, /device:TPU:1, one launch (start us, length us, event | category | flops | bytes accessed | tf_op | source)
XLA Modules:
  0.0 188.3 jit_solution(14534606312008049286)
XLA Ops:
  0.6 0.0 copy-start
  0.7 0.8 shift-right-arithmetic_convert_fusion
  1.5 0.7 convert_element_type.8
  2.2 0.1 copy-done
  2.3 1.9 %convolution_convert_fusion = bf16[4,768]{1,0:T(4,128)(2,1)S(1)} fusion(f32[4,768]{1,0:T(4,128)} %param.4, f32[768,768]{1,0:T(8,128)S(1)} %copy-done), kind=kOutput, calls=%fused_computation | convolution fusion | flops 28314624 | bytes 2377728 | tf_op jit(solution)/shard_map/dot_general | solution.py:403
  4.2 0.1 fusion.6
  4.4 16.4 %all_to_all.45 = bf16[8,4,1664]{2,1,0:T(4,128)(2,1)S(1)} all-to-all(bf16[8,4,1664]{2,1,0:T(4,128)(2,1)S(1)} %broadcast_in_dim.4), channel_id=1, replica_groups=mesh['x'=4,'z'=8,'y'=4,'c'=2] {'z'}, dimensions={0} | all-to-all | bytes 212992 | tf_op jit(solution)/shard_map/all_to_all | solution.py:386
  20.8 0.1 broadcast_in_dim.5
  20.9 19.2 %all_to_all.46.packet_ref = bf16[16,32,896]{2,1,0:T(8,128)(2,1)S(1)} all-to-all(bf16[16,32,896]{2,1,0:T(8,128)(2,1)S(1)} %broadcast_in_dim.5), channel_id=1, replica_groups=mesh['x'=4,'z'=8,'y'=4,'c'=2] {'x','y'}, dimensions={0} | all-to-all | bytes 1835008 | tf_op jit(solution)/shard_map/all_to_all | solution.py:386
  40.0 9.0 %score.1 = (f32[512,4096]{1,0:T(8,128)S(1)}, bf16[16,40,768]{2,1,0:T(8,128)(2,1)S(1)}, s32[4,512,128]{2,1,0:T(8,128)S(1)}) custom-call(s32[1]{0:T(128)} %bitcast.shard_ref, bf16[16,32,896]{2,1,0:T(8,128)(2,1)S(1)} %all_to_all.46.packet_ref, bf16[32,768]{1,0:T(8,128)(2,1)S(1)} %slice.13.raw_ref, bf16[4096,768]{1,0:T(8,128)(2,1)} %passages_hbm.3), custom_call_target="tpu_custom_call" | custom-call | flops 6442450944 | bytes 14680064 | tf_op jit(solution)/shard_map/score/pallas_call | solution.py:122
  49.0 16.1 %all_to_all.47.notes_ref = bf16[16,40,768]{2,1,0:T(8,128)(2,1)S(1)} all-to-all(bf16[16,40,768]{2,1,0:T(8,128)(2,1)S(1)} %get-tuple-element.22), channel_id=1, replica_groups=mesh['x'=4,'z'=8,'y'=4,'c'=2] {'x','y'}, dimensions={0} | all-to-all | bytes 1966080 | tf_op jit(solution)/shard_map/all_to_all | solution.py:386
  65.1 4.8 %collective-permute-start = (bf16[16,40,768]{2,1,0:T(8,128)(2,1)S(1)}, bf16[16,40,768]{2,1,0:T(8,128)(2,1)S(1)}, u32[]{:S(2)}, u32[]{:S(2)}) collective-permute-start(bf16[16,40,768]{2,1,0:T(8,128)(2,1)S(1)} %all_to_all.47.notes_ref), channel_id=1, source_target_pairs={{0,1},{1,0},{2,3},{3,2},{4,5},{5,4},{6,7},{7,6},{8,9},{9,8},{10,11... | collective-permute-start | bytes 2949128 | tf_op jit(solution)/shard_map/ppermute | solution.py:416
  69.9 0.1 read.1
  70.0 11.9 %all_to_all.48.pos_ref = f32[8,8,512]{2,1,0:T(8,128)S(1)} all-to-all(f32[8,8,512]{2,1,0:T(8,128)S(1)} %read.1), channel_id=1, replica_groups=mesh['x'=4,'z'=8,'y'=4,'c'=2] {'z'}, dimensions={0} | all-to-all | bytes 262144 | tf_op jit(solution)/shard_map/all_to_all | solution.py:386
  81.9 0.0 collective-permute-done.peer_ref
  81.9 0.0 copy-start.1
  81.9 0.9 copy-done.1
  82.8 21.3 %sigmoid.1 = (f32[512,4096]{1,0:T(8,128)S(1)}, f32[16,8,512]{2,1,0:T(8,128)S(1)}) custom-call(f32[8,8,512]{2,1,0:T(8,128)S(1)} %all_to_all.48.pos_ref, f32[512,4096]{1,0:T(8,128)S(1)} %get-tuple-element.24.scores_ref), custom_call_target="tpu_custom_call", output_to_operand_aliasing={{0}: (1, {})} | custom-call | flops 83886080 | bytes 16777216 | tf_op jit(solution)/shard_map/sigmoid/pallas_call | solution.py:208
  104.1 10.5 %all_to_all.49.parts_ref = f32[16,8,512]{2,1,0:T(8,128)S(1)} all-to-all(f32[16,8,512]{2,1,0:T(8,128)S(1)} %get-tuple-element.25), channel_id=1, replica_groups=mesh['x'=4,'z'=8,'y'=4,'c'=2] {'x','y'}, dimensions={0} | all-to-all | bytes 524288 | tf_op jit(solution)/shard_map/all_to_all | solution.py:386
  114.6 10.3 %all_to_all.50.sums_ref = f32[8,8,512]{2,1,0:T(8,128)S(1)} all-to-all(f32[8,8,512]{2,1,0:T(8,128)S(1)} %fold.2), channel_id=1, replica_groups=mesh['x'=4,'z'=8,'y'=4,'c'=2] {'z'}, dimensions={0} | all-to-all | bytes 262144 | tf_op jit(solution)/shard_map/all_to_all | solution.py:386
  124.9 8.0 %grad.1 = (bf16[16,32,768]{2,1,0:T(8,128)(2,1)S(1)}, f32[8,512]{1,0:T(8,128)S(1)}) custom-call(f32[8,8,512]{2,1,0:T(8,128)S(1)} %all_to_all.50.sums_ref, f32[512,4096]{1,0:T(8,128)S(1)} %get-tuple-element.26.slopes_ref, bf16[4096,768]{1,0:T(8,128)(2,1)} %passages_hbm.3, s32[4,512,128]{2,1,0:T(8,128)S(1)} %get-tuple-element.27.ids_ref), custom_call_target="tpu_custom_call" | custom-call | flops 6442450944 | bytes 14680064 | tf_op jit(solution)/shard_map/grad/pallas_call | solution.py:285
  132.9 14.0 %all_to_all.51.parts_ref = bf16[16,32,768]{2,1,0:T(8,128)(2,1)S(1)} all-to-all(bf16[16,32,768]{2,1,0:T(8,128)(2,1)S(1)} %get-tuple-element.29), channel_id=1, replica_groups=mesh['x'=4,'z'=8,'y'=4,'c'=2] {'x','y'}, dimensions={0} | all-to-all | bytes 1572864 | tf_op jit(solution)/shard_map/all_to_all | solution.py:386
  146.9 0.1 fold.3
  147.0 13.3 %all_to_all.52.parts_ref = bf16[8,32,768]{2,1,0:T(8,128)(2,1)S(1)} all-to-all(bf16[8,32,768]{2,1,0:T(8,128)(2,1)S(1)} %fold.3), channel_id=1, replica_groups=mesh['x'=4,'z'=8,'y'=4,'c'=2] {'z'}, dimensions={0} | all-to-all | bytes 786432 | tf_op jit(solution)/shard_map/all_to_all | solution.py:386
  160.2 0.1 fold_both.1
  160.3 13.8 %all_to_all.53.mine_ref = bf16[16,32,768]{2,1,0:T(8,128)(2,1)} all-to-all(bf16[16,32,768]{2,1,0:T(8,128)(2,1)S(1)} %get-tuple-element.32), channel_id=1, replica_groups=mesh['x'=4,'z'=8,'y'=4,'c'=2] {'x','y'}, dimensions={0} | all-to-all | bytes 1572864 | tf_op jit(solution)/shard_map/all_to_all | solution.py:386
  174.1 6.6 %collective-permute-start.1 = (bf16[16,32,768]{2,1,0:T(8,128)(2,1)}, bf16[16,32,768]{2,1,0:T(8,128)(2,1)}, u32[]{:S(2)}, u32[]{:S(2)}) collective-permute-start(bf16[16,32,768]{2,1,0:T(8,128)(2,1)} %all_to_all.53.mine_ref), channel_id=1, source_target_pairs={{0,1},{1,0},{2,3},{3,2},{4,5},{5,4},{6,7},{7,6},{8,9},{9,8},{10,11... | collective-permute-start | bytes 2359304 | tf_op jit(solution)/shard_map/ppermute | solution.py:426
  180.7 0.0 copy-start.2
  180.7 0.6 dynamic-slice_bitcast_fusion
  181.3 2.6 %fusion = f32[4,768]{1,0:T(4,128)} fusion(f32[768,768]{1,0:T(8,128)S(1)} %copy-done, f32[32,768]{1,0:T(8,128)S(1)} %get-tuple-element.30, s32[]{:T(128)S(6)} %select_n.7), kind=kOutput, calls=%fused_computation.2 | convolution fusion | flops 28311552 | bytes 2383876 | tf_op jit(solution)/shard_map/dot_general | solution.py:430
  183.9 0.0 collective-permute-done.1.other_ref
  183.9 0.0 copy-done.2
  183.9 4.4 %final.1 = f32[768,768]{1,0:T(8,128)} custom-call(s32[1]{0:T(128)} %bitcast.2.core_ref, bf16[16,40,768]{2,1,0:T(8,128)(2,1)S(1)} %all_to_all.47.notes_ref, bf16[16,40,768]{2,1,0:T(8,128)(2,1)S(1)} %copy-done.2, bf16[16,32,768]{2,1,0:T(8,128)(2,1)} %all_to_all.53.mine_ref, bf16[16,32,768]{2,1,0:T(8,128)(2,1)} %collective-permute-done.1.other_ref), custom_call_target="tpu_custom_call" | custom-call | tf_op jit(solution)/shard_map/final/pallas_call | solution.py:376
  (7 shorter events, 0.1 us)
Async XLA Ops:
  0.6 1.7 copy-start
  65.1 16.7 %collective-permute-start = (bf16[16,40,768]{2,1,0:T(8,128)(2,1)S(1)}, bf16[16,40,768]{2,1,0:T(8,128)(2,1)S(1)}, u32[]{:S(2)}, u32[]{:S(2)}) collective-permute-start(bf16[16,40,768]{2,1,0:T(8,128)(2,1)S(1)} %all_to_all.47.notes_ref), channel_id=1, source_target_pairs={{0,1},{1,0},{2,3},{3,2},{4,5},{5,4},{6,7},{7,6},{8,9},{9,8},{10,11... | collective-permute-start | bytes 2949128 | tf_op jit(solution)/shard_map/ppermute | solution.py:416
  81.9 0.9 copy-start.1
  174.1 9.8 %collective-permute-start.1 = (bf16[16,32,768]{2,1,0:T(8,128)(2,1)}, bf16[16,32,768]{2,1,0:T(8,128)(2,1)}, u32[]{:S(2)}, u32[]{:S(2)}) collective-permute-start(bf16[16,32,768]{2,1,0:T(8,128)(2,1)} %all_to_all.53.mine_ref), channel_id=1, source_target_pairs={{0,1},{1,0},{2,3},{3,2},{4,5},{5,4},{6,7},{7,6},{8,9},{9,8},{10,11... | collective-permute-start | bytes 2359304 | tf_op jit(solution)/shard_map/ppermute | solution.py:426
  180.7 3.2 %copy-start.2 = (bf16[16,40,768]{2,1,0:T(8,128)(2,1)S(1)}, bf16[16,40,768]{2,1,0:T(8,128)(2,1)}, u32[]{:S(2)}) copy-start(bf16[16,40,768]{2,1,0:T(8,128)(2,1)} %copy-done.1) | copy-start | bytes 2949124

commit v5 on v4

--- a/solution.py
+++ b/solution.py
@@ -57,8 +57,7 @@
     steps = sems.shape[0]
     width = rows // steps
     copy = passage_copies(passages_hbm, passages, sems)
-    for j in range(steps):
-        copy(j).start()
+    copy(0).start()
 
     codes = packet_ref[:, :, dim:].reshape(queries, LANES).astype(F32).astype(jnp.int32)
     for k in range(POS):
@@ -67,10 +66,11 @@
         ids = jnp.broadcast_to(ids, (queries, LANES))
         ids_ref[k] = ids
         chunk[k] = ids >> 7
+    for j in range(1, 4):
+        copy(j).start()
     found[...] = jnp.zeros_like(found)
 
     def product(j):
-        copy(j).wait()
         at = pl.multiple_of(j * width, width)
         emb = packet_ref[:, :, :dim].reshape(queries, dim)
         scores_ref[:, pl.ds(at, width)] = lax.dot_general(
@@ -93,10 +93,16 @@
                 found[k, here, :] = best
 
     def step(j, carry):
+        @pl.when(j + 3 < steps)
+        def _():
+            copy(j + 3).start()
+
+        copy(j).wait()
         extract(j - 1)
         product(j)
         return carry
 
+    copy(0).wait()
     product(0)
     lax.fori_loop(1, steps, step, 0)
     extract(steps - 1)
@@ -177,30 +183,81 @@
         rows = rows + pos_ref[g]
     pos[...] = rows_to_columns(rows)
 
-    def tile(t, carry):
+    def place(t):
         at = pl.ds(pl.multiple_of(t * size, size), size)
         columns = pos[at, :]
-        p = [jnp.broadcast_to(columns[:, k : k + 1], (size, LANES)) for k in range(POS)]
-        slope_acc = [jnp.zeros((size, LANES), F32) for _ in range(POS)]
-        loss_acc = jnp.zeros((size, LANES), F32)
+        return at, [jnp.broadcast_to(columns[:, k : k + 1], (size, LANES)) for k in range(POS)]
+
+    def tile(t, carry):
+        at, p = place(t)
+        p = [0.5 * q for q in p]
+        square_acc = [jnp.zeros((size, LANES), F32) for _ in range(POS)]
+        tanh_acc = jnp.zeros((size, LANES), F32)
         for c in range(width // LANES):
-            s = scores_ref[at, c * LANES : (c + 1) * LANES]
-            sigs = [jax.nn.sigmoid(s - p[k]) for k in range(POS)]
-            slopes = [sig * (1.0 - sig) for sig in sigs]
-            loss_acc = loss_acc + ((sigs[0] + sigs[1]) + (sigs[2] + sigs[3]))
-            slope_acc = [slope_acc[k] + slopes[k] for k in range(POS)]
-            both = (slopes[0] + slopes[1]) + (slopes[2] + slopes[3])
-            slopes_ref[at, c * LANES : (c + 1) * LANES] = both * scale
+            s = 0.5 * scores_ref[at, c * LANES : (c + 1) * LANES]
+            tanhs = [jnp.tanh(s - p[k]) for k in range(POS)]
+            squares = [th * th for th in tanhs]
+            tanh_acc = tanh_acc + ((tanhs[0] + tanhs[1]) + (tanhs[2] + tanhs[3]))
+            square_acc = [square_acc[k] + squares[k] for k in range(POS)]
+            both = (squares[0] + squares[1]) + (squares[2] + squares[3])
+            slopes_ref[at, c * LANES : (c + 1) * LANES] = float(POS) - both
+        chunks = float(width // LANES)
         for k in range(POS):
-            sums[k, at, :] = slope_acc[k]
-        sums[POS, at, :] = loss_acc
+            sums[k, at, :] = 0.25 * (chunks - square_acc[k])
+        sums[POS, at, :] = 0.5 * (POS * chunks + tanh_acc)
         return carry
 
-    lax.fori_loop(0, queries // size, tile, 0)
-    columns = [jnp.sum(sums[k], axis=1, keepdims=True) * (scale if k == POS else -scale) for k in range(POS + 1)]
-    rows = columns_to_rows(columns)
-    for g in range(sums_ref.shape[0]):
-        sums_ref[g] = rows
+    lax.fori_loop(0, queries // size, tile, 0, unroll=2)
+
+    def again(t):
+        at, p = place(t)
+        zero = jnp.zeros((size, LANES), F32)
+
+        def chunk(c, acc):
+            here = pl.ds(pl.multiple_of(c * LANES, LANES), LANES)
+            s = scores_ref[at, here]
+            acc, both = list(acc), zero
+            for k in range(POS):
+                x = s - p[k]
+                e = jnp.exp(-jnp.abs(x))
+                r = 1.0 / (1.0 + e)
+                slope = e * r * r
+                acc[k] = acc[k] + slope
+                acc[POS] = acc[POS] + jnp.where(x < 0.0, e * r, r)
+                both = both + slope
+            slopes_ref[at, here] = 4.0 * both
+            return tuple(acc)
+
+        acc = lax.fori_loop(0, width // LANES, chunk, (zero,) * (POS + 1))
+        for k in range(POS + 1):
+            sums[k, at, :] = acc[k]
+
+    def totals(at):
+        return [jnp.sum(sums[k, at, :], axis=1, keepdims=True) for k in range(POS + 1)]
+
+    def least(columns):
+        return jnp.min((columns[0] + columns[1]) + (columns[2] + columns[3]))
+
+    def finish(columns):
+        rows = columns_to_rows([c * (scale if k == POS else -scale) for k, c in enumerate(columns)])
+        for g in range(sums_ref.shape[0]):
+            sums_ref[g] = rows
+
+    columns = totals(slice(None))
+    finish(columns)
+    enough = width / 1024.0
+
+    @pl.when(least(columns) < enough)
+    def _():
+        def check(t, carry):
+            @pl.when(least(totals(place(t)[0])) < enough)
+            def _():
+                again(t)
+
+            return carry
+
+        lax.fori_loop(0, queries // size, check, 0)
+        finish(totals(slice(None)))
 
 
 def sigmoid_call(pos, scores, scale, groups):
@@ -220,25 +277,24 @@
         cost_estimate=pl.CostEstimate(
             flops=40 * queries * width, bytes_accessed=queries * width * 8, transcendentals=8 * queries * width
         ),
-        input_output_aliases={1: 0},
         name="sigmoid",
     )(pos, scores)
 
 
 def grad_kernel(
-    sums_ref, slopes_ref, passages_hbm, ids_ref, part_ref, total_ref, grads, left_a, left_b, acc, passages, sems
+    scale, sums_ref, slopes_ref, passages_hbm, ids_ref, part_ref, total_ref, grads, left_a, left_b, acc, passages, sems
 ):
     queries, rows = slopes_ref.shape
     width = left_a.shape[1]
     steps = sems.shape[0]
     copy = passage_copies(passages_hbm, passages, sems)
-    for j in range(steps):
-        copy(j).start()
+    copy(0).start()
+    copy(1).start()
     table = sums_ref[0]
     for g in range(1, sums_ref.shape[0]):
         table = table + sums_ref[g]
     total_ref[...] = table
-    columns = rows_to_columns(table)
+    columns = rows_to_columns(table) * (4.0 / scale)
     for k in range(POS):
         give = columns[:, k : k + 1]
         for other in range(POS):
@@ -268,6 +324,8 @@
     build(left_a, 0)
     for j in range(steps):
         now, later = (left_a, left_b) if j % 2 == 0 else (left_b, left_a)
+        if j + 2 < steps:
+            copy(j + 2).start()
         if j + 1 < steps:
             build(later, j + 1)
         term = product(now, j)
@@ -276,14 +334,14 @@
         elif j + 1 < steps:
             acc[...] += term
         else:
-            part_ref[...] = (acc[...] + term).astype(BF16).reshape(part_ref.shape)
-
-
-def grad_call(sums, slopes, passages, ids, groups, block=1024):
+            part_ref[...] = ((acc[...] + term) * (0.25 * scale)).astype(BF16).reshape(part_ref.shape)
+
+
+def grad_call(sums, slopes, passages, ids, scale, groups, block=1024):
     rows, dim = passages.shape
     queries = slopes.shape[0]
     return pl.pallas_call(
-        grad_kernel,
+        functools.partial(grad_kernel, scale),
         in_specs=[
             pl.BlockSpec(memory_space=pltpu.VMEM),
             pl.BlockSpec(memory_space=pltpu.VMEM),
@@ -348,27 +406,32 @@
     )(parts)
 
 
-def final_kernel(core_ref, notes_ref, peer_ref, mine_ref, other_ref, out_ref):
+def final_kernel(core_ref, notes_ref, peer_ref, mine_ref, other_ref, out_hbm, near, sems):
     groups, plane, dim = mine_ref.shape
     queries = groups * plane
+    parts = sems.shape[0]
+    width = dim // parts
+    even = core_ref[0] == 0
+
+    def ordered(own, peer):
+        own, peer = own.reshape(queries, own.shape[-1]), peer.reshape(queries, peer.shape[-1])
+        return jnp.where(even, own, peer), jnp.where(even, peer, own)
 
     def term(raw, grads):
         return lax.dot_general(raw, grads, (((0,), (0,)), ((), ())), preferred_element_type=F32)
 
-    def both(first, second):
-        out_ref[...] = term(*first)
-        out_ref[...] += term(*second)
-
-    own = (notes_ref[:, :plane, :].reshape(queries, dim), mine_ref[...].reshape(queries, dim))
-    peer = (peer_ref[:, :plane, :].reshape(queries, dim), other_ref[...].reshape(queries, dim))
-
-    @pl.when(core_ref[0] == 0)
-    def _():
-        both(own, peer)
-
-    @pl.when(core_ref[0] != 0)
-    def _():
-        both(peer, own)
+    def copy(i):
+        at = pl.ds(i * width, width)
+        return pltpu.make_async_copy(near.at[at, :], out_hbm.at[at, :], sems.at[i])
+
+    grads = ordered(mine_ref[...], other_ref[...])
+    for i in range(parts):
+        at = slice(i * width, (i + 1) * width)
+        raw = ordered(notes_ref[:, :plane, at], peer_ref[:, :plane, at])
+        near[at, :] = term(raw[0], grads[0]) + term(raw[1], grads[1])
+        copy(i).start()
+    for i in range(parts):
+        copy(i).wait()
 
 
 def final_call(core, notes, peer, mine, other):
@@ -376,10 +439,38 @@
     return pl.pallas_call(
         final_kernel,
         in_specs=[pl.BlockSpec(memory_space=pltpu.SMEM)] + [pl.BlockSpec(memory_space=pltpu.VMEM)] * 4,
+        out_specs=pl.BlockSpec(memory_space=pl.ANY),
         out_shape=jax.ShapeDtypeStruct((dim, dim), F32),
+        scratch_shapes=[pltpu.VMEM((dim, dim), F32), pltpu.SemaphoreType.DMA((3,))],
         compiler_params=params(20),
         name="final",
     )(core, notes, peer, mine, other)
+
+
+def head_kernel(raw_ref, projection_ref, positives_ref, out_ref):
+    own, dim = raw_ref.shape
+    raw = raw_ref[...]
+    projected = jnp.dot(raw, projection_ref[...], precision=lax.Precision.HIGHEST, preferred_element_type=F32)
+    lane = lax.broadcasted_iota(jnp.int32, (own, LANES), 1)
+    codes = jnp.zeros((own, LANES), jnp.int32)
+    for k in range(POS):
+        ids = positives_ref[:, k : k + 1]
+        for part, piece in enumerate((ids >> 14, (ids >> 7) & 127, ids & 127)):
+            codes = jnp.where(lane == k + POS * part, piece, codes)
+    for g in range(out_ref.shape[0]):
+        out_ref[g, :, :dim] = projected.astype(BF16)
+        out_ref[g, :, dim : dim + LANES] = codes.astype(F32).astype(BF16)
+        out_ref[g, :, dim + LANES :] = raw.astype(BF16)
+
+
+def head_call(raw, projection, positives, n):
+    own, dim = raw.shape
+    return pl.pallas_call(
+        head_kernel,
+        out_shape=jax.ShapeDtypeStruct((n, own, 2 * dim + LANES), BF16),
+        compiler_params=params(12),
+        name="head",
+    )(raw, projection, positives)
 
 
 def exchange(v, axes):
@@ -400,27 +491,24 @@
     core = lax.axis_index("c")
     swap = [(0, 1), (1, 0)]
 
-    projected = jnp.dot(queries_raw, projection, precision=hp, preferred_element_type=F32)
-    ids = jnp.concatenate([positives >> 14, (positives >> 7) & 127, positives & 127], axis=1)
-    ids = jnp.pad(ids, ((0, 0), (0, LANES - 3 * POS)))
-    packet = jnp.concatenate([projected.astype(BF16), ids.astype(BF16), queries_raw.astype(BF16)], axis=1)
     shard = (lax.axis_index("x") * nz + lax.axis_index("z")) * lax.axis_size("y") + lax.axis_index("y")
-    packet, shard = lax.optimization_barrier((packet, shard))
-    packet = spread(packet, "z").reshape(plane, 2 * dim + LANES)
+    packet, shard = lax.optimization_barrier((head_call(queries_raw, projection, positives, nz), shard))
+    packet = exchange(packet, "z").reshape(plane, 2 * dim + LANES)
     packet, raw = lax.optimization_barrier((packet[:, : dim + LANES], packet[:, dim + LANES :]))
     packet = spread(packet, XY)
 
     passages = pltpu.with_memory_space_constraint(passages, pltpu.HBM)
     scores, notes, local_pos = score_call(shard.reshape(1), packet, raw, passages)
     notes = exchange(notes, XY)
-    peer = lax.ppermute(notes, "c", swap)
     pos = exchange(read_call(notes, nz, nxy * plane), "z")
-    pos, peer = lax.optimization_barrier((pos, peer))
     slopes, sums = sigmoid_call(pos, scores, scale, nxy)
     sums = exchange(fold_call(exchange(sums, XY), nz), "z")
-    part, sums = grad_call(sums, slopes, passages, local_pos, nxy)
-
-    part = exchange(fold_call(exchange(part, XY), nz), "z")
+    part, sums = grad_call(sums, slopes, passages, local_pos, scale, nxy)
+
+    part, notes = lax.optimization_barrier((part, notes))
+    peer = lax.ppermute(notes, "c", swap)
+    part, peer = lax.optimization_barrier((exchange(part, XY), peer))
+    part = exchange(fold_call(part, nz), "z")
     part, summed = fold_both_call(part, nxy)
     mine = exchange(part, XY)
     other = lax.ppermute(mine, "c", swap)

time: 189 us -> 181 us (0.958)
  Pallas kernels: 42.9 us -> 29.9 us
  blocking collectives: 125 us -> 131 us
  local copies, waits for them, and re-layouts: 1.8 us -> 4.7 us
  matrix products: 4.53 us -> 2.62 us
    pallas_call x1, Pallas kernels: 21.3 us -> 9.45 us  [sigmoid_call(): pl.pallas_call(functools.partial(sigmoid_kernel, scale), in_specs=[pl.Blo...]
    all_to_all x9, blocking collectives: 125 us -> 131 us  [exchange(): return lax.all_to_all(v, axes, 0, 0, tiled=False)]
    ppermute x1, starting transfers between devices: 4.81 us -> 8.4 us  [shards(): peer = lax.ppermute(notes, 'c', swap)]
    ppermute x1, starting transfers between devices: 6.6 us -> 3.32 us  [shards(): other = lax.ppermute(mine, 'c', swap)]
    unnamed x6 -> x12, local copies, waits for them, and re-layouts: 1.07 us -> 4 us
    dot_general x1 -> x0, matrix products: 1.91 us -> none  [shards(): jnp.dot(queries_raw, projection, precision=hp, preferred_element_type=F32)]
    pallas_call x1 -> x2, Pallas kernels: 7.96 us -> 9.1 us  [the longest x1 7.96 us: grad_call(): pl.pallas_call(functools.partial(grad_kernel, scale), in_specs=[pl.BlockS...]
where the time goes in v5:
time: 181 us
  blocking collectives  131 us (72%)
  Pallas kernels  29.9 us (17%)
  starting transfers between devices  11.7 us (6%)
  local copies, waits for them, and re-layouts  4.7 us (3%)
  matrix products  2.62 us (1%)
    all_to_all x9, blocking collectives, exchange(): return lax.all_to_all(v, axes, 0, 0, tiled=False)  131 us
    pallas_call x1, Pallas kernels, sigmoid_call(): pl.pallas_call(functools.partial(sigmoid_kernel, scale), in_specs=[pl.Blo...  9.45 us
    ppermute x1, starting transfers between devices, shards(): peer = lax.ppermute(notes, 'c', swap)  8.4 us
    pallas_call x1, Pallas kernels, grad_call(): pl.pallas_call(functools.partial(grad_kernel, scale), in_specs=[pl.BlockS...  7.96 us
    pallas_call x1, Pallas kernels, score_call(): pl.pallas_call(score_kernel, in_specs=[pl.BlockSpec(memory_space=pltpu.SM...  7.39 us
    unnamed x12, local copies, waits for them, and re-layouts  4 us
    pallas_call x1, Pallas kernels, final_call(): pl.pallas_call(final_kernel, in_specs=[pl.BlockSpec(memory_space=pltpu.SM...  3.71 us
  transfers between devices with their start and end apart: 2, of which 0 were waited for; matrix products, arithmetic and copies ran while one was open for 2% of the time, Pallas kernels for 0%

profile of v5, /device:TPU:1, one launch (start us, length us, event | category | flops | bytes accessed | tf_op | source)
XLA Modules:
  0.0 180.7 jit_solution(2425891049787395779)
XLA Ops:
  0.6 0.0 copy-start
  0.7 1.7 copy-done
  2.3 0.0 copy-start.4
  2.3 0.7 copy-done.4
  3.0 0.0 copy-start.5
  3.0 0.7 copy-done.5
  3.7 1.1 head.1
  4.8 16.3 %all_to_all.45 = bf16[8,4,1664]{2,1,0:T(4,128)(2,1)S(1)} all-to-all(bf16[8,4,1664]{2,1,0:T(4,128)(2,1)S(1)} %head.1), channel_id=1, replica_groups=mesh['x'=4,'z'=8,'y'=4,'c'=2] {'z'}, dimensions={0} | all-to-all | bytes 212992 | tf_op jit(solution)/shard_map/all_to_all | solution.py:477
  21.3 0.1 broadcast_in_dim.2
  21.3 19.2 %all_to_all.46.packet_ref = bf16[16,32,896]{2,1,0:T(8,128)(2,1)S(1)} all-to-all(bf16[16,32,896]{2,1,0:T(8,128)(2,1)S(1)} %broadcast_in_dim.2), channel_id=1, replica_groups=mesh['x'=4,'z'=8,'y'=4,'c'=2] {'x','y'}, dimensions={0} | all-to-all | bytes 1835008 | tf_op jit(solution)/shard_map/all_to_all | solution.py:477
  40.5 7.4 %score.1 = (f32[512,4096]{1,0:T(8,128)S(1)}, bf16[16,40,768]{2,1,0:T(8,128)(2,1)S(1)}, s32[4,512,128]{2,1,0:T(8,128)S(1)}) custom-call(s32[1]{0:T(128)} %bitcast.shard_ref, bf16[16,32,896]{2,1,0:T(8,128)(2,1)S(1)} %all_to_all.46.packet_ref, bf16[32,768]{1,0:T(8,128)(2,1)S(1)} %slice.13.raw_ref, bf16[4096,768]{1,0:T(8,128)(2,1)} %passages_hbm.3), custom_call_target="tpu_custom_call" | custom-call | flops 6442450944 | bytes 14680064 | tf_op jit(solution)/shard_map/score/pallas_call | solution.py:128
  47.9 16.1 %all_to_all.47.notes_ref = bf16[16,40,768]{2,1,0:T(8,128)(2,1)S(1)} all-to-all(bf16[16,40,768]{2,1,0:T(8,128)(2,1)S(1)} %get-tuple-element.24), channel_id=1, replica_groups=mesh['x'=4,'z'=8,'y'=4,'c'=2] {'x','y'}, dimensions={0} | all-to-all | bytes 1966080 | tf_op jit(solution)/shard_map/all_to_all | solution.py:477
  64.0 0.1 read.1
  64.1 10.3 %all_to_all.48.pos_ref = f32[8,8,512]{2,1,0:T(8,128)S(1)} all-to-all(f32[8,8,512]{2,1,0:T(8,128)S(1)} %read.1), channel_id=1, replica_groups=mesh['x'=4,'z'=8,'y'=4,'c'=2] {'z'}, dimensions={0} | all-to-all | bytes 262144 | tf_op jit(solution)/shard_map/all_to_all | solution.py:477
  74.4 9.4 %sigmoid.1 = (f32[512,4096]{1,0:T(8,128)S(1)}, f32[16,8,512]{2,1,0:T(8,128)S(1)}) custom-call(f32[8,8,512]{2,1,0:T(8,128)S(1)} %all_to_all.48.pos_ref, f32[512,4096]{1,0:T(8,128)S(1)} %get-tuple-element.25.scores_ref), custom_call_target="tpu_custom_call" | custom-call | flops 83886080 | bytes 16777216 | tf_op jit(solution)/shard_map/sigmoid/pallas_call | solution.py:265
  83.8 10.6 %all_to_all.49.parts_ref = f32[16,8,512]{2,1,0:T(8,128)S(1)} all-to-all(f32[16,8,512]{2,1,0:T(8,128)S(1)} %get-tuple-element.26), channel_id=1, replica_groups=mesh['x'=4,'z'=8,'y'=4,'c'=2] {'x','y'}, dimensions={0} | all-to-all | bytes 524288 | tf_op jit(solution)/shard_map/all_to_all | solution.py:477
  94.5 10.3 %all_to_all.50.sums_ref = f32[8,8,512]{2,1,0:T(8,128)S(1)} all-to-all(f32[8,8,512]{2,1,0:T(8,128)S(1)} %fold.2), channel_id=1, replica_groups=mesh['x'=4,'z'=8,'y'=4,'c'=2] {'z'}, dimensions={0} | all-to-all | bytes 262144 | tf_op jit(solution)/shard_map/all_to_all | solution.py:477
  104.8 8.0 %grad.1 = (bf16[16,32,768]{2,1,0:T(8,128)(2,1)S(1)}, f32[8,512]{1,0:T(8,128)S(1)}) custom-call(f32[8,8,512]{2,1,0:T(8,128)S(1)} %all_to_all.50.sums_ref, f32[512,4096]{1,0:T(8,128)S(1)} %get-tuple-element.27.slopes_ref, bf16[4096,768]{1,0:T(8,128)(2,1)} %passages_hbm.3, s32[4,512,128]{2,1,0:T(8,128)S(1)} %get-tuple-element.28.ids_ref), custom_call_target="tpu_custom_call" | custom-call | flops 6442450944 | bytes 14680064 | tf_op jit(solution)/shard_map/grad/pallas_call | solution.py:343
  112.7 8.4 %collective-permute-start = (bf16[16,40,768]{2,1,0:T(8,128)(2,1)S(1)}, bf16[16,40,768]{2,1,0:T(8,128)(2,1)S(1)}, u32[]{:S(2)}, u32[]{:S(2)}) collective-permute-start(bf16[16,40,768]{2,1,0:T(8,128)(2,1)S(1)} %all_to_all.47.notes_ref), channel_id=1, source_target_pairs={{0,1},{1,0},{2,3},{3,2},{4,5},{5,4},{6,7},{7,6},{8,9},{9,8},{10,11... | collective-permute-start | bytes 2949128 | tf_op jit(solution)/shard_map/ppermute | solution.py:509
  121.1 16.6 %all_to_all.51.parts_ref = bf16[16,32,768]{2,1,0:T(8,128)(2,1)S(1)} all-to-all(bf16[16,32,768]{2,1,0:T(8,128)(2,1)S(1)} %get-tuple-element.31), channel_id=1, replica_groups=mesh['x'=4,'z'=8,'y'=4,'c'=2] {'x','y'}, dimensions={0} | all-to-all | bytes 1572864 | tf_op jit(solution)/shard_map/all_to_all | solution.py:477
  137.7 0.0 copy-start.1
  137.7 0.0 collective-permute-done.peer_ref
  137.7 0.0 copy-start.2
  137.7 0.9 copy-done.2
  138.7 0.1 fold.3
  138.8 15.0 %all_to_all.52.parts_ref = bf16[8,32,768]{2,1,0:T(8,128)(2,1)S(1)} all-to-all(bf16[8,32,768]{2,1,0:T(8,128)(2,1)S(1)} %fold.3), channel_id=1, replica_groups=mesh['x'=4,'z'=8,'y'=4,'c'=2] {'z'}, dimensions={0} | all-to-all | bytes 786432 | tf_op jit(solution)/shard_map/all_to_all | solution.py:477
  153.8 0.1 fold_both.1
  153.9 16.4 %all_to_all.53.mine_ref = bf16[16,32,768]{2,1,0:T(8,128)(2,1)} all-to-all(bf16[16,32,768]{2,1,0:T(8,128)(2,1)S(1)} %get-tuple-element.36), channel_id=1, replica_groups=mesh['x'=4,'z'=8,'y'=4,'c'=2] {'x','y'}, dimensions={0} | all-to-all | bytes 1572864 | tf_op jit(solution)/shard_map/all_to_all | solution.py:477
  170.2 3.3 %collective-permute-start.1 = (bf16[16,32,768]{2,1,0:T(8,128)(2,1)}, bf16[16,32,768]{2,1,0:T(8,128)(2,1)}, u32[]{:S(2)}, u32[]{:S(2)}) collective-permute-start(bf16[16,32,768]{2,1,0:T(8,128)(2,1)} %all_to_all.53.mine_ref), channel_id=1, source_target_pairs={{0,1},{1,0},{2,3},{3,2},{4,5},{5,4},{6,7},{7,6},{8,9},{9,8},{10,11... | collective-permute-start | bytes 2359304 | tf_op jit(solution)/shard_map/ppermute | solution.py:514
  173.6 0.0 copy-start.3
  173.6 0.6 dynamic-slice_bitcast_fusion
  174.2 0.0 copy-done.1
  174.2 2.6 %fusion = f32[4,768]{1,0:T(4,128)} fusion(f32[768,768]{1,0:T(8,128)S(1)} %copy-done.1, f32[32,768]{1,0:T(8,128)S(1)} %get-tuple-element.34, s32[]{:T(128)S(6)} %select_n.7), kind=kOutput, calls=%fused_computation | convolution fusion | flops 28311552 | bytes 2383876 | tf_op jit(solution)/shard_map/dot_general | solution.py:518
  176.8 0.0 collective-permute-done.1.other_ref
  176.8 0.0 copy-done.3
  176.8 3.7 %final.1 = f32[768,768]{1,0:T(8,128)} custom-call(s32[1]{0:T(128)} %bitcast.2.core_ref, bf16[16,40,768]{2,1,0:T(8,128)(2,1)S(1)} %all_to_all.47.notes_ref, bf16[16,40,768]{2,1,0:T(8,128)(2,1)S(1)} %copy-done.3, bf16[16,32,768]{2,1,0:T(8,128)(2,1)} %all_to_all.53.mine_ref, bf16[16,32,768]{2,1,0:T(8,128)(2,1)} %collective-permute-done.1.other_ref), custom_call_target="tpu_custom_call" | custom-call | tf_op jit(solution)/shard_map/final/pallas_call | solution.py:439
  (5 shorter events, 0.1 us)
Async XLA Ops:
  0.6 1.7 copy-start
  2.3 0.7 copy-start.4
  3.0 0.7 copy-start.5
  112.7 25.0 %collective-permute-start = (bf16[16,40,768]{2,1,0:T(8,128)(2,1)S(1)}, bf16[16,40,768]{2,1,0:T(8,128)(2,1)S(1)}, u32[]{:S(2)}, u32[]{:S(2)}) collective-permute-start(bf16[16,40,768]{2,1,0:T(8,128)(2,1)S(1)} %all_to_all.47.notes_ref), channel_id=1, source_target_pairs={{0,1},{1,0},{2,3},{3,2},{4,5},{5,4},{6,7},{7,6},{8,9},{9,8},{10,11... | collective-permute-start | bytes 2949128 | tf_op jit(solution)/shard_map/ppermute | solution.py:509
  137.7 36.4 %copy-start.1 = (f32[768,768]{1,0:T(8,128)S(1)}, f32[768,768]{1,0:T(8,128)}, u32[]{:S(2)}) copy-start(f32[768,768]{1,0:T(8,128)} %projection_ref.1) | copy-start | bytes 7077892
  137.7 0.9 copy-start.2
  170.2 6.5 %collective-permute-start.1 = (bf16[16,32,768]{2,1,0:T(8,128)(2,1)}, bf16[16,32,768]{2,1,0:T(8,128)(2,1)}, u32[]{:S(2)}, u32[]{:S(2)}) collective-permute-start(bf16[16,32,768]{2,1,0:T(8,128)(2,1)} %all_to_all.53.mine_ref), channel_id=1, source_target_pairs={{0,1},{1,0},{2,3},{3,2},{4,5},{5,4},{6,7},{7,6},{8,9},{9,8},{10,11... | collective-permute-start | bytes 2359304 | tf_op jit(solution)/shard_map/ppermute | solution.py:514
  173.6 3.2 %copy-start.3 = (bf16[16,40,768]{2,1,0:T(8,128)(2,1)S(1)}, bf16[16,40,768]{2,1,0:T(8,128)(2,1)}, u32[]{:S(2)}) copy-start(bf16[16,40,768]{2,1,0:T(8,128)(2,1)} %copy-done.2) | copy-start | bytes 2949124

commit v6 on v5

--- a/solution.py
+++ b/solution.py
@@ -282,14 +282,11 @@
 
 
 def grad_kernel(
-    scale, sums_ref, slopes_ref, passages_hbm, ids_ref, part_ref, total_ref, grads, left_a, left_b, acc, passages, sems
+    scale, sums_ref, slopes_ref, passages_ref, ids_ref, part_ref, total_ref, grads, left_a, left_b, acc
 ):
     queries, rows = slopes_ref.shape
     width = left_a.shape[1]
-    steps = sems.shape[0]
-    copy = passage_copies(passages_hbm, passages, sems)
-    copy(0).start()
-    copy(1).start()
+    steps = rows // width
     table = sums_ref[0]
     for g in range(1, sums_ref.shape[0]):
         table = table + sums_ref[g]
@@ -317,15 +314,12 @@
                 left[here, c * LANES : (c + 1) * LANES] = (slopes_ref[here, at] + extra).astype(BF16)
 
     def product(left, j):
-        copy(j).wait()
-        block = passages[pl.ds(pl.multiple_of(j * width, width), width), :]
+        block = passages_ref[pl.ds(pl.multiple_of(j * width, width), width), :]
         return jnp.dot(left[...], block, preferred_element_type=F32)
 
     build(left_a, 0)
     for j in range(steps):
         now, later = (left_a, left_b) if j % 2 == 0 else (left_b, left_a)
-        if j + 2 < steps:
-            copy(j + 2).start()
         if j + 1 < steps:
             build(later, j + 1)
         term = product(now, j)
@@ -345,7 +339,7 @@
         in_specs=[
             pl.BlockSpec(memory_space=pltpu.VMEM),
             pl.BlockSpec(memory_space=pltpu.VMEM),
-            pl.BlockSpec(memory_space=pltpu.HBM),
+            pl.BlockSpec(memory_space=pltpu.VMEM),
             pl.BlockSpec(memory_space=pltpu.VMEM),
         ],
         out_shape=[
@@ -357,8 +351,6 @@
             pltpu.VMEM((queries, block), BF16),
             pltpu.VMEM((queries, block), BF16),
             pltpu.VMEM((queries, dim), F32),
-            pltpu.VMEM((rows, dim), BF16),
-            pltpu.SemaphoreType.DMA((rows // block,)),
         ],
         compiler_params=params(30),
         cost_estimate=pl.CostEstimate(
@@ -406,71 +398,77 @@
     )(parts)
 
 
-def final_kernel(core_ref, notes_ref, peer_ref, mine_ref, other_ref, out_hbm, near, sems):
+def term_kernel(first, notes_ref, mine_ref, out_ref):
     groups, plane, dim = mine_ref.shape
-    queries = groups * plane
-    parts = sems.shape[0]
-    width = dim // parts
-    even = core_ref[0] == 0
-
-    def ordered(own, peer):
-        own, peer = own.reshape(queries, own.shape[-1]), peer.reshape(queries, peer.shape[-1])
-        return jnp.where(even, own, peer), jnp.where(even, peer, own)
-
-    def term(raw, grads):
-        return lax.dot_general(raw, grads, (((0,), (0,)), ((), ())), preferred_element_type=F32)
-
-    def copy(i):
-        at = pl.ds(i * width, width)
-        return pltpu.make_async_copy(near.at[at, :], out_hbm.at[at, :], sems.at[i])
-
-    grads = ordered(mine_ref[...], other_ref[...])
-    for i in range(parts):
-        at = slice(i * width, (i + 1) * width)
-        raw = ordered(notes_ref[:, :plane, at], peer_ref[:, :plane, at])
-        near[at, :] = term(raw[0], grads[0]) + term(raw[1], grads[1])
-        copy(i).start()
-    for i in range(parts):
-        copy(i).wait()
-
-
-def final_call(core, notes, peer, mine, other):
+    raw = notes_ref[:, :plane, first : first + out_ref.shape[0]].reshape(groups * plane, out_ref.shape[0])
+    grads = mine_ref[...].reshape(groups * plane, dim)
+    out_ref[...] = lax.dot_general(raw, grads, (((0,), (0,)), ((), ())), preferred_element_type=F32)
+
+
+def term_call(notes, mine, first, width):
     dim = mine.shape[-1]
     return pl.pallas_call(
-        final_kernel,
-        in_specs=[pl.BlockSpec(memory_space=pltpu.SMEM)] + [pl.BlockSpec(memory_space=pltpu.VMEM)] * 4,
-        out_specs=pl.BlockSpec(memory_space=pl.ANY),
-        out_shape=jax.ShapeDtypeStruct((dim, dim), F32),
-        scratch_shapes=[pltpu.VMEM((dim, dim), F32), pltpu.SemaphoreType.DMA((3,))],
-        compiler_params=params(20),
-        name="final",
-    )(core, notes, peer, mine, other)
-
-
-def head_kernel(raw_ref, projection_ref, positives_ref, out_ref):
+        functools.partial(term_kernel, first),
+        out_shape=jax.ShapeDtypeStruct((width, dim), F32),
+        compiler_params=params(12),
+        cost_estimate=pl.CostEstimate(
+            flops=4 * width * dim * mine.shape[0] * mine.shape[1], bytes_accessed=width * dim * 4, transcendentals=0
+        ),
+        name="term",
+    )(notes, mine)
+
+
+def join_kernel(first_ref, first_other_ref, second_ref, second_other_ref, out_ref):
+    half = first_ref.shape[0]
+    out_ref[:half, :] = first_ref[...] + first_other_ref[...]
+    out_ref[half:, :] = second_ref[...] + second_other_ref[...]
+
+
+def join_call(terms, others):
+    half, dim = terms[0].shape
+    return pl.pallas_call(
+        join_kernel,
+        out_shape=jax.ShapeDtypeStruct((2 * half, dim), F32),
+        compiler_params=params(12),
+        name="join",
+    )(terms[0], others[0], terms[1], others[1])
+
+
+def head_kernel(raw_hbm, projection_hbm, positives_hbm, out_ref, raw_ref, projection_ref, positives_ref, sems):
+    far_near = ((projection_hbm, projection_ref), (raw_hbm, raw_ref), (positives_hbm, positives_ref))
+    copies = [pltpu.make_async_copy(far, near, sems.at[i]) for i, (far, near) in enumerate(far_near)]
+    for copy in copies:
+        copy.start()
     own, dim = raw_ref.shape
-    raw = raw_ref[...]
-    projected = jnp.dot(raw, projection_ref[...], precision=lax.Precision.HIGHEST, preferred_element_type=F32)
+    copies[2].wait()
     lane = lax.broadcasted_iota(jnp.int32, (own, LANES), 1)
     codes = jnp.zeros((own, LANES), jnp.int32)
     for k in range(POS):
         ids = positives_ref[:, k : k + 1]
         for part, piece in enumerate((ids >> 14, (ids >> 7) & 127, ids & 127)):
             codes = jnp.where(lane == k + POS * part, piece, codes)
+    copies[1].wait()
+    raw = raw_ref[...]
+    for g in range(out_ref.shape[0]):
+        out_ref[g, :, dim : dim + LANES] = codes.astype(F32).astype(BF16)
+        out_ref[g, :, dim + LANES :] = raw.astype(BF16)
+    copies[0].wait()
+    projected = jnp.dot(raw, projection_ref[...], precision=lax.Precision.HIGHEST, preferred_element_type=F32)
     for g in range(out_ref.shape[0]):
         out_ref[g, :, :dim] = projected.astype(BF16)
-        out_ref[g, :, dim : dim + LANES] = codes.astype(F32).astype(BF16)
-        out_ref[g, :, dim + LANES :] = raw.astype(BF16)
 
 
 def head_call(raw, projection, positives, n):
     own, dim = raw.shape
+    arrays = (raw, projection, positives)
     return pl.pallas_call(
         head_kernel,
+        in_specs=[pl.BlockSpec(memory_space=pltpu.HBM)] * 3,
         out_shape=jax.ShapeDtypeStruct((n, own, 2 * dim + LANES), BF16),
+        scratch_shapes=[pltpu.VMEM(v.shape, v.dtype) for v in arrays] + [pltpu.SemaphoreType.DMA((3,))],
         compiler_params=params(12),
         name="head",
-    )(raw, projection, positives)
+    )(*(pltpu.with_memory_space_constraint(v, pltpu.HBM) for v in arrays))
 
 
 def exchange(v, axes):
@@ -488,8 +486,6 @@
     nz, nxy = lax.axis_size("z"), lax.axis_size(XY)
     plane = nz * own
     scale = 1.0 / (4.0 * rows * nz * nxy)
-    core = lax.axis_index("c")
-    swap = [(0, 1), (1, 0)]
 
     shard = (lax.axis_index("x") * nz + lax.axis_index("z")) * lax.axis_size("y") + lax.axis_index("y")
     packet, shard = lax.optimization_barrier((head_call(queries_raw, projection, positives, nz), shard))
@@ -497,28 +493,27 @@
     packet, raw = lax.optimization_barrier((packet[:, : dim + LANES], packet[:, dim + LANES :]))
     packet = spread(packet, XY)
 
-    passages = pltpu.with_memory_space_constraint(passages, pltpu.HBM)
-    scores, notes, local_pos = score_call(shard.reshape(1), packet, raw, passages)
+    held = pltpu.with_memory_space_constraint(passages, pltpu.HBM)
+    scores, notes, local_pos = score_call(shard.reshape(1), packet, raw, held)
     notes = exchange(notes, XY)
     pos = exchange(read_call(notes, nz, nxy * plane), "z")
     slopes, sums = sigmoid_call(pos, scores, scale, nxy)
     sums = exchange(fold_call(exchange(sums, XY), nz), "z")
     part, sums = grad_call(sums, slopes, passages, local_pos, scale, nxy)
 
-    part, notes = lax.optimization_barrier((part, notes))
-    peer = lax.ppermute(notes, "c", swap)
-    part, peer = lax.optimization_barrier((exchange(part, XY), peer))
-    part = exchange(fold_call(part, nz), "z")
+    part = exchange(fold_call(exchange(part, XY), nz), "z")
     part, summed = fold_both_call(part, nxy)
     mine = exchange(part, XY)
-    other = lax.ppermute(mine, "c", swap)
+    half = dim // 2
+    terms = [term_call(notes, mine, first, half) for first in (0, half)]
+    others = [lax.ppermute(term, "c", [(0, 1), (1, 0)]) for term in terms]
+    grad_projection = join_call(terms, others)
 
     home = lax.axis_index("z") * own
     query_grad = lax.dynamic_slice_in_dim(summed, home, own, 0)
     grad_raw = jnp.dot(query_grad, projection.T, precision=hp, preferred_element_type=F32)
     first = lax.axis_index(XY) * plane + home
     loss = lax.dynamic_slice_in_dim(sums[POS], first, own, 0)
-    grad_projection = final_call(core.reshape(1), notes, peer, mine, other)
     return (loss, grad_raw, grad_projection)
 
 

time: 181 us -> 173 us (0.956)
  blocking collectives: 131 us -> 123 us
  Pallas kernels: 29.9 us -> 36.4 us
  starting transfers between devices: 11.7 us -> 6.89 us
  local copies, waits for them, and re-layouts: 4.7 us -> 1.35 us
    all_to_all x9, blocking collectives: 131 us -> 123 us  [exchange(): return lax.all_to_all(v, axes, 0, 0, tiled=False)]
    pallas_call x1, Pallas kernels: 9.45 us -> 15.3 us  [sigmoid_call(): pl.pallas_call(functools.partial(sigmoid_kernel, scale), in_specs=[pl.Blo...]
    ppermute x2, starting transfers between devices: 11.7 us -> 6.89 us  [shards(): others = [lax.ppermute(term, 'c', [(0, 1), (1, 0)]) for term in terms]]
    unnamed x12 -> x6, local copies, waits for them, and re-layouts: 4 us -> 0.64 us
    pallas_call x2 -> x4, Pallas kernels: 4.86 us -> 6.74 us  [the longest x1 2.91 us: join_call(): pl.pallas_call(join_kernel, out_shape=jax.ShapeDtypeStruct((2 * half, dim...]
  transfers between devices with their start and end apart: 2 -> 2, of which waited for: 0 -> 0; matrix products, arithmetic and copies ran while one was open for 2% -> 3% of each run, Pallas kernels for 0% -> 0%
where the time goes in v6:
time: 173 us
  blocking collectives  123 us (71%)
  Pallas kernels  36.4 us (21%)
  starting transfers between devices  6.89 us (4%)
  matrix products  4.28 us (2%)
    all_to_all x9, blocking collectives, exchange(): return lax.all_to_all(v, axes, 0, 0, tiled=False)  123 us
    pallas_call x1, Pallas kernels, sigmoid_call(): pl.pallas_call(functools.partial(sigmoid_kernel, scale), in_specs=[pl.Blo...  15.3 us
    pallas_call x1, Pallas kernels, score_call(): pl.pallas_call(score_kernel, in_specs=[pl.BlockSpec(memory_space=pltpu.SM...  7.28 us
    ppermute x2, starting transfers between devices, shards(): others = [lax.ppermute(term, 'c', [(0, 1), (1, 0)]) for term in terms]  6.89 us
    pallas_call x1, Pallas kernels, grad_call(): pl.pallas_call(functools.partial(grad_kernel, scale), in_specs=[pl.BlockS...  6.85 us
    dot_general x1, matrix products, shards(): jnp.dot(query_grad, projection.T, precision=hp, preferred_element_type=F32)  4.28 us
  transfers between devices with their start and end apart: 2, of which 0 were waited for; matrix products, arithmetic and copies ran while one was open for 3% of the time, Pallas kernels for 0%

profile of v6, /device:TPU:1, one launch (start us, length us, event | category | flops | bytes accessed | tf_op | source)
XLA Modules:
  0.0 172.9 jit_solution(17014168649156203991)
XLA Ops:
  0.6 2.8 %head.1 = bf16[8,4,1664]{2,1,0:T(4,128)(2,1)S(1)} custom-call(f32[4,768]{1,0:T(4,128)} %raw_hbm.1, f32[768,768]{1,0:T(8,128)} %projection_hbm.1, s32[4,4]{1,0:T(4,128)} %positives_hbm.1), custom_call_target="tpu_custom_call" | custom-call | tf_op jit(solution)/shard_map/head/pallas_call | solution.py:464
  3.5 16.4 %all_to_all.45 = bf16[8,4,1664]{2,1,0:T(4,128)(2,1)S(1)} all-to-all(bf16[8,4,1664]{2,1,0:T(4,128)(2,1)S(1)} %head.1), channel_id=1, replica_groups=mesh['x'=4,'z'=8,'y'=4,'c'=2] {'z'}, dimensions={0} | all-to-all | bytes 212992 | tf_op jit(solution)/shard_map/all_to_all | solution.py:475
  19.9 0.1 broadcast_in_dim.2
  19.9 19.2 %all_to_all.46.packet_ref = bf16[16,32,896]{2,1,0:T(8,128)(2,1)S(1)} all-to-all(bf16[16,32,896]{2,1,0:T(8,128)(2,1)S(1)} %broadcast_in_dim.2), channel_id=1, replica_groups=mesh['x'=4,'z'=8,'y'=4,'c'=2] {'x','y'}, dimensions={0} | all-to-all | bytes 1835008 | tf_op jit(solution)/shard_map/all_to_all | solution.py:475
  39.1 7.3 %score.1 = (f32[512,4096]{1,0:T(8,128)S(1)}, bf16[16,40,768]{2,1,0:T(8,128)(2,1)S(1)}, s32[4,512,128]{2,1,0:T(8,128)S(1)}) custom-call(s32[1]{0:T(128)} %bitcast.shard_ref, bf16[16,32,896]{2,1,0:T(8,128)(2,1)S(1)} %all_to_all.46.packet_ref, bf16[32,768]{1,0:T(8,128)(2,1)S(1)} %slice.13.raw_ref, bf16[4096,768]{1,0:T(8,128)(2,1)} %passages_ref.1), custom_call_target="tpu_custom_call" | custom-call | flops 6442450944 | bytes 14680064 | tf_op jit(solution)/shard_map/score/pallas_call | solution.py:128
  46.4 16.0 %all_to_all.47.notes_ref = bf16[16,40,768]{2,1,0:T(8,128)(2,1)S(1)} all-to-all(bf16[16,40,768]{2,1,0:T(8,128)(2,1)S(1)} %get-tuple-element.20), channel_id=1, replica_groups=mesh['x'=4,'z'=8,'y'=4,'c'=2] {'x','y'}, dimensions={0} | all-to-all | bytes 1966080 | tf_op jit(solution)/shard_map/all_to_all | solution.py:475
  62.4 0.0 slice-start
  62.4 0.1 read.1
  62.5 10.6 %all_to_all.48.pos_ref = f32[8,8,512]{2,1,0:T(8,128)S(1)} all-to-all(f32[8,8,512]{2,1,0:T(8,128)S(1)} %read.1), channel_id=1, replica_groups=mesh['x'=4,'z'=8,'y'=4,'c'=2] {'z'}, dimensions={0} | all-to-all | bytes 262144 | tf_op jit(solution)/shard_map/all_to_all | solution.py:475
  73.1 0.0 slice-start.1
  73.1 15.3 %sigmoid.1 = (f32[512,4096]{1,0:T(8,128)S(1)}, f32[16,8,512]{2,1,0:T(8,128)S(1)}) custom-call(f32[8,8,512]{2,1,0:T(8,128)S(1)} %all_to_all.48.pos_ref, f32[512,4096]{1,0:T(8,128)S(1)} %get-tuple-element.21.scores_ref), custom_call_target="tpu_custom_call" | custom-call | flops 83886080 | bytes 16777216 | tf_op jit(solution)/shard_map/sigmoid/pallas_call | solution.py:265
  88.3 10.0 %all_to_all.49.parts_ref = f32[16,8,512]{2,1,0:T(8,128)S(1)} all-to-all(f32[16,8,512]{2,1,0:T(8,128)S(1)} %get-tuple-element.22), channel_id=1, replica_groups=mesh['x'=4,'z'=8,'y'=4,'c'=2] {'x','y'}, dimensions={0} | all-to-all | bytes 524288 | tf_op jit(solution)/shard_map/all_to_all | solution.py:475
  98.4 10.4 %all_to_all.50.sums_ref = f32[8,8,512]{2,1,0:T(8,128)S(1)} all-to-all(f32[8,8,512]{2,1,0:T(8,128)S(1)} %fold.2), channel_id=1, replica_groups=mesh['x'=4,'z'=8,'y'=4,'c'=2] {'z'}, dimensions={0} | all-to-all | bytes 262144 | tf_op jit(solution)/shard_map/all_to_all | solution.py:475
  108.8 0.0 slice-done
  108.8 0.0 slice-done.1
  108.8 6.8 %grad.1 = (bf16[16,32,768]{2,1,0:T(8,128)(2,1)S(1)}, f32[8,512]{1,0:T(8,128)S(1)}) custom-call(f32[8,8,512]{2,1,0:T(8,128)S(1)} %all_to_all.50.sums_ref, f32[512,4096]{1,0:T(8,128)S(1)} %get-tuple-element.23.slopes_ref, bf16[4096,768]{1,0:T(8,128)(2,1)S(1)} %bitcast.5, s32[4,512,128]{2,1,0:T(8,128)S(1)} %get-tuple-element.24.ids_ref), custom_call_target="tpu_custom_call" | custom-call | flops 6442450944 | bytes 14680064 | tf_op jit(solution)/shard_map/grad/pallas_call | solution.py:337
  115.7 13.7 %all_to_all.51.parts_ref = bf16[16,32,768]{2,1,0:T(8,128)(2,1)S(1)} all-to-all(bf16[16,32,768]{2,1,0:T(8,128)(2,1)S(1)} %get-tuple-element.26), channel_id=1, replica_groups=mesh['x'=4,'z'=8,'y'=4,'c'=2] {'x','y'}, dimensions={0} | all-to-all | bytes 1572864 | tf_op jit(solution)/shard_map/all_to_all | solution.py:475
  129.3 0.1 fold.3
  129.5 13.2 %all_to_all.52.parts_ref = bf16[8,32,768]{2,1,0:T(8,128)(2,1)S(1)} all-to-all(bf16[8,32,768]{2,1,0:T(8,128)(2,1)S(1)} %fold.3), channel_id=1, replica_groups=mesh['x'=4,'z'=8,'y'=4,'c'=2] {'z'}, dimensions={0} | all-to-all | bytes 786432 | tf_op jit(solution)/shard_map/all_to_all | solution.py:475
  142.7 0.1 fold_both.1
  142.8 0.0 copy-start
  142.8 0.6 copy-done
  143.4 13.7 %all_to_all.53.mine_ref = bf16[16,32,768]{2,1,0:T(8,128)(2,1)S(1)} all-to-all(bf16[16,32,768]{2,1,0:T(8,128)(2,1)S(1)} %get-tuple-element.28), channel_id=1, replica_groups=mesh['x'=4,'z'=8,'y'=4,'c'=2] {'x','y'}, dimensions={0} | all-to-all | bytes 1572864 | tf_op jit(solution)/shard_map/all_to_all | solution.py:475
  157.2 0.5 term.2.first_ref
  157.7 6.8 %collective-permute-start = (f32[384,768]{1,0:T(8,128)S(1)}, f32[384,768]{1,0:T(8,128)S(1)}, u32[]{:S(2)}, u32[]{:S(2)}) collective-permute-start(f32[384,768]{1,0:T(8,128)S(1)} %term.2.first_ref), channel_id=1, source_target_pairs={{0,1},{1,0},{2,3},{3,2},{4,5},{5,4},{6,7},{7,6},{8,9},{9,8},{10,11... | collective-permute-start | bytes 3538952 | tf_op jit(solution)/shard_map/ppermute | solution.py:509
  164.5 0.5 term.3.second_ref
  165.0 0.1 collective-permute-start.1
  165.1 0.6 dynamic-slice_bitcast_fusion
  165.7 4.3 %fusion = f32[4,768]{1,0:T(4,128)} fusion(f32[768,768]{1,0:T(8,128)} %projection_hbm.1, f32[32,768]{1,0:T(8,128)} %copy-done, s32[]{:T(128)S(6)} %select_n.7), kind=kOutput, calls=%fused_computation | convolution fusion | flops 28311552 | bytes 2383876 | tf_op jit(solution)/shard_map/dot_general | solution.py:514
  170.0 0.0 collective-permute-done.first_other_ref
  170.0 0.0 collective-permute-done.1.second_other_ref
  170.0 2.9 %join.1 = f32[768,768]{1,0:T(8,128)} custom-call(f32[384,768]{1,0:T(8,128)S(1)} %term.2.first_ref, f32[384,768]{1,0:T(8,128)S(1)} %collective-permute-done.first_other_ref, f32[384,768]{1,0:T(8,128)S(1)} %term.3.second_ref, f32[384,768]{1,0:T(8,128)} %collective-permute-done.1.second_other_ref), custom_call_target="tpu_custom_call" | custom-call | tf_op jit(solution)/shard_map/join/pallas_call | solution.py:429
  (6 shorter events, 0.1 us)
Async XLA Ops:
  62.4 46.4 %slice-start = ((s8[6291456]{0:T(1024)(128)(4,1)}), s8[4194304]{0:T(1024)(128)(4,1)S(1)}, s32[]{:S(2)}) async-start(s8[6291456]{0:T(1024)(128)(4,1)} %bitcast.4), calls=%async_computation.9 | async-start | bytes 8388608
  73.1 35.7 %slice-start.1 = ((s8[6291456]{0:T(1024)(128)(4,1)}), s8[2097152]{0:T(1024)(128)(4,1)S(1)}, s32[]{:S(2)}) async-start(s8[6291456]{0:T(1024)(128)(4,1)} %bitcast.4), calls=%async_computation.10 | async-start | bytes 4194304
  142.8 0.6 copy-start
  157.7 12.3 %collective-permute-start = (f32[384,768]{1,0:T(8,128)S(1)}, f32[384,768]{1,0:T(8,128)S(1)}, u32[]{:S(2)}, u32[]{:S(2)}) collective-permute-start(f32[384,768]{1,0:T(8,128)S(1)} %term.2.first_ref), channel_id=1, source_target_pairs={{0,1},{1,0},{2,3},{3,2},{4,5},{5,4},{6,7},{7,6},{8,9},{9,8},{10,11... | collective-permute-start | bytes 3538952 | tf_op jit(solution)/shard_map/ppermute | solution.py:509
  165.0 5.0 %collective-permute-start.1 = (f32[384,768]{1,0:T(8,128)S(1)}, f32[384,768]{1,0:T(8,128)}, u32[]{:S(2)}, u32[]{:S(2)}) collective-permute-start(f32[384,768]{1,0:T(8,128)S(1)} %term.3.second_ref), channel_id=1, source_target_pairs={{0,1},{1,0},{2,3},{3,2},{4,5},{5,4},{6,7},{7,6},{8,9},{9,8},{10,11... | collective-permute-start | bytes 3538952 | tf_op jit(solution)/shard_map/ppermute | solution.py:509

commit v7 on v6

--- a/solution.py
+++ b/solution.py
@@ -144,7 +144,7 @@
             pltpu.VMEM((rows, dim), BF16),
             pltpu.SemaphoreType.DMA((8,)),
         ],
-        compiler_params=params(24),
+        compiler_params=params(23),
         cost_estimate=pl.CostEstimate(
             flops=4 * queries * rows * dim, bytes_accessed=rows * dim * 2 + queries * rows * 4, transcendentals=0
         ),
@@ -207,7 +207,7 @@
         sums[POS, at, :] = 0.5 * (POS * chunks + tanh_acc)
         return carry
 
-    lax.fori_loop(0, queries // size, tile, 0, unroll=2)
+    lax.fori_loop(0, queries // size, tile, 0, unroll=4)
 
     def again(t):
         at, p = place(t)
@@ -273,7 +273,7 @@
             pltpu.VMEM((queries, LANES), F32),
             pltpu.VMEM((POS + 1, queries, LANES), F32),
         ],
-        compiler_params=params(24),
+        compiler_params=params(21),
         cost_estimate=pl.CostEstimate(
             flops=40 * queries * width, bytes_accessed=queries * width * 8, transcendentals=8 * queries * width
         ),
@@ -352,7 +352,7 @@
             pltpu.VMEM((queries, block), BF16),
             pltpu.VMEM((queries, dim), F32),
         ],
-        compiler_params=params(30),
+        compiler_params=params(28),
         cost_estimate=pl.CostEstimate(
             flops=4 * queries * rows * dim, bytes_accessed=rows * dim * 2 + queries * rows * 4, transcendentals=0
         ),
@@ -418,17 +418,29 @@
     )(notes, mine)
 
 
-def join_kernel(first_ref, first_other_ref, second_ref, second_other_ref, out_ref):
+def join_kernel(first_ref, first_other_ref, second_ref, second_other_ref, out_hbm, near, sems):
     half = first_ref.shape[0]
-    out_ref[:half, :] = first_ref[...] + first_other_ref[...]
-    out_ref[half:, :] = second_ref[...] + second_other_ref[...]
+    parts = sems.shape[0] // 2
+    width = half // parts
+    copies = []
+    for begin, own_ref, other_ref in ((0, first_ref, first_other_ref), (half, second_ref, second_other_ref)):
+        for i in range(parts):
+            here = slice(i * width, (i + 1) * width)
+            at = pl.ds(begin + i * width, width)
+            near[at, :] = own_ref[here, :] + other_ref[here, :]
+            copies.append(pltpu.make_async_copy(near.at[at, :], out_hbm.at[at, :], sems.at[len(copies)]))
+            copies[-1].start()
+    for copy in copies:
+        copy.wait()
 
 
 def join_call(terms, others):
     half, dim = terms[0].shape
     return pl.pallas_call(
         join_kernel,
+        out_specs=pl.BlockSpec(memory_space=pl.ANY),
         out_shape=jax.ShapeDtypeStruct((2 * half, dim), F32),
+        scratch_shapes=[pltpu.VMEM((2 * half, dim), F32), pltpu.SemaphoreType.DMA((4,))],
         compiler_params=params(12),
         name="join",
     )(terms[0], others[0], terms[1], others[1])
@@ -480,7 +492,6 @@
 
 
 def shards(queries_raw, projection, passages, positives):
-    hp = lax.Precision.HIGHEST
     rows, dim = passages.shape
     own = queries_raw.shape[0]
     nz, nxy = lax.axis_size("z"), lax.axis_size(XY)
@@ -509,10 +520,9 @@
     others = [lax.ppermute(term, "c", [(0, 1), (1, 0)]) for term in terms]
     grad_projection = join_call(terms, others)
 
-    home = lax.axis_index("z") * own
-    query_grad = lax.dynamic_slice_in_dim(summed, home, own, 0)
-    grad_raw = jnp.dot(query_grad, projection.T, precision=hp, preferred_element_type=F32)
-    first = lax.axis_index(XY) * plane + home
+    query_grad = lax.dynamic_slice_in_dim(summed, lax.axis_index("z") * own, own, 0)
+    grad_raw = jnp.dot(query_grad, projection.T, precision=lax.Precision.HIGHEST, preferred_element_type=F32)
+    first = lax.axis_index(XY) * plane + lax.axis_index("z") * own
     loss = lax.dynamic_slice_in_dim(sums[POS], first, own, 0)
     return (loss, grad_raw, grad_projection)
 

time: 173 us -> 172 us (level)
  Pallas kernels: 36.4 us -> 29.8 us
  starting transfers between devices: 6.89 us -> 12.5 us
    pallas_call x1, Pallas kernels: 15.3 us -> 8.76 us  [sigmoid_call(): pl.pallas_call(functools.partial(sigmoid_kernel, scale), in_specs=[pl.Blo...]
    ppermute x2, starting transfers between devices: 6.89 us -> 12.5 us  [shards(): others = [lax.ppermute(term, 'c', [(0, 1), (1, 0)]) for term in terms]]
where the time goes in v7:
time: 172 us
  blocking collectives  123 us (72%)
  Pallas kernels  29.8 us (17%)
  starting transfers between devices  12.5 us (7%)
  matrix products  4.28 us (2%)
    all_to_all x9, blocking collectives, exchange(): return lax.all_to_all(v, axes, 0, 0, tiled=False)  123 us
    ppermute x2, starting transfers between devices, shards(): others = [lax.ppermute(term, 'c', [(0, 1), (1, 0)]) for term in terms]  12.5 us
    pallas_call x1, Pallas kernels, sigmoid_call(): pl.pallas_call(functools.partial(sigmoid_kernel, scale), in_specs=[pl.Blo...  8.76 us
    pallas_call x1, Pallas kernels, score_call(): pl.pallas_call(score_kernel, in_specs=[pl.BlockSpec(memory_space=pltpu.SM...  7.28 us
    pallas_call x1, Pallas kernels, grad_call(): pl.pallas_call(functools.partial(grad_kernel, scale), in_specs=[pl.BlockS...  6.85 us
    dot_general x1, matrix products, shards(): jnp.dot(query_grad, projection.T, precision=lax.Precision.HIGHEST, prefer...  4.28 us
  transfers between devices with their start and end apart: 2, of which 0 were waited for; matrix products, arithmetic and copies ran while one was open for 3% of the time, Pallas kernels for 0%

profile of v7, /device:TPU:1, one launch (start us, length us, event | category | flops | bytes accessed | tf_op | source)
XLA Modules:
  0.0 171.7 jit_solution(17582651859155344424)
XLA Ops:
  0.6 2.8 %head.1 = bf16[8,4,1664]{2,1,0:T(4,128)(2,1)S(1)} custom-call(f32[4,768]{1,0:T(4,128)} %raw_hbm.1, f32[768,768]{1,0:T(8,128)} %projection_hbm.1, s32[4,4]{1,0:T(4,128)} %positives_hbm.1), custom_call_target="tpu_custom_call" | custom-call | tf_op jit(solution)/shard_map/head/pallas_call | solution.py:476
  3.5 16.4 %all_to_all.45 = bf16[8,4,1664]{2,1,0:T(4,128)(2,1)S(1)} all-to-all(bf16[8,4,1664]{2,1,0:T(4,128)(2,1)S(1)} %head.1), channel_id=1, replica_groups=mesh['x'=4,'z'=8,'y'=4,'c'=2] {'z'}, dimensions={0} | all-to-all | bytes 212992 | tf_op jit(solution)/shard_map/all_to_all | solution.py:487
  19.9 0.1 broadcast_in_dim.2
  19.9 19.2 %all_to_all.46.packet_ref = bf16[16,32,896]{2,1,0:T(8,128)(2,1)S(1)} all-to-all(bf16[16,32,896]{2,1,0:T(8,128)(2,1)S(1)} %broadcast_in_dim.2), channel_id=1, replica_groups=mesh['x'=4,'z'=8,'y'=4,'c'=2] {'x','y'}, dimensions={0} | all-to-all | bytes 1835008 | tf_op jit(solution)/shard_map/all_to_all | solution.py:487
  39.1 7.3 %score.1 = (f32[512,4096]{1,0:T(8,128)S(1)}, bf16[16,40,768]{2,1,0:T(8,128)(2,1)S(1)}, s32[4,512,128]{2,1,0:T(8,128)S(1)}) custom-call(s32[1]{0:T(128)} %bitcast.shard_ref, bf16[16,32,896]{2,1,0:T(8,128)(2,1)S(1)} %all_to_all.46.packet_ref, bf16[32,768]{1,0:T(8,128)(2,1)S(1)} %slice.13.raw_ref, bf16[4096,768]{1,0:T(8,128)(2,1)} %passages_ref.1), custom_call_target="tpu_custom_call" | custom-call | flops 6442450944 | bytes 14680064 | tf_op jit(solution)/shard_map/score/pallas_call | solution.py:128
  46.4 16.0 %all_to_all.47.notes_ref = bf16[16,40,768]{2,1,0:T(8,128)(2,1)S(1)} all-to-all(bf16[16,40,768]{2,1,0:T(8,128)(2,1)S(1)} %get-tuple-element.20), channel_id=1, replica_groups=mesh['x'=4,'z'=8,'y'=4,'c'=2] {'x','y'}, dimensions={0} | all-to-all | bytes 1966080 | tf_op jit(solution)/shard_map/all_to_all | solution.py:487
  62.4 0.0 slice-start
  62.4 0.1 read.1
  62.5 10.6 %all_to_all.48.pos_ref = f32[8,8,512]{2,1,0:T(8,128)S(1)} all-to-all(f32[8,8,512]{2,1,0:T(8,128)S(1)} %read.1), channel_id=1, replica_groups=mesh['x'=4,'z'=8,'y'=4,'c'=2] {'z'}, dimensions={0} | all-to-all | bytes 262144 | tf_op jit(solution)/shard_map/all_to_all | solution.py:487
  73.1 0.0 slice-start.1
  73.1 8.8 %sigmoid.1 = (f32[512,4096]{1,0:T(8,128)S(1)}, f32[16,8,512]{2,1,0:T(8,128)S(1)}) custom-call(f32[8,8,512]{2,1,0:T(8,128)S(1)} %all_to_all.48.pos_ref, f32[512,4096]{1,0:T(8,128)S(1)} %get-tuple-element.21.scores_ref), custom_call_target="tpu_custom_call" | custom-call | flops 83886080 | bytes 16777216 | tf_op jit(solution)/shard_map/sigmoid/pallas_call | solution.py:265
  81.8 10.7 %all_to_all.49.parts_ref = f32[16,8,512]{2,1,0:T(8,128)S(1)} all-to-all(f32[16,8,512]{2,1,0:T(8,128)S(1)} %get-tuple-element.22), channel_id=1, replica_groups=mesh['x'=4,'z'=8,'y'=4,'c'=2] {'x','y'}, dimensions={0} | all-to-all | bytes 524288 | tf_op jit(solution)/shard_map/all_to_all | solution.py:487
  92.6 10.3 %all_to_all.50.sums_ref = f32[8,8,512]{2,1,0:T(8,128)S(1)} all-to-all(f32[8,8,512]{2,1,0:T(8,128)S(1)} %fold.2), channel_id=1, replica_groups=mesh['x'=4,'z'=8,'y'=4,'c'=2] {'z'}, dimensions={0} | all-to-all | bytes 262144 | tf_op jit(solution)/shard_map/all_to_all | solution.py:487
  102.9 0.0 slice-done
  102.9 0.0 slice-done.1
  102.9 6.8 %grad.1 = (bf16[16,32,768]{2,1,0:T(8,128)(2,1)S(1)}, f32[8,512]{1,0:T(8,128)S(1)}) custom-call(f32[8,8,512]{2,1,0:T(8,128)S(1)} %all_to_all.50.sums_ref, f32[512,4096]{1,0:T(8,128)S(1)} %get-tuple-element.23.slopes_ref, bf16[4096,768]{1,0:T(8,128)(2,1)S(1)} %bitcast.5, s32[4,512,128]{2,1,0:T(8,128)S(1)} %get-tuple-element.24.ids_ref), custom_call_target="tpu_custom_call" | custom-call | flops 6442450944 | bytes 14680064 | tf_op jit(solution)/shard_map/grad/pallas_call | solution.py:337
  109.8 13.4 %all_to_all.51.parts_ref = bf16[16,32,768]{2,1,0:T(8,128)(2,1)S(1)} all-to-all(bf16[16,32,768]{2,1,0:T(8,128)(2,1)S(1)} %get-tuple-element.26), channel_id=1, replica_groups=mesh['x'=4,'z'=8,'y'=4,'c'=2] {'x','y'}, dimensions={0} | all-to-all | bytes 1572864 | tf_op jit(solution)/shard_map/all_to_all | solution.py:487
  123.1 0.1 fold.3
  123.2 13.1 %all_to_all.52.parts_ref = bf16[8,32,768]{2,1,0:T(8,128)(2,1)S(1)} all-to-all(bf16[8,32,768]{2,1,0:T(8,128)(2,1)S(1)} %fold.3), channel_id=1, replica_groups=mesh['x'=4,'z'=8,'y'=4,'c'=2] {'z'}, dimensions={0} | all-to-all | bytes 786432 | tf_op jit(solution)/shard_map/all_to_all | solution.py:487
  136.4 0.1 fold_both.1
  136.5 0.0 copy-start
  136.5 0.6 copy-done
  137.1 13.3 %all_to_all.53.mine_ref = bf16[16,32,768]{2,1,0:T(8,128)(2,1)S(1)} all-to-all(bf16[16,32,768]{2,1,0:T(8,128)(2,1)S(1)} %get-tuple-element.28), channel_id=1, replica_groups=mesh['x'=4,'z'=8,'y'=4,'c'=2] {'x','y'}, dimensions={0} | all-to-all | bytes 1572864 | tf_op jit(solution)/shard_map/all_to_all | solution.py:487
  150.4 0.5 term.2.first_ref
  150.9 12.4 %collective-permute-start = (f32[384,768]{1,0:T(8,128)S(1)}, f32[384,768]{1,0:T(8,128)S(1)}, u32[]{:S(2)}, u32[]{:S(2)}) collective-permute-start(f32[384,768]{1,0:T(8,128)S(1)} %term.2.first_ref), channel_id=1, source_target_pairs={{0,1},{1,0},{2,3},{3,2},{4,5},{5,4},{6,7},{7,6},{8,9},{9,8},{10,11... | collective-permute-start | bytes 3538952 | tf_op jit(solution)/shard_map/ppermute | solution.py:520
  163.3 0.5 term.3.second_ref
  163.8 0.1 collective-permute-start.1
  163.9 0.6 dynamic-slice_bitcast_fusion
  164.5 4.3 %fusion = f32[4,768]{1,0:T(4,128)} fusion(f32[768,768]{1,0:T(8,128)} %projection_hbm.1, f32[32,768]{1,0:T(8,128)} %copy-done, s32[]{:T(128)S(6)} %select_n.7), kind=kOutput, calls=%fused_computation | convolution fusion | flops 28311552 | bytes 2383876 | tf_op jit(solution)/shard_map/dot_general | solution.py:524
  168.8 0.0 collective-permute-done.first_other_ref
  168.8 0.0 collective-permute-done.1.second_other_ref
  168.8 2.8 %join.1 = f32[768,768]{1,0:T(8,128)} custom-call(f32[384,768]{1,0:T(8,128)S(1)} %term.2.first_ref, f32[384,768]{1,0:T(8,128)S(1)} %collective-permute-done.first_other_ref, f32[384,768]{1,0:T(8,128)S(1)} %term.3.second_ref, f32[384,768]{1,0:T(8,128)} %collective-permute-done.1.second_other_ref), custom_call_target="tpu_custom_call" | custom-call | tf_op jit(solution)/shard_map/join/pallas_call | solution.py:439
  (6 shorter events, 0.1 us)
Async XLA Ops:
  62.4 40.5 %slice-start = ((s8[6291456]{0:T(1024)(128)(4,1)}), s8[4194304]{0:T(1024)(128)(4,1)S(1)}, s32[]{:S(2)}) async-start(s8[6291456]{0:T(1024)(128)(4,1)} %bitcast.4), calls=%async_computation.9 | async-start | bytes 8388608
  73.1 29.8 %slice-start.1 = ((s8[6291456]{0:T(1024)(128)(4,1)}), s8[2097152]{0:T(1024)(128)(4,1)S(1)}, s32[]{:S(2)}) async-start(s8[6291456]{0:T(1024)(128)(4,1)} %bitcast.4), calls=%async_computation.10 | async-start | bytes 4194304
  136.5 0.6 copy-start
  150.9 17.9 %collective-permute-start = (f32[384,768]{1,0:T(8,128)S(1)}, f32[384,768]{1,0:T(8,128)S(1)}, u32[]{:S(2)}, u32[]{:S(2)}) collective-permute-start(f32[384,768]{1,0:T(8,128)S(1)} %term.2.first_ref), channel_id=1, source_target_pairs={{0,1},{1,0},{2,3},{3,2},{4,5},{5,4},{6,7},{7,6},{8,9},{9,8},{10,11... | collective-permute-start | bytes 3538952 | tf_op jit(solution)/shard_map/ppermute | solution.py:520
  163.8 5.0 %collective-permute-start.1 = (f32[384,768]{1,0:T(8,128)S(1)}, f32[384,768]{1,0:T(8,128)}, u32[]{:S(2)}, u32[]{:S(2)}) collective-permute-start(f32[384,768]{1,0:T(8,128)S(1)} %term.3.second_ref), channel_id=1, source_target_pairs={{0,1},{1,0},{2,3},{3,2},{4,5},{5,4},{6,7},{7,6},{8,9},{9,8},{10,11... | collective-permute-start | bytes 3538952 | tf_op jit(solution)/shard_map/ppermute | solution.py:520

commit v8 on v7

--- a/solution.py
+++ b/solution.py
@@ -207,7 +207,7 @@
         sums[POS, at, :] = 0.5 * (POS * chunks + tanh_acc)
         return carry
 
-    lax.fori_loop(0, queries // size, tile, 0, unroll=4)
+    lax.fori_loop(0, queries // size, tile, 0, unroll=8)
 
     def again(t):
         at, p = place(t)

time: 172 us -> 172 us (level)
  no operation moved by 1% of the time
where the time goes in v8:
time: 172 us; the launch traced here: 171 us
  blocking collectives  123 us (72%)
  Pallas kernels  29.5 us (17%)
  starting transfers between devices  12.5 us (7%)
  matrix products  4.28 us (2%)
    all_to_all x9, blocking collectives, exchange(): return lax.all_to_all(v, axes, 0, 0, tiled=False)  123 us
    ppermute x2, starting transfers between devices, shards(): others = [lax.ppermute(term, 'c', [(0, 1), (1, 0)]) for term in terms]  12.5 us
    pallas_call x1, Pallas kernels, sigmoid_call(): pl.pallas_call(functools.partial(sigmoid_kernel, scale), in_specs=[pl.Blo...  8.52 us
    pallas_call x1, Pallas kernels, score_call(): pl.pallas_call(score_kernel, in_specs=[pl.BlockSpec(memory_space=pltpu.SM...  7.28 us
    pallas_call x1, Pallas kernels, grad_call(): pl.pallas_call(functools.partial(grad_kernel, scale), in_specs=[pl.BlockS...  6.85 us
    dot_general x1, matrix products, shards(): jnp.dot(query_grad, projection.T, precision=lax.Precision.HIGHEST, prefer...  4.28 us
  transfers between devices with their start and end apart: 2, of which 0 were waited for; matrix products, arithmetic and copies ran while one was open for 3% of the time, Pallas kernels for 0%

profile of v8, /device:TPU:1, one launch (start us, length us, event | category | flops | bytes accessed | tf_op | source)
XLA Modules:
  0.0 171.5 jit_solution(16146809766679111002)
XLA Ops:
  0.6 2.8 %head.1 = bf16[8,4,1664]{2,1,0:T(4,128)(2,1)S(1)} custom-call(f32[4,768]{1,0:T(4,128)} %raw_hbm.1, f32[768,768]{1,0:T(8,128)} %projection_hbm.1, s32[4,4]{1,0:T(4,128)} %positives_hbm.1), custom_call_target="tpu_custom_call" | custom-call | tf_op jit(solution)/shard_map/head/pallas_call | solution.py:476
  3.5 16.4 %all_to_all.45 = bf16[8,4,1664]{2,1,0:T(4,128)(2,1)S(1)} all-to-all(bf16[8,4,1664]{2,1,0:T(4,128)(2,1)S(1)} %head.1), channel_id=1, replica_groups=mesh['x'=4,'z'=8,'y'=4,'c'=2] {'z'}, dimensions={0} | all-to-all | bytes 212992 | tf_op jit(solution)/shard_map/all_to_all | solution.py:487
  19.9 0.1 broadcast_in_dim.2
  19.9 19.2 %all_to_all.46.packet_ref = bf16[16,32,896]{2,1,0:T(8,128)(2,1)S(1)} all-to-all(bf16[16,32,896]{2,1,0:T(8,128)(2,1)S(1)} %broadcast_in_dim.2), channel_id=1, replica_groups=mesh['x'=4,'z'=8,'y'=4,'c'=2] {'x','y'}, dimensions={0} | all-to-all | bytes 1835008 | tf_op jit(solution)/shard_map/all_to_all | solution.py:487
  39.1 7.3 %score.1 = (f32[512,4096]{1,0:T(8,128)S(1)}, bf16[16,40,768]{2,1,0:T(8,128)(2,1)S(1)}, s32[4,512,128]{2,1,0:T(8,128)S(1)}) custom-call(s32[1]{0:T(128)} %bitcast.shard_ref, bf16[16,32,896]{2,1,0:T(8,128)(2,1)S(1)} %all_to_all.46.packet_ref, bf16[32,768]{1,0:T(8,128)(2,1)S(1)} %slice.13.raw_ref, bf16[4096,768]{1,0:T(8,128)(2,1)} %passages_ref.1), custom_call_target="tpu_custom_call" | custom-call | flops 6442450944 | bytes 14680064 | tf_op jit(solution)/shard_map/score/pallas_call | solution.py:128
  46.4 16.0 %all_to_all.47.notes_ref = bf16[16,40,768]{2,1,0:T(8,128)(2,1)S(1)} all-to-all(bf16[16,40,768]{2,1,0:T(8,128)(2,1)S(1)} %get-tuple-element.20), channel_id=1, replica_groups=mesh['x'=4,'z'=8,'y'=4,'c'=2] {'x','y'}, dimensions={0} | all-to-all | bytes 1966080 | tf_op jit(solution)/shard_map/all_to_all | solution.py:487
  62.4 0.0 slice-start
  62.4 0.1 read.1
  62.5 10.6 %all_to_all.48.pos_ref = f32[8,8,512]{2,1,0:T(8,128)S(1)} all-to-all(f32[8,8,512]{2,1,0:T(8,128)S(1)} %read.1), channel_id=1, replica_groups=mesh['x'=4,'z'=8,'y'=4,'c'=2] {'z'}, dimensions={0} | all-to-all | bytes 262144 | tf_op jit(solution)/shard_map/all_to_all | solution.py:487
  73.1 0.0 slice-start.1
  73.1 8.5 %sigmoid.1 = (f32[512,4096]{1,0:T(8,128)S(1)}, f32[16,8,512]{2,1,0:T(8,128)S(1)}) custom-call(f32[8,8,512]{2,1,0:T(8,128)S(1)} %all_to_all.48.pos_ref, f32[512,4096]{1,0:T(8,128)S(1)} %get-tuple-element.21.scores_ref), custom_call_target="tpu_custom_call" | custom-call | flops 83886080 | bytes 16777216 | tf_op jit(solution)/shard_map/sigmoid/pallas_call | solution.py:265
  81.6 10.7 %all_to_all.49.parts_ref = f32[16,8,512]{2,1,0:T(8,128)S(1)} all-to-all(f32[16,8,512]{2,1,0:T(8,128)S(1)} %get-tuple-element.22), channel_id=1, replica_groups=mesh['x'=4,'z'=8,'y'=4,'c'=2] {'x','y'}, dimensions={0} | all-to-all | bytes 524288 | tf_op jit(solution)/shard_map/all_to_all | solution.py:487
  92.3 10.3 %all_to_all.50.sums_ref = f32[8,8,512]{2,1,0:T(8,128)S(1)} all-to-all(f32[8,8,512]{2,1,0:T(8,128)S(1)} %fold.2), channel_id=1, replica_groups=mesh['x'=4,'z'=8,'y'=4,'c'=2] {'z'}, dimensions={0} | all-to-all | bytes 262144 | tf_op jit(solution)/shard_map/all_to_all | solution.py:487
  102.7 0.0 slice-done
  102.7 0.0 slice-done.1
  102.7 6.8 %grad.1 = (bf16[16,32,768]{2,1,0:T(8,128)(2,1)S(1)}, f32[8,512]{1,0:T(8,128)S(1)}) custom-call(f32[8,8,512]{2,1,0:T(8,128)S(1)} %all_to_all.50.sums_ref, f32[512,4096]{1,0:T(8,128)S(1)} %get-tuple-element.23.slopes_ref, bf16[4096,768]{1,0:T(8,128)(2,1)S(1)} %bitcast.5, s32[4,512,128]{2,1,0:T(8,128)S(1)} %get-tuple-element.24.ids_ref), custom_call_target="tpu_custom_call" | custom-call | flops 6442450944 | bytes 14680064 | tf_op jit(solution)/shard_map/grad/pallas_call | solution.py:337
  109.5 13.4 %all_to_all.51.parts_ref = bf16[16,32,768]{2,1,0:T(8,128)(2,1)S(1)} all-to-all(bf16[16,32,768]{2,1,0:T(8,128)(2,1)S(1)} %get-tuple-element.26), channel_id=1, replica_groups=mesh['x'=4,'z'=8,'y'=4,'c'=2] {'x','y'}, dimensions={0} | all-to-all | bytes 1572864 | tf_op jit(solution)/shard_map/all_to_all | solution.py:487
  122.9 0.1 fold.3
  123.0 13.1 %all_to_all.52.parts_ref = bf16[8,32,768]{2,1,0:T(8,128)(2,1)S(1)} all-to-all(bf16[8,32,768]{2,1,0:T(8,128)(2,1)S(1)} %fold.3), channel_id=1, replica_groups=mesh['x'=4,'z'=8,'y'=4,'c'=2] {'z'}, dimensions={0} | all-to-all | bytes 786432 | tf_op jit(solution)/shard_map/all_to_all | solution.py:487
  136.1 0.1 fold_both.1
  136.2 0.0 copy-start
  136.2 0.6 copy-done
  136.9 13.3 %all_to_all.53.mine_ref = bf16[16,32,768]{2,1,0:T(8,128)(2,1)S(1)} all-to-all(bf16[16,32,768]{2,1,0:T(8,128)(2,1)S(1)} %get-tuple-element.28), channel_id=1, replica_groups=mesh['x'=4,'z'=8,'y'=4,'c'=2] {'x','y'}, dimensions={0} | all-to-all | bytes 1572864 | tf_op jit(solution)/shard_map/all_to_all | solution.py:487
  150.2 0.5 term.2.first_ref
  150.7 12.4 %collective-permute-start = (f32[384,768]{1,0:T(8,128)S(1)}, f32[384,768]{1,0:T(8,128)S(1)}, u32[]{:S(2)}, u32[]{:S(2)}) collective-permute-start(f32[384,768]{1,0:T(8,128)S(1)} %term.2.first_ref), channel_id=1, source_target_pairs={{0,1},{1,0},{2,3},{3,2},{4,5},{5,4},{6,7},{7,6},{8,9},{9,8},{10,11... | collective-permute-start | bytes 3538952 | tf_op jit(solution)/shard_map/ppermute | solution.py:520
  163.0 0.5 term.3.second_ref
  163.6 0.1 collective-permute-start.1
  163.7 0.6 dynamic-slice_bitcast_fusion
  164.3 4.3 %fusion = f32[4,768]{1,0:T(4,128)} fusion(f32[768,768]{1,0:T(8,128)} %projection_hbm.1, f32[32,768]{1,0:T(8,128)} %copy-done, s32[]{:T(128)S(6)} %select_n.7), kind=kOutput, calls=%fused_computation | convolution fusion | flops 28311552 | bytes 2383876 | tf_op jit(solution)/shard_map/dot_general | solution.py:524
  168.6 0.0 collective-permute-done.first_other_ref
  168.6 0.0 collective-permute-done.1.second_other_ref
  168.6 2.8 %join.1 = f32[768,768]{1,0:T(8,128)} custom-call(f32[384,768]{1,0:T(8,128)S(1)} %term.2.first_ref, f32[384,768]{1,0:T(8,128)S(1)} %collective-permute-done.first_other_ref, f32[384,768]{1,0:T(8,128)S(1)} %term.3.second_ref, f32[384,768]{1,0:T(8,128)} %collective-permute-done.1.second_other_ref), custom_call_target="tpu_custom_call" | custom-call | tf_op jit(solution)/shard_map/join/pallas_call | solution.py:439
  (6 shorter events, 0.1 us)
Async XLA Ops:
  62.4 40.3 %slice-start = ((s8[6291456]{0:T(1024)(128)(4,1)}), s8[4194304]{0:T(1024)(128)(4,1)S(1)}, s32[]{:S(2)}) async-start(s8[6291456]{0:T(1024)(128)(4,1)} %bitcast.4), calls=%async_computation.9 | async-start | bytes 8388608
  73.1 29.6 %slice-start.1 = ((s8[6291456]{0:T(1024)(128)(4,1)}), s8[2097152]{0:T(1024)(128)(4,1)S(1)}, s32[]{:S(2)}) async-start(s8[6291456]{0:T(1024)(128)(4,1)} %bitcast.4), calls=%async_computation.10 | async-start | bytes 4194304
  136.2 0.6 copy-start
  150.7 17.9 %collective-permute-start = (f32[384,768]{1,0:T(8,128)S(1)}, f32[384,768]{1,0:T(8,128)S(1)}, u32[]{:S(2)}, u32[]{:S(2)}) collective-permute-start(f32[384,768]{1,0:T(8,128)S(1)} %term.2.first_ref), channel_id=1, source_target_pairs={{0,1},{1,0},{2,3},{3,2},{4,5},{5,4},{6,7},{7,6},{8,9},{9,8},{10,11... | collective-permute-start | bytes 3538952 | tf_op jit(solution)/shard_map/ppermute | solution.py:520
  163.6 5.0 %collective-permute-start.1 = (f32[384,768]{1,0:T(8,128)S(1)}, f32[384,768]{1,0:T(8,128)}, u32[]{:S(2)}, u32[]{:S(2)}) collective-permute-start(f32[384,768]{1,0:T(8,128)S(1)} %term.3.second_ref), channel_id=1, source_target_pairs={{0,1},{1,0},{2,3},{3,2},{4,5},{5,4},{6,7},{7,6},{8,9},{9,8},{10,11... | collective-permute-start | bytes 3538952 | tf_op jit(solution)/shard_map/ppermute | solution.py:520
